TPU v7x, 32 devices: a whole 2x2x4 slice. The times are simulated.
32 devices in a mesh: fsdp: 8 (over y, x, core), loop: 4 (over z).
Axes of the slice: x: 2, y: 2, z: 4, core: 2. Of those that a mesh axis runs over, the one named last changes fastest.
Arguments:
- iterate: bfloat16 [4, 7168, 2048], P(None, 'fsdp', 'loop'), may hold values from -0.0625 to 0.0625
- expert_order: int32 [4], replicated, may hold values from 0 to 3, each once
Outputs:
- update: bfloat16 [4, 7168, 2048], P(None, 'fsdp', 'loop')
Inputs may be any that keep to these rules, and one draw needn't show every extreme that they name: `expert_order`: each value names a different expert.
All inputs are finite; a program needn't handle non-finite values.
Results may differ from a plain program's by a relative error of at most 0.006.
Values may be sent and summed in bfloat16 or wider, within the bound.
No kernel may reach another device: no remote copies, remote signals or barrier semaphores. Data moves between devices by JAX's collectives and lax.ppermute only.
A program may use at most 128 MiB of HBM per device.

v0:
```python
import jax
import jax.numpy as jnp
from jax import lax
from jax.sharding import PartitionSpec as P

D = 7168


coef_linear = 3.4445
coef_cubic = -4.775


def half_step(left, right):
    factor = 0.2 * D**0.5
    partial_gram = jnp.einsum("eic,eik->eck", left, right, preferred_element_type=jnp.float32)
    summed = lax.psum(partial_gram, "fsdp")
    gram_block = summed.astype(jnp.bfloat16)
    product = jnp.einsum("eik,eck->eic", right, gram_block, preferred_element_type=jnp.float32)
    result = factor * (coef_linear * left.astype(jnp.float32) + coef_cubic * product)
    return result.astype(jnp.bfloat16)


def body(iterate, expert_order):
    chosen = jnp.take(iterate, expert_order, axis=0)
    gathered = lax.all_gather(chosen, "loop", axis=2, tiled=True)
    return half_step(chosen, gathered)


def solution(mesh):
    placed = (P(None, "fsdp", "loop"), P())
    return jax.shard_map(
        body, mesh=mesh, in_specs=placed, out_specs=P(None, "fsdp", "loop"), check_vma=False
    )
```

profile of v0, /device:TPU:8, one launch (start us, length us, event | category | flops | bytes accessed | tf_op | source)
XLA Modules:
  0.0 637.7 jit_solution(1627725262971974548)
XLA Ops:
  6.5 0.0 all-gather.2.cloned.1.call-start
  6.5 0.7 compare_and_fusion
  7.2 0.7 compare_select_fusion
  7.9 4.7 gather_fusion
  12.5 4.3 broadcast_select_fusion
  16.8 0.0 all-gather.2.cloned.1.call-update
  16.8 250.8 %all-gather.2.cloned.1.call-done = bf16[4,896,2048]{2,1,0:T(8,128)(2,1)} async-done(((bf16[4,896,512]{2,1,0:T(8,128)(2,1)}), bf16[4,896,2048]{2,1,0:T(8,128)(2,1)}) %all-gather.2.cloned.1.call-update) | async-done | bytes 14680080 | tf_op jit(solution)/shard_map/all_gather | solution.py:25
  267.7 18.0 %fusion.4 = f32[4,512,2048]{2,1,0:T(8,128)} fusion(bf16[4,896,512]{2,1,0:T(8,128)(2,1)} %broadcast_select_fusion, bf16[4,896,2048]{2,1,0:T(8,128)(2,1)} %all-gather.2.cloned.1.call-done), kind=kOutput, calls=%fused_computation.8 | convolution fusion | flops 7516192768 | bytes 35127296 | tf_op jit(solution)/shard_map/eic,eik->eck/dot_general | solution.py:15
  285.7 329.4 %all-reduce.1 = bf16[4,512,2048]{2,1,0:T(8,128)(2,1)} all-reduce(f32[4,512,2048]{2,1,0:T(8,128)} %fusion.4), channel_id=1, replica_groups=mesh['fsdp'=8,'loop'=4] {'fsdp'}, use_global_device_ids=true, to_apply=%region_0.1 | all-reduce | flops 4194304 | bytes 25165824 | tf_op jit(solution)/shard_map/psum | solution.py:16
  615.1 15.8 %multiply_convert_fusion = bf16[4,896,512]{2,1,0:T(8,128)(2,1)} fusion(bf16[4,896,512]{2,1,0:T(8,128)(2,1)} %broadcast_select_fusion, bf16[4,896,2048]{2,1,0:T(8,128)(2,1)} %all-gather.2.cloned.1.call-done, bf16[4,512,2048]{2,1,0:T(8,128)(2,1)} %all-reduce.1), kind=kOutput, calls=%fused_computation.3 | convolution fusion | flops 7527202816 | bytes 30408704 | tf_op jit(solution)/shard_map/eik,eck->eic/dot_general | solution.py:18
  (1 shorter events, 0.0 us)
Async XLA Ops:
  6.5 261.1 %all-gather.2.cloned.1.call-start = ((), (), s32[]{:S(2)}) async-start(), calls=%async_computation | async-start | bytes 18350080 | tf_op jit(solution)/shard_map/all_gather | solution.py:25
Sparse Core Ops, SparseCore 0:
  17.0 250.6 all-gather.1
where the time goes:
time: 642 us; the launch traced here: 638 us
  blocking collectives  329 us (51%)
  waiting for transfers between devices  251 us (39%)
  matrix products  33.8 us (5%)
  between operations  13.4 us (2%)
    psum x1, blocking collectives, half_step(): summed = lax.psum(partial_gram, 'fsdp')  329 us
    all_gather x1, waiting for transfers between devices, body(): gathered = lax.all_gather(chosen, 'loop', axis=2, tiled=True)  251 us
    dot_general x1, matrix products, half_step(): jnp.einsum('eic,eik->eck', left, right, preferred_element_type=jnp.float32)  18 us
    dot_general x1, matrix products, half_step(): jnp.einsum('eik,eck->eic', right, gram_block, preferred_element_type=jnp....  15.8 us
  transfers between devices with their start and end apart: 1, of which 1 were waited for; matrix products, arithmetic and copies ran while one was open for 0% of the time, Pallas kernels for 0%

commit v1 on v0

v1 whole, which is shorter than its diff:
```python
import jax
import jax.numpy as jnp
from jax import lax
from jax.sharding import PartitionSpec as P

D = 7168

coef_linear = 3.4445
coef_cubic = -4.775


def all_pairs(count):
    if count == 4:
        return [[1, 0, 3, 2], [2, 3, 0, 1], [3, 2, 1, 0]]
    return [[(place + step) % count for place in range(count)] for step in range(1, count)]


def swap(value, axis, bit, count):
    return lax.ppermute(value, axis, [(i, i ^ bit) for i in range(count)])


def halves(value, side):
    rows = value.shape[0] // 2
    low, high = value[:rows], value[rows:]
    return jnp.where(side == 0, low, high), jnp.where(side == 0, high, low)


def reduce_rows(partial, axis, bits, count):
    me = lax.axis_index(axis)
    for bit in bits:
        side = (me // bit) % 2
        keep, send = halves(partial, side)
        partial = keep.astype(jnp.float32) + swap(send.astype(jnp.bfloat16), axis, bit, count).astype(jnp.float32)
    return partial


def gather_rows(piece, axis, bits, count):
    me = lax.axis_index(axis)
    for bit in reversed(bits):
        side = (me // bit) % 2
        other = swap(piece, axis, bit, count)
        piece = jnp.where(side == 0, jnp.concatenate([piece, other]), jnp.concatenate([other, piece]))
    return piece


def reduce_all(partial, axis, count):
    bits = [1 << i for i in range(count.bit_length() - 1)]
    orders = [bits, bits[:1] + bits[:0:-1]]
    width = partial.shape[1] // 2
    parts = []
    for part, order in enumerate(orders):
        piece = reduce_rows(partial[:, part * width : (part + 1) * width], axis, order, count)
        parts.append(gather_rows(piece.astype(jnp.bfloat16), axis, order, count))
    return jnp.concatenate(parts, axis=1)


def body(iterate, expert_order, fsdp, loop):
    place = lax.axis_index("loop")
    tables = all_pairs(loop)
    width = iterate.shape[2]

    def mine(slot):
        return lax.dynamic_index_in_dim(iterate, expert_order[slot], 0, keepdims=False)

    targets = [jnp.asarray(table, jnp.int32)[place] for table in tables]
    blocks = [mine(place)]
    for table, target in zip(tables, targets):
        blocks.append(lax.ppermute(mine(target), "loop", list(enumerate(table))))
    matrix = jnp.concatenate(blocks, axis=1)

    slabs = []
    for a in range(loop):
        slabs.append(
            lax.dot_general(
                blocks[a], matrix[:, a * width :], (((0,), (0,)), ((), ())), preferred_element_type=jnp.float32
            )
        )
    packed = reduce_all(jnp.concatenate(slabs, axis=1), "fsdp", fsdp)
    rows = []
    start = [0]
    for a in range(loop):
        start.append(start[-1] + (loop - a) * width)
    for a in range(loop):
        left = [packed[:, start[b] + (a - b) * width : start[b] + (a - b + 1) * width].T for b in range(a)]
        rows.append(jnp.concatenate(left + [packed[:, start[a] : start[a + 1]]], axis=1))
    gram = jnp.concatenate(rows, axis=0)

    factor = 0.2 * D**0.5
    product = jnp.dot(matrix, gram, preferred_element_type=jnp.float32)
    update = (factor * (coef_linear * matrix.astype(jnp.float32) + coef_cubic * product)).astype(jnp.bfloat16)

    out = jnp.zeros_like(iterate)
    out = lax.dynamic_update_index_in_dim(out, update[:, :width], place, 0)
    for index, (table, target) in enumerate(zip(tables, targets), 1):
        back = [(to, source) for source, to in enumerate(table)]
        piece = lax.ppermute(update[:, index * width : (index + 1) * width], "loop", back)
        out = lax.dynamic_update_index_in_dim(out, piece, target, 0)
    return out


def solution(mesh):
    fsdp, loop = mesh.shape["fsdp"], mesh.shape["loop"]
    placed = (P(None, "fsdp", "loop"), P())

    def step(iterate, expert_order):
        return body(iterate, expert_order, fsdp, loop)

    return jax.shard_map(
        step, mesh=mesh, in_specs=placed, out_specs=P(None, "fsdp", "loop"), check_vma=False
    )
```

time: 642 us -> 330 us (0.51)
  blocking collectives: 329 us -> 0 us
  waiting for transfers between devices: 251 us -> 192 us
  local copies, waits for them, and re-layouts: 4.65 us -> 34.4 us
  starting transfers between devices: 0.01 us -> 20.2 us
  other arithmetic: 5.61 us -> 22.1 us
  matrix products: 33.8 us -> 46.8 us
    psum x1 -> x0, blocking collectives: 329 us -> none  [half_step(): summed = lax.psum(partial_gram, 'fsdp')]
    all_gather x1 -> x0, waiting for transfers between devices: 251 us -> none  [body(): gathered = lax.all_gather(chosen, 'loop', axis=2, tiled=True)]
    ppermute x0 -> x18, waiting for transfers between devices: none -> 192 us  [the longest x3 78 us: body(): lax.ppermute(update[:, index * width:(index + 1) * width], 'loop', back)]
    ppermute x0 -> x18, starting transfers between devices: none -> 20.2 us  [the longest x12 12 us: swap(): return lax.ppermute(value, axis, [(i, i ^ bit) for i in range(count)])]
    dot_general x2 -> x5, matrix products: 33.8 us -> 46.8 us  [the longest x1 32.4 us: body(): product = jnp.dot(matrix, gram, preferred_element_type=jnp.float32)]
    slice x0 -> x9, local copies, waits for them, and re-layouts: none -> 7.9 us  [the longest x5 3.96 us: body(): packed[:, start[a]:start[a + 1]]]
    add x0 -> x3, other arithmetic: none -> 6.85 us  [reduce_rows(): keep.astype(jnp.float32)]
    convert_element_type x0 -> x7, other arithmetic: none -> 6.66 us  [the longest x5 5.19 us: reduce_rows(): send.astype(jnp.bfloat16)]
  transfers between devices with their start and end apart: 1 -> 18, of which waited for: 1 -> 14; matrix products, arithmetic and copies ran while one was open for 0% -> 7% of each run, Pallas kernels for 0% -> 0%
where the time goes in v1:
time: 330 us; the launch traced here: 329 us
  waiting for transfers between devices  192 us (58%)
  matrix products  46.8 us (14%)
  local copies, waits for them, and re-layouts  34.4 us (10%)
  other arithmetic  22.1 us (7%)
  starting transfers between devices  20.2 us (6%)
  between operations  13.4 us (4%)
    ppermute x3, waiting for transfers between devices, body(): lax.ppermute(update[:, index * width:(index + 1) * width], 'loop', back)  78 us
    ppermute x3, waiting for transfers between devices, body(): blocks.append(lax.ppermute(mine(target), 'loop', list(enumerate(table))))  73.9 us
    ppermute x12, waiting for transfers between devices, swap(): return lax.ppermute(value, axis, [(i, i ^ bit) for i in range(count)])  40.2 us
    dot_general x1, matrix products, body(): product = jnp.dot(matrix, gram, preferred_element_type=jnp.float32)  32.4 us
    dot_general x4, matrix products, body(): lax.dot_general(blocks[a], matrix[:, a * width:], (((0,), (0,)), ((), ())...  14.3 us
    ppermute x12, starting transfers between devices, swap(): return lax.ppermute(value, axis, [(i, i ^ bit) for i in range(count)])  12 us
    add x3, other arithmetic, reduce_rows(): keep.astype(jnp.float32)  6.85 us
  transfers between devices with their start and end apart: 18, of which 14 were waited for; matrix products, arithmetic and copies ran while one was open for 7% of the time, Pallas kernels for 0%

profile of v1, /device:TPU:8, one launch (start us, length us, event | category | flops | bytes accessed | tf_op | source)
XLA Modules:
  0.0 329.0 jit_solution(8888492731691315576)
XLA Ops:
  18.3 3.3 %dynamic-slice_bitcast_fusion.3 = (bf16[896,512]{1,0:T(8,128)(2,1)}, bf16[896,512]{1,0:T(8,128)(2,1)S(1)}, bf16[896,512]{1,0:T(8,128)(2,1)S(1)}, bf16[896,512]{1,0:T(8,128)(2,1)S(1)}) fusion(bf16[4,896,512]{2,1,0:T(8,128)(2,1)} %param.5, s32[]{:T(128)S(6)} %select_n.184, s32[]{:T(128)S(6)} %select_n.186, s32[]{:T(128)S(6)} %select_n.190, s32[]{:T(128)S(6)} %select_n.188), kind=kLoop, calls=%fused_computation.62 | loop fusion | bytes 7340048 | tf_op jit(solution)/shard_map/jit(dynamic_index_in_dim)/squeeze | solution.py:63
  25.7 58.4 %collective-permute-done.2 = bf16[896,512]{1,0:T(8,128)(2,1)} collective-permute-done((bf16[896,512]{1,0:T(8,128)(2,1)S(1)}, bf16[896,512]{1,0:T(8,128)(2,1)}, u32[]{:S(2)}, u32[]{:S(2)}) %collective-permute-start.2) | collective-permute-done | bytes 917536 | tf_op jit(solution)/shard_map/ppermute | solution.py:68
  84.1 2.2 fusion.44
  86.3 15.5 %collective-permute-done.1 = bf16[896,512]{1,0:T(8,128)(2,1)} collective-permute-done((bf16[896,512]{1,0:T(8,128)(2,1)S(1)}, bf16[896,512]{1,0:T(8,128)(2,1)}, u32[]{:S(2)}, u32[]{:S(2)}) %collective-permute-start.1) | collective-permute-done | bytes 917536 | tf_op jit(solution)/shard_map/ppermute | solution.py:68
  101.8 3.1 fusion.29
  104.9 4.6 %fusion.21 = f32[512,1536]{0,1:T(8,128)S(1)} fusion(bf16[896,512]{1,0:T(8,128)(2,1)} %collective-permute-done, bf16[896,512]{1,0:T(8,128)(2,1)} %collective-permute-done.2, bf16[896,512]{1,0:T(8,128)(2,1)} %collective-permute-done.1), kind=kOutput, calls=%fused_computation.22 | convolution fusion | flops 1417543680 | bytes 5898240 | tf_op jit(solution)/shard_map/dot_general | solution.py:74
  109.5 4.4 %fusion.33 = f32[512,2048]{0,1:T(8,128)S(1)} fusion(bf16[896,512]{1,0:T(8,128)(2,1)S(1)} %copy-done.7, bf16[896,512]{1,0:T(8,128)(2,1)} %collective-permute-done.2, bf16[896,512]{1,0:T(8,128)(2,1)} %collective-permute-done.1, bf16[896,512]{1,0:T(8,128)(2,1)} %collective-permute-done), kind=kOutput, calls=%fused_computation.53 | convolution fusion | flops 1893728256 | bytes 7864320 | tf_op jit(solution)/shard_map/dot_general | solution.py:74
  114.0 3.1 select_convert_fusion.1
  117.6 2.9 collective-permute-done.3
  122.3 4.6 %convert_add_fusion.1 = (f32[256,2560]{0,1:T(8,128)S(1)}, f32[256,2560]{0,1:T(8,128)S(1)}) fusion(bf16[256,2560]{0,1:T(8,128)(2,1)} %collective-permute-done.3, pred[]{:T(512)S(6)} %eq.19, f32[512,1536]{0,1:T(8,128)S(1)} %fusion.21, f32[512,2048]{0,1:T(8,128)} %copy-done.2, bf16[256,2560]{0,1:T(8,128)(2,1)} %collective-permute-done.9, ...), kind=kLoop, calls=%fused_computation.37 | loop fusion | flops 7864320 | bytes 18350080 | tf_op jit(solution)/shard_map/add | solution.py:33
  131.1 12.8 %collective-permute-done.10 = bf16[128,2560]{0,1:T(8,128)(2,1)S(1)} collective-permute-done((bf16[128,2560]{0,1:T(8,128)(2,1)S(1)}, bf16[128,2560]{0,1:T(8,128)(2,1)S(1)}, u32[]{:S(2)}, u32[]{:S(2)}) %collective-permute-start.10) | collective-permute-done | bytes 655392 | tf_op jit(solution)/shard_map/ppermute | solution.py:19
  152.4 3.1 collective-permute-done.11
  166.4 6.3 %collective-permute-done.6 = bf16[64,2560]{1,0:T(8,128)(2,1)} collective-permute-done((bf16[64,2560]{1,0:T(8,128)(2,1)S(1)}, bf16[64,2560]{1,0:T(8,128)(2,1)}, u32[]{:S(2)}, u32[]{:S(2)}) %collective-permute-start.6) | collective-permute-done | bytes 327712 | tf_op jit(solution)/shard_map/ppermute | solution.py:19
  175.3 8.5 %collective-permute-done.13 = bf16[128,2560]{1,0:T(8,128)(2,1)S(1)} collective-permute-done((bf16[128,2560]{1,0:T(8,128)(2,1)S(1)}, bf16[128,2560]{1,0:T(8,128)(2,1)S(1)}, u32[]{:S(2)}, u32[]{:S(2)}) %collective-permute-start.13) | collective-permute-done | bytes 655392 | tf_op jit(solution)/shard_map/ppermute | solution.py:19
  188.1 3.0 copy.80
  191.2 3.1 maximum_select_fusion
  196.8 2.7 slice_bitcast_fusion.4
  201.7 3.9 %copy.84 = bf16[512,2048]{1,0:T(8,128)(2,1)} copy(bf16[512,2048]{0,1:T(8,128)(2,1)} %get-tuple-element.16) | data formatting | bytes 4194304 | tf_op jit(solution)/shard_map/slice | solution.py:85
  205.6 4.1 %copy.85 = bf16[512,2048]{1,0:T(8,128)(2,1)} copy(bf16[512,2048]{0,1:T(8,128)(2,1)} %get-tuple-element.17) | data formatting | bytes 4194304 | tf_op jit(solution)/shard_map/concatenate | solution.py:85
  209.8 32.4 %multiply_convert_fusion = bf16[896,2048]{1,0:T(8,128)(2,1)} fusion(bf16[512,512]{1,0:T(8,128)(2,1)S(1)} %slice-done.1, bf16[512,512]{1,0:T(8,128)(2,1)} %get-tuple-element.22, bf16[512,512]{1,0:T(8,128)(2,1)} %get-tuple-element.23, bf16[512,512]{1,0:T(8,128)(2,1)S(1)} %copy-done.9, bf16[512,1024]{1,0:T(8,128)(2,1)S(1)} %slice-done, ...), kind=kOutput, calls=%fused_computation.18 | convolution fusion | flops 7630225408 | bytes 15728640 | tf_op jit(solution)/shard_map/dot_general | solution.py:89
  244.1 2.5 collective-permute-start.15
  249.8 36.5 %collective-permute-done.15 = bf16[896,512]{1,0:T(8,128)(2,1)S(1)} collective-permute-done((bf16[896,512]{1,0:T(8,128)(2,1)S(1)}, bf16[896,512]{1,0:T(8,128)(2,1)S(1)}, u32[]{:S(2)}, u32[]{:S(2)}) %collective-permute-start.15) | collective-permute-done | bytes 917536 | tf_op jit(solution)/shard_map/ppermute | solution.py:96
  286.4 21.4 %collective-permute-done.16 = bf16[896,512]{1,0:T(8,128)(2,1)S(1)} collective-permute-done((bf16[896,512]{1,0:T(8,128)(2,1)S(1)}, bf16[896,512]{1,0:T(8,128)(2,1)S(1)}, u32[]{:S(2)}, u32[]{:S(2)}) %collective-permute-start.16) | collective-permute-done | bytes 917536 | tf_op jit(solution)/shard_map/ppermute | solution.py:96
  307.9 20.1 %collective-permute-done.17 = bf16[896,512]{1,0:T(8,128)(2,1)S(1)} collective-permute-done((bf16[896,512]{1,0:T(8,128)(2,1)S(1)}, bf16[896,512]{1,0:T(8,128)(2,1)S(1)}, u32[]{:S(2)}, u32[]{:S(2)}) %collective-permute-start.17) | collective-permute-done | bytes 917536 | tf_op jit(solution)/shard_map/ppermute | solution.py:96
  (84 shorter events, 52.9 us)
Async XLA Ops:
  21.6 62.5 %collective-permute-start.2 = (bf16[896,512]{1,0:T(8,128)(2,1)S(1)}, bf16[896,512]{1,0:T(8,128)(2,1)}, u32[]{:S(2)}, u32[]{:S(2)}) collective-permute-start(bf16[896,512]{1,0:T(8,128)(2,1)S(1)} %get-tuple-element.10), channel_id=1, source_target_pairs={{0,3},{1,2},{2,1},{3,0},{4,7},{5,6},{6,5},{7,4},{8,11},{9,10},{10,... | collective-permute-start | bytes 2752520 | tf_op jit(solution)/shard_map/ppermute | solution.py:68
  23.2 78.6 %collective-permute-start.1 = (bf16[896,512]{1,0:T(8,128)(2,1)S(1)}, bf16[896,512]{1,0:T(8,128)(2,1)}, u32[]{:S(2)}, u32[]{:S(2)}) collective-permute-start(bf16[896,512]{1,0:T(8,128)(2,1)S(1)} %get-tuple-element.11), channel_id=1, source_target_pairs={{0,2},{1,3},{2,0},{3,1},{4,6},{5,7},{6,4},{7,5},{8,10},{9,11},{10,... | collective-permute-start | bytes 2752520 | tf_op jit(solution)/shard_map/ppermute | solution.py:68
  24.2 80.7 %collective-permute-start = (bf16[896,512]{1,0:T(8,128)(2,1)S(1)}, bf16[896,512]{1,0:T(8,128)(2,1)}, u32[]{:S(2)}, u32[]{:S(2)}) collective-permute-start(bf16[896,512]{1,0:T(8,128)(2,1)S(1)} %get-tuple-element.9), channel_id=1, source_target_pairs={{0,1},{1,0},{2,3},{3,2},{4,5},{5,4},{6,7},{7,6},{8,9},{9,8},{10,11... | collective-permute-start | bytes 2752520 | tf_op jit(solution)/shard_map/ppermute | solution.py:68
  86.3 27.7 %copy-start.5 = (f32[512,512]{0,1:T(8,128)}, f32[512,512]{0,1:T(8,128)S(1)}, u32[]{:S(2)}) copy-start(f32[512,512]{0,1:T(8,128)S(1)} %fusion.44) | copy-start | bytes 3145732
  104.8 9.1 %copy-start.4 = (f32[512,1024]{0,1:T(8,128)}, f32[512,1024]{0,1:T(8,128)S(1)}, u32[]{:S(2)}) copy-start(f32[512,1024]{0,1:T(8,128)S(1)} %fusion.29) | copy-start | bytes 6291460
  104.9 4.7 %copy-start.7 = (bf16[896,512]{1,0:T(8,128)(2,1)S(1)}, bf16[896,512]{1,0:T(8,128)(2,1)}, u32[]{:S(2)}) copy-start(bf16[896,512]{1,0:T(8,128)(2,1)} %get-tuple-element.8) | copy-start | bytes 2752516
  117.1 3.4 %collective-permute-start.3 = (bf16[256,2560]{0,1:T(8,128)(2,1)}, bf16[256,2560]{0,1:T(8,128)(2,1)}, u32[]{:S(2)}, u32[]{:S(2)}) collective-permute-start(bf16[256,2560]{0,1:T(8,128)(2,1)} %get-tuple-element.14), channel_id=1, source_target_pairs={{0,4},{4,0},{8,12},{12,8},{16,20},{20,16},{24,28},{28,24},{1,5},{5... | collective-permute-start | bytes 3932168 | tf_op jit(solution)/shard_map/ppermute | solution.py:19
  117.1 5.2 %collective-permute-start.9 = (bf16[256,2560]{0,1:T(8,128)(2,1)}, bf16[256,2560]{0,1:T(8,128)(2,1)}, u32[]{:S(2)}, u32[]{:S(2)}) collective-permute-start(bf16[256,2560]{0,1:T(8,128)(2,1)} %get-tuple-element.15), channel_id=1, source_target_pairs={{0,4},{4,0},{8,12},{12,8},{16,20},{20,16},{24,28},{28,24},{1,5},{5... | collective-permute-start | bytes 3932168 | tf_op jit(solution)/shard_map/ppermute | solution.py:19
  126.9 17.2 %copy-start.3 = (f32[256,2560]{0,1:T(8,128)}, f32[256,2560]{0,1:T(8,128)S(1)}, u32[]{:S(2)}) copy-start(f32[256,2560]{0,1:T(8,128)S(1)} %get-tuple-element.12) | copy-start | bytes 7864324
  127.0 16.8 %collective-permute-start.10 = (bf16[128,2560]{0,1:T(8,128)(2,1)S(1)}, bf16[128,2560]{0,1:T(8,128)(2,1)S(1)}, u32[]{:S(2)}, u32[]{:S(2)}) collective-permute-start(bf16[128,2560]{0,1:T(8,128)(2,1)S(1)} %select_convert_fusion.2), channel_id=1, source_target_pairs={{0,16},{4,20},{8,24},{12,28},{16,0},{20,4},{24,8},{28,12},{1,17},{... | collective-permute-start | bytes 1966088 | tf_op jit(solution)/shard_map/ppermute | solution.py:19
  129.6 18.0 %collective-permute-start.4 = (bf16[128,2560]{0,1:T(8,128)(2,1)}, bf16[128,2560]{0,1:T(8,128)(2,1)}, u32[]{:S(2)}, u32[]{:S(2)}) collective-permute-start(bf16[128,2560]{0,1:T(8,128)(2,1)} %select_convert_fusion.4), channel_id=1, source_target_pairs={{0,8},{4,12},{8,0},{12,4},{16,24},{20,28},{24,16},{28,20},{1,9},{5... | collective-permute-start | bytes 1966088 | tf_op jit(solution)/shard_map/ppermute | solution.py:19
  146.1 9.3 %collective-permute-start.11 = (bf16[64,2560]{1,0:T(8,128)(2,1)}, bf16[64,2560]{1,0:T(8,128)(2,1)}, u32[]{:S(2)}, u32[]{:S(2)}) collective-permute-start(bf16[64,2560]{1,0:T(8,128)(2,1)} %select_convert_fusion.5), channel_id=1, source_target_pairs={{0,8},{4,12},{8,0},{12,4},{16,24},{20,28},{24,16},{28,20},{1,9},{5... | collective-permute-start | bytes 983048 | tf_op jit(solution)/shard_map/ppermute | solution.py:19
  150.9 9.1 %collective-permute-start.5 = (bf16[64,2560]{1,0:T(8,128)(2,1)}, bf16[64,2560]{1,0:T(8,128)(2,1)}, u32[]{:S(2)}, u32[]{:S(2)}) collective-permute-start(bf16[64,2560]{1,0:T(8,128)(2,1)} %copy.67), channel_id=1, source_target_pairs={{0,16},{4,20},{8,24},{12,28},{16,0},{20,4},{24,8},{28,12},{1,17},{... | collective-permute-start | bytes 983048 | tf_op jit(solution)/shard_map/ppermute | solution.py:19
  156.5 8.2 %collective-permute-start.12 = (bf16[64,2560]{1,0:T(8,128)(2,1)S(1)}, bf16[64,2560]{1,0:T(8,128)(2,1)S(1)}, u32[]{:S(2)}, u32[]{:S(2)}) collective-permute-start(bf16[64,2560]{1,0:T(8,128)(2,1)S(1)} %add_convert_fusion.1), channel_id=1, source_target_pairs={{0,8},{4,12},{8,0},{12,4},{16,24},{20,28},{24,16},{28,20},{1,9},{5... | collective-permute-start | bytes 983048 | tf_op jit(solution)/shard_map/ppermute | solution.py:19
  161.9 10.8 %collective-permute-start.6 = (bf16[64,2560]{1,0:T(8,128)(2,1)S(1)}, bf16[64,2560]{1,0:T(8,128)(2,1)}, u32[]{:S(2)}, u32[]{:S(2)}) collective-permute-start(bf16[64,2560]{1,0:T(8,128)(2,1)S(1)} %copy.69), channel_id=1, source_target_pairs={{0,16},{4,20},{8,24},{12,28},{16,0},{20,4},{24,8},{28,12},{1,17},{... | collective-permute-start | bytes 983048 | tf_op jit(solution)/shard_map/ppermute | solution.py:19
  164.8 19.0 %collective-permute-start.13 = (bf16[128,2560]{1,0:T(8,128)(2,1)S(1)}, bf16[128,2560]{1,0:T(8,128)(2,1)S(1)}, u32[]{:S(2)}, u32[]{:S(2)}) collective-permute-start(bf16[128,2560]{1,0:T(8,128)(2,1)S(1)} %maximum_select_fusion.5), channel_id=1, source_target_pairs={{0,16},{4,20},{8,24},{12,28},{16,0},{20,4},{24,8},{28,12},{1,17},{... | collective-permute-start | bytes 1966088 | tf_op jit(solution)/shard_map/ppermute | solution.py:19
  174.7 11.2 %collective-permute-start.7 = (bf16[128,2560]{0,1:T(8,128)(2,1)S(1)}, bf16[128,2560]{0,1:T(8,128)(2,1)S(1)}, u32[]{:S(2)}, u32[]{:S(2)}) collective-permute-start(bf16[128,2560]{0,1:T(8,128)(2,1)S(1)} %maximum_select_fusion.4), channel_id=1, source_target_pairs={{0,8},{4,12},{8,0},{12,4},{16,24},{20,28},{24,16},{28,20},{1,9},{5... | collective-permute-start | bytes 1966088 | tf_op jit(solution)/shard_map/ppermute | solution.py:19
  184.1 3.3 %collective-permute-start.14 = (bf16[256,2560]{1,0:T(8,128)(2,1)S(1)}, bf16[256,2560]{1,0:T(8,128)(2,1)S(1)}, u32[]{:S(2)}, u32[]{:S(2)}) collective-permute-start(bf16[256,2560]{1,0:T(8,128)(2,1)S(1)} %maximum_select_fusion.3), channel_id=1, source_target_pairs={{0,4},{4,0},{8,12},{12,8},{16,20},{20,16},{24,28},{28,24},{1,5},{5... | collective-permute-start | bytes 3932168 | tf_op jit(solution)/shard_map/ppermute | solution.py:19
  187.4 3.7 %collective-permute-start.8 = (bf16[256,2560]{0,1:T(8,128)(2,1)}, bf16[256,2560]{0,1:T(8,128)(2,1)}, u32[]{:S(2)}, u32[]{:S(2)}) collective-permute-start(bf16[256,2560]{0,1:T(8,128)(2,1)} %maximum_select_fusion.2), channel_id=1, source_target_pairs={{0,4},{4,0},{8,12},{12,8},{16,20},{20,16},{24,28},{28,24},{1,5},{5... | collective-permute-start | bytes 3932168 | tf_op jit(solution)/shard_map/ppermute | solution.py:19
  205.6 4.1 %copy-start.10 = (bf16[512,512]{1,0:T(8,128)(2,1)S(1)}, bf16[512,512]{1,0:T(8,128)(2,1)}, u32[]{:S(2)}) copy-start(bf16[512,512]{1,0:T(8,128)(2,1)} %get-tuple-element.20) | copy-start | bytes 1572868
  244.1 42.2 %collective-permute-start.15 = (bf16[896,512]{1,0:T(8,128)(2,1)S(1)}, bf16[896,512]{1,0:T(8,128)(2,1)S(1)}, u32[]{:S(2)}, u32[]{:S(2)}) collective-permute-start(bf16[896,512]{1,0:T(8,128)(2,1)S(1)} %get-tuple-element.7), channel_id=1, source_target_pairs={{1,0},{0,1},{3,2},{2,3},{5,4},{4,5},{7,6},{6,7},{9,8},{8,9},{11,10... | collective-permute-start | bytes 2752520 | tf_op jit(solution)/shard_map/ppermute | solution.py:96
  246.7 61.1 %collective-permute-start.16 = (bf16[896,512]{1,0:T(8,128)(2,1)S(1)}, bf16[896,512]{1,0:T(8,128)(2,1)S(1)}, u32[]{:S(2)}, u32[]{:S(2)}) collective-permute-start(bf16[896,512]{1,0:T(8,128)(2,1)S(1)} %get-tuple-element.6), channel_id=1, source_target_pairs={{2,0},{3,1},{0,2},{1,3},{6,4},{7,5},{4,6},{5,7},{10,8},{11,9},{8,1... | collective-permute-start | bytes 2752520 | tf_op jit(solution)/shard_map/ppermute | solution.py:96
  247.8 80.3 %collective-permute-start.17 = (bf16[896,512]{1,0:T(8,128)(2,1)S(1)}, bf16[896,512]{1,0:T(8,128)(2,1)S(1)}, u32[]{:S(2)}, u32[]{:S(2)}) collective-permute-start(bf16[896,512]{1,0:T(8,128)(2,1)S(1)} %get-tuple-element.5), channel_id=1, source_target_pairs={{3,0},{2,1},{1,2},{0,3},{7,4},{6,5},{5,6},{4,7},{11,8},{10,9},{9,1... | collective-permute-start | bytes 2752520 | tf_op jit(solution)/shard_map/ppermute | solution.py:96
  307.9 20.1 %copy-start.6 = (bf16[4,896,512]{2,1,0:T(8,128)(2,1)}, bf16[4,896,512]{2,1,0:T(8,128)(2,1)S(1)}, u32[]{:S(2)}) copy-start(bf16[4,896,512]{2,1,0:T(8,128)(2,1)S(1)} %bitcast_dynamic-update-slice_fusion.1) | copy-start | bytes 11010052
  (7 other events, 25.4 us)

commit v2 on v0

v2 whole, which is shorter than its diff:
```python
import functools

import jax
import jax.numpy as jnp
from jax import lax
from jax.experimental import pallas as pl
from jax.experimental.pallas import tpu as pltpu
from jax.sharding import PartitionSpec as P

D = 7168

coef_linear = 3.4445
coef_cubic = -4.775

VMEM_LIMIT = 56 * 2**20
F32, BF16 = jnp.float32, jnp.bfloat16
ANY = pl.BlockSpec(memory_space=pl.ANY)
SMEM = pl.BlockSpec(memory_space=pltpu.SMEM)
VMEM = pl.BlockSpec(memory_space=pltpu.VMEM)


def plan(loop):
    if loop == 4:
        phases = [[[(1, 2), (2, 1)], [(0, 1), (3, 2)]], [[(0, 2), (3, 1)]]]
        return [({1: 1, 2: 2}, phases), ({1: 0, 2: 3}, phases)]
    rounds = [[(p, (p + step) % loop) for p in range(loop)] for step in range(1, loop)]
    return [({p: p for p in range(loop)}, [rounds])]


def merge(tables):
    merged, index = [], []
    for table in tables:
        for i, other in enumerate(merged):
            if all(other.get(key, value) == value for key, value in table.items()):
                other.update(table)
                index.append(i)
                break
        else:
            merged.append(dict(table))
            index.append(len(merged) - 1)
    return merged, index


def lookup(table, place):
    items = sorted(table.items())
    value = jnp.int32(items[0][1])
    for key, entry in items[1:]:
        value = jnp.where(place == key, jnp.int32(entry), value)
    return value


def params():
    return pltpu.CompilerParams(vmem_limit_bytes=VMEM_LIMIT)


def struct(shape, dtype):
    return jax.ShapeDtypeStruct(shape, dtype)


def run_copies(copies):
    for copy in copies:
        copy.start()
    for copy in copies:
        copy.wait()


def pick(iterate, expert_order, tables, deps):
    def kernel(order, source, *rest):
        outs, sems = rest[len(deps) : -1], rest[-1]
        place = lax.axis_index("loop")
        run_copies(
            [
                pltpu.make_async_copy(source.at[order[lookup(table, place)]], out, sems.at[i])
                for i, (table, out) in enumerate(zip(tables, outs))
            ]
        )

    return pl.pallas_call(
        kernel,
        out_shape=[struct(iterate.shape[1:], iterate.dtype)] * len(tables),
        in_specs=[SMEM, ANY] + [ANY] * len(deps),
        out_specs=[ANY] * len(tables),
        scratch_shapes=[pltpu.SemaphoreType.DMA((len(tables),))],
        compiler_params=params(),
        name="pick",
    )(expert_order, iterate, *deps)


def gram_part(blocks, pairs):
    rows, width = blocks[0].shape
    half = width // 2
    count = len(blocks)

    def kernel(*refs):
        xs, keep, send = refs[:count], refs[count], refs[count + 1]
        side = lax.rem(lax.axis_index("fsdp"), 2)
        for out, part in ((send, 1 - side), (keep, side)):
            at = pl.multiple_of(part * half, half)
            for a in sorted({a for a, _ in pairs}):
                left = xs[a][:, pl.ds(at, half)].T
                for index, (first, b) in enumerate(pairs):
                    if first == a:
                        out[:, index * width : (index + 1) * width] = jnp.dot(
                            left, xs[b][...], preferred_element_type=F32
                        ).astype(out.dtype)

    shape = (half, len(pairs) * width)
    return pl.pallas_call(
        kernel,
        out_shape=[struct(shape, F32), struct(shape, BF16)],
        in_specs=[VMEM] * count,
        out_specs=[VMEM] * 2,
        compiler_params=params(),
        cost_estimate=pl.CostEstimate(
            flops=2 * rows * width * width * len(pairs), bytes_accessed=8 * 2**20, transcendentals=0
        ),
        name="gram_part",
    )(*blocks)


def add_split(keeps, received, bits, split):
    count = len(keeps)

    def kernel(*refs):
        ins, news, outs = refs[:count], refs[count : 2 * count], refs[2 * count :]
        me = lax.axis_index("fsdp")
        for i, bit in enumerate(bits):
            if not split:
                outs[i][...] = (ins[i][...] + news[i][...].astype(F32)).astype(BF16)
                continue
            half = ins[i].shape[0] // 2
            side = lax.rem(lax.div(me, bit), 2)
            for out, part in ((outs[count + i], 1 - side), (outs[i], side)):
                at = pl.ds(pl.multiple_of(part * half, half), half)
                out[...] = (ins[i][at, :] + news[i][at, :].astype(F32)).astype(out.dtype)

    if split:
        shapes = [(k.shape[0] // 2, k.shape[1]) for k in keeps]
        outs = [struct(s, F32) for s in shapes] + [struct(s, BF16) for s in shapes]
    else:
        outs = [struct(k.shape, BF16) for k in keeps]
    result = pl.pallas_call(
        kernel,
        out_shape=outs,
        in_specs=[VMEM] * (2 * count),
        out_specs=[VMEM] * len(outs),
        compiler_params=params(),
        name="add_split",
    )(*keeps, *received)
    return result[:count], result[count:]


def first_split(keep, received, bits):
    rows, columns = keep.shape
    half, width = rows // 2, columns // 2

    def kernel(kept, new, *outs):
        me = lax.axis_index("fsdp")
        for i, bit in enumerate(bits):
            side = lax.rem(lax.div(me, bit), 2)
            cols = slice(i * width, (i + 1) * width)
            for out, part in ((outs[2 + i], 1 - side), (outs[i], side)):
                at = pl.ds(pl.multiple_of(part * half, half), half)
                out[...] = (kept[at, cols] + new[at, cols].astype(F32)).astype(out.dtype)

    result = pl.pallas_call(
        kernel,
        out_shape=[struct((half, width), F32)] * 2 + [struct((half, width), BF16)] * 2,
        in_specs=[VMEM] * 2,
        out_specs=[VMEM] * 4,
        compiler_params=params(),
        name="first_split",
    )(keep, received)
    return result[:2], result[2:]


def join(pieces, orders, rows, columns):
    flat = [(part, mask, piece) for part, group in enumerate(pieces) for mask, piece in group]
    width = columns // 2

    def kernel(*refs):
        ins, out, sems = refs[: len(flat)], refs[-2], refs[-1]
        me = lax.axis_index("fsdp")
        copies = []
        for index, (part, mask, piece) in enumerate(flat):
            height, at = rows, jnp.int32(0)
            for bit in orders[part]:
                height //= 2
                side = lax.rem(lax.div(me, bit), 2)
                at = at + height * ((1 - side) if mask & bit else side)
            where = pl.ds(pl.multiple_of(at, height), height)
            copies.append(
                pltpu.make_async_copy(
                    ins[index], out.at[where, part * width : (part + 1) * width], sems.at[index]
                )
            )
        run_copies(copies)

    return pl.pallas_call(
        kernel,
        out_shape=struct((rows, columns), BF16),
        in_specs=[ANY] * len(flat),
        out_specs=ANY,
        scratch_shapes=[pltpu.SemaphoreType.DMA((len(flat),))],
        compiler_params=params(),
        name="join",
    )(*[piece for _, _, piece in flat])


def swap(value, bit, fsdp, places, loop):
    pairs = [(i * loop + p, (i ^ bit) * loop + p) for i in range(fsdp) for p in places]
    return lax.ppermute(value, ("fsdp", "loop"), pairs)


def reduce_gram(keep, send, fsdp, places, loop):
    rows, columns = keep.shape
    move = functools.partial(swap, fsdp=fsdp, places=places, loop=loop)
    bits = [1 << i for i in range(1, fsdp.bit_length() - 1)]
    orders = [bits, bits[::-1]]
    keeps, sends = first_split(keep, move(send, 1), [order[0] for order in orders])
    for step in range(1, len(bits) + 1):
        received = [move(value, order[step - 1]) for value, order in zip(sends, orders)]
        last = step == len(bits)
        keeps, sends = add_split(
            keeps, received, [order[0 if last else step] for order in orders], not last
        )
    pieces = []
    for value, order in zip(keeps, orders):
        group = [(0, value)]
        for bit in reversed(order):
            group = group + [(mask | bit, move(piece, bit)) for mask, piece in group]
        pieces.append(group)
    own = join(pieces, orders, rows, columns)
    return own, move(own, 1)


def update_blocks(blocks, groups, strips):
    rows, width = blocks[0].shape
    half, count = width // 2, len(blocks)
    total = count * width
    factor = 0.2 * D**0.5

    def kernel(*refs):
        xs, refs = refs[:count], refs[count:]
        gs, refs = refs[: 2 * len(groups)], refs[2 * len(groups) :]
        outs, (x, g, sems) = refs[:count], refs[count:]
        side = lax.rem(lax.axis_index("fsdp"), 2)
        copies = [
            pltpu.make_async_copy(xs[a], x.at[:, a * width : (a + 1) * width], sems.at[a])
            for a in range(count)
        ]
        for which, pairs in enumerate(groups):
            for index, (a, b) in enumerate(pairs):
                for other in range(2):
                    part = (1 - side) if other else side
                    where = pl.ds(pl.multiple_of(a * width + part * half, half), half)
                    copies.append(
                        pltpu.make_async_copy(
                            gs[2 * which + other].at[:, index * width : (index + 1) * width],
                            g.at[where, b * width : (b + 1) * width],
                            sems.at[len(copies)],
                        )
                    )
        run_copies(copies)
        for b in range(count):
            low, high = b * width, (b + 1) * width
            product = jnp.dot(x[:, :high], g[:high, low:high], preferred_element_type=F32)
            if b < count - 1:
                product += lax.dot_general(
                    x[:, high:], g[low:high, high:], (((1,), (1,)), ((), ())), preferred_element_type=F32
                )
            outs[b][...] = (
                factor * (coef_linear * x[:, low:high].astype(F32) + coef_cubic * product)
            ).astype(BF16)

    copies = count + 2 * sum(len(pairs) for pairs in groups)
    return pl.pallas_call(
        kernel,
        out_shape=[struct((rows, width), BF16)] * count,
        in_specs=[ANY] * (count + 2 * len(groups)),
        out_specs=[VMEM] * count,
        scratch_shapes=[
            pltpu.VMEM((rows, total), BF16),
            pltpu.VMEM((total, total), BF16),
            pltpu.SemaphoreType.DMA((copies,)),
        ],
        compiler_params=params(),
        cost_estimate=pl.CostEstimate(flops=2 * rows * total * total, bytes_accessed=16 * 2**20, transcendentals=0),
        name="update",
    )(*blocks, *[half for strip in strips for half in strip])


def place_slots(candidates, slots, like):
    flat = [value for wave in candidates for value in wave]

    def kernel(*refs):
        ins, out, sems = refs[: len(flat)], refs[-2], refs[-1]
        place = lax.axis_index("loop")
        for wave, tables in enumerate(slots):
            base = sum(len(candidates[w]) for w in range(wave))
            for index, table in enumerate(tables):
                for key, slot in table.items():

                    @pl.when(place == key)
                    def _(index=index, slot=slot, base=base):
                        pltpu.make_async_copy(ins[base + index], out.at[slot], sems.at[slot]).start()

        for slot in range(like.shape[0]):
            pltpu.make_async_copy(ins[0], out.at[slot], sems.at[slot]).wait()

    return pl.pallas_call(
        kernel,
        out_shape=struct(like.shape, like.dtype),
        in_specs=[ANY] * len(flat),
        out_specs=ANY,
        scratch_shapes=[pltpu.SemaphoreType.DMA((like.shape[0],))],
        compiler_params=params(),
        name="place_slots",
    )(*flat)


def body(iterate, expert_order, fsdp, loop):
    count = loop
    pairs = [(a, b) for a in range(count) for b in range(a, count)]
    groups = [pairs]
    waves = plan(loop)

    arrived, token = [], []
    for owners, phases in waves:
        blocks = []
        for rounds in phases:
            tables = [{source: owners[owner] for source, owner in step} for step in rounds]
            merged, index = merge(tables if blocks else tables + [owners])
            picked = pick(iterate, expert_order, merged, token)
            if not blocks:
                blocks.append(picked[index[-1]])
            token = [lax.ppermute(picked[i], "loop", step) for i, step in zip(index, rounds)]
            blocks.extend(token)
        arrived.append(blocks)

    candidates, slots = [], []
    for (owners, phases), blocks in zip(waves, arrived):
        places = sorted(owners)
        strips = []
        for group in groups:
            keep, send = gram_part(blocks, group)
            strips.append(reduce_gram(keep, send, fsdp, places, loop))
        updates = update_blocks(blocks, groups, strips)
        found, tables = [updates[0]], [dict(owners)]
        for value, step in zip(updates[1:], [step for rounds in phases for step in rounds]):
            found.append(lax.ppermute(value, "loop", [(owner, source) for source, owner in step]))
            tables.append({source: owners[owner] for source, owner in step})
        candidates.append(found)
        slots.append(tables)
    return place_slots(candidates, slots, iterate)


def solution(mesh):
    fsdp, loop = mesh.shape["fsdp"], mesh.shape["loop"]
    placed = (P(None, "fsdp", "loop"), P())

    def step(iterate, expert_order):
        return body(iterate, expert_order, fsdp, loop)

    return jax.shard_map(
        step, mesh=mesh, in_specs=placed, out_specs=P(None, "fsdp", "loop"), check_vma=False
    )
```

time: 642 us -> 797 us (1.24)
  Pallas kernels: 0 us -> 517 us
  blocking collectives: 329 us -> 0 us
  starting transfers between devices: 0.01 us -> 89.7 us
  waiting for transfers between devices: 251 us -> 168 us
  matrix products: 33.8 us -> 0 us
  local copies, waits for them, and re-layouts: 4.65 us -> 17.4 us
  between operations: 13.4 us -> 0.88 us
    pallas_call x0 -> x17, Pallas kernels: none -> 517 us  [the longest x4 174 us: pick(): pl.pallas_call(kernel, out_shape=[struct(iterate.shape[1:], iterate.dtype...]
    psum x1 -> x0, blocking collectives: 329 us -> none  [half_step(): summed = lax.psum(partial_gram, 'fsdp')]
    all_gather x1 -> x0, waiting for transfers between devices: 251 us -> none  [body(): gathered = lax.all_gather(chosen, 'loop', axis=2, tiled=True)]
    ppermute x0 -> x36, waiting for transfers between devices: none -> 168 us  [the longest x6 71.6 us: body(): lax.ppermute(picked[i], 'loop', step)]
    ppermute x0 -> x36, starting transfers between devices: none -> 89.7 us  [the longest x24 66.1 us: swap(): return lax.ppermute(value, ('fsdp', 'loop'), pairs)]
    dot_general x2 -> x0, matrix products: 33.8 us -> none  [the longest x1 18 us: half_step(): jnp.einsum('eic,eik->eck', left, right, preferred_element_type=jnp.float32)]
    unnamed x0 -> x72, local copies, waits for them, and re-layouts: none -> 17.4 us
  transfers between devices with their start and end apart: 1 -> 36, of which waited for: 1 -> 17; matrix products, arithmetic and copies ran while one was open for 0% -> 0% of each run, Pallas kernels for 0% -> 29%
where the time goes in v2:
time: 797 us; the launch traced here: 792 us
  Pallas kernels  517 us (65%)
  waiting for transfers between devices  168 us (21%)
  starting transfers between devices  89.7 us (11%)
  local copies, waits for them, and re-layouts  17.4 us (2%)
    pallas_call x4, Pallas kernels, pick(): pl.pallas_call(kernel, out_shape=[struct(iterate.shape[1:], iterate.dtype...  174 us
    pallas_call x2, Pallas kernels, join(): pl.pallas_call(kernel, out_shape=struct((rows, columns), BF16), in_specs=...  161 us
    pallas_call x1, Pallas kernels, place_slots(): pl.pallas_call(kernel, out_shape=struct(like.shape, like.dtype), in_specs...  112 us
    ppermute x6, waiting for transfers between devices, body(): lax.ppermute(picked[i], 'loop', step)  71.6 us
    ppermute x24, starting transfers between devices, swap(): return lax.ppermute(value, ('fsdp', 'loop'), pairs)  66.1 us
    ppermute x6, waiting for transfers between devices, body(): lax.ppermute(value, 'loop', [(owner, source) for source, owner in step])  58.3 us
    ppermute x24, waiting for transfers between devices, swap(): return lax.ppermute(value, ('fsdp', 'loop'), pairs)  37.8 us
    pallas_call x2, Pallas kernels, update_blocks(): pl.pallas_call(kernel, out_shape=[struct((rows, width), BF16)] * count, i...  26 us
  transfers between devices with their start and end apart: 36, of which 17 were waited for; matrix products, arithmetic and copies ran while one was open for 0% of the time, Pallas kernels for 29%

profile of v2, /device:TPU:8, one launch (start us, length us, event | category | flops | bytes accessed | tf_op | source)
XLA Modules:
  0.0 792.4 jit_solution(8276058931810796386)
XLA Ops:
  0.0 57.4 %pick.4 = (bf16[896,512]{1,0:T(8,128)(2,1)}, bf16[896,512]{1,0:T(8,128)(2,1)}) custom-call(s32[4]{0:T(128)} %order.7, bf16[4,896,512]{2,1,0:T(8,128)(2,1)} %source.7), custom_call_target="tpu_custom_call" | custom-call | tf_op jit(solution)/shard_map/pick/pallas_call | solution.py:78
  62.2 19.4 %collective-permute-done.1.rest_1_.refs_2_ = bf16[896,512]{1,0:T(8,128)(2,1)S(1)} collective-permute-done((bf16[896,512]{1,0:T(8,128)(2,1)}, bf16[896,512]{1,0:T(8,128)(2,1)S(1)}, u32[]{:S(2)}, u32[]{:S(2)}) %collective-permute-start.1) | collective-permute-done | bytes 917536 | tf_op jit(solution)/shard_map/ppermute | solution.py:337
  83.9 29.6 %pick.5 = bf16[896,512]{1,0:T(8,128)(2,1)} custom-call(s32[4]{0:T(128)} %order.7, bf16[4,896,512]{2,1,0:T(8,128)(2,1)} %source.7, bf16[896,512]{1,0:T(8,128)(2,1)} %copy-done.4, bf16[896,512]{1,0:T(8,128)(2,1)} %copy-done.2), custom_call_target="tpu_custom_call" | custom-call | tf_op jit(solution)/shard_map/pick/pallas_call | solution.py:78
  114.8 22.9 %collective-permute-done.2.refs_3_.rest_0_ = bf16[896,512]{1,0:T(8,128)(2,1)S(1)} collective-permute-done((bf16[896,512]{1,0:T(8,128)(2,1)}, bf16[896,512]{1,0:T(8,128)(2,1)S(1)}, u32[]{:S(2)}, u32[]{:S(2)}) %collective-permute-start.2) | collective-permute-done | bytes 917536 | tf_op jit(solution)/shard_map/ppermute | solution.py:337
  138.6 57.4 %pick.6 = (bf16[896,512]{1,0:T(8,128)(2,1)}, bf16[896,512]{1,0:T(8,128)(2,1)}) custom-call(s32[4]{0:T(128)} %order.7, bf16[4,896,512]{2,1,0:T(8,128)(2,1)} %source.7, bf16[896,512]{1,0:T(8,128)(2,1)} %copy-done.6), custom_call_target="tpu_custom_call" | custom-call | tf_op jit(solution)/shard_map/pick/pallas_call | solution.py:78
  200.8 17.6 %collective-permute-done.19.rest_1_.refs_2_ = bf16[896,512]{1,0:T(8,128)(2,1)S(1)} collective-permute-done((bf16[896,512]{1,0:T(8,128)(2,1)}, bf16[896,512]{1,0:T(8,128)(2,1)S(1)}, u32[]{:S(2)}, u32[]{:S(2)}) %collective-permute-start.19) | collective-permute-done | bytes 917536 | tf_op jit(solution)/shard_map/ppermute | solution.py:337
  220.7 29.6 %pick.7 = bf16[896,512]{1,0:T(8,128)(2,1)} custom-call(s32[4]{0:T(128)} %order.7, bf16[4,896,512]{2,1,0:T(8,128)(2,1)} %source.7, bf16[896,512]{1,0:T(8,128)(2,1)} %copy-done.5, bf16[896,512]{1,0:T(8,128)(2,1)} %copy-done.3), custom_call_target="tpu_custom_call" | custom-call | tf_op jit(solution)/shard_map/pick/pallas_call | solution.py:78
  251.6 10.0 %gram_part.2 = (f32[256,5120]{1,0:T(8,128)}, bf16[256,5120]{1,0:T(8,128)(2,1)}) custom-call(bf16[896,512]{1,0:T(8,128)(2,1)} %get-tuple-element.41.refs_0_, bf16[896,512]{1,0:T(8,128)(2,1)} %copy-done.4, bf16[896,512]{1,0:T(8,128)(2,1)} %copy-done.2, bf16[896,512]{1,0:T(8,128)(2,1)} %copy-done.6), custom_call_target="tpu_custom_call" | custom-call | flops 4697620480 | bytes 8388608 | tf_op jit(solution)/shard_map/gram_part/pallas_call | solution.py:108
  263.5 9.1 %collective-permute-done.20.refs_3_ = bf16[896,512]{1,0:T(8,128)(2,1)S(1)} collective-permute-done((bf16[896,512]{1,0:T(8,128)(2,1)}, bf16[896,512]{1,0:T(8,128)(2,1)S(1)}, u32[]{:S(2)}, u32[]{:S(2)}) %collective-permute-start.20) | collective-permute-done | bytes 917536 | tf_op jit(solution)/shard_map/ppermute | solution.py:337
  273.5 10.0 %gram_part.3 = (f32[256,5120]{1,0:T(8,128)}, bf16[256,5120]{1,0:T(8,128)(2,1)}) custom-call(bf16[896,512]{1,0:T(8,128)(2,1)} %get-tuple-element.59.refs_0_, bf16[896,512]{1,0:T(8,128)(2,1)} %copy-done.5, bf16[896,512]{1,0:T(8,128)(2,1)} %copy-done.3, bf16[896,512]{1,0:T(8,128)(2,1)} %copy-done.35), custom_call_target="tpu_custom_call" | custom-call | flops 4697620480 | bytes 8388608 | tf_op jit(solution)/shard_map/gram_part/pallas_call | solution.py:108
  287.0 5.7 first_split.2
  299.5 12.4 %collective-permute-done.4.refs_2_ = bf16[128,2560]{1,0:T(8,128)(2,1)S(1)} collective-permute-done((bf16[128,2560]{1,0:T(8,128)(2,1)}, bf16[128,2560]{1,0:T(8,128)(2,1)S(1)}, u32[]{:S(2)}, u32[]{:S(2)}) %collective-permute-start.4) | collective-permute-done | bytes 655392 | tf_op jit(solution)/shard_map/ppermute | solution.py:212
  326.8 5.7 first_split.3
  350.8 9.4 %collective-permute-done.8.refs_1_ = bf16[64,2560]{1,0:T(8,128)(2,1)S(1)} collective-permute-done((bf16[64,2560]{1,0:T(8,128)(2,1)}, bf16[64,2560]{1,0:T(8,128)(2,1)S(1)}, u32[]{:S(2)}, u32[]{:S(2)}) %collective-permute-start.8) | collective-permute-done | bytes 327712 | tf_op jit(solution)/shard_map/ppermute | solution.py:212
  380.6 80.6 %join.2.refs_4_ = bf16[256,5120]{1,0:T(8,128)(2,1)} custom-call(bf16[64,2560]{1,0:T(8,128)(2,1)} %get-tuple-element.53.refs_0_, bf16[64,2560]{1,0:T(8,128)(2,1)} %copy-done.17, bf16[64,2560]{1,0:T(8,128)(2,1)} %copy-done.19, bf16[64,2560]{1,0:T(8,128)(2,1)} %copy-done.21, bf16[64,2560]{1,0:T(8,128)(2,1)} %get-tuple-element.54.refs_4_, ...), custom_call_target="tpu_custom_call" | custom-call | tf_op jit(solution)/shard_map/join/pallas_call | solution.py:199
  484.8 4.6 collective-permute-done.27.refs_2_
  489.4 6.3 collective-permute-done.28.refs_3_
  497.2 80.6 %join.3.refs_4_ = bf16[256,5120]{1,0:T(8,128)(2,1)} custom-call(bf16[64,2560]{1,0:T(8,128)(2,1)} %get-tuple-element.71.refs_0_, bf16[64,2560]{1,0:T(8,128)(2,1)} %copy-done.23, bf16[64,2560]{1,0:T(8,128)(2,1)} %copy-done.25, bf16[64,2560]{1,0:T(8,128)(2,1)} %copy-done.27, bf16[64,2560]{1,0:T(8,128)(2,1)} %get-tuple-element.72.refs_4_, ...), custom_call_target="tpu_custom_call" | custom-call | tf_op jit(solution)/shard_map/join/pallas_call | solution.py:199
  581.2 13.0 %update.2 = (bf16[896,512]{1,0:T(8,128)(2,1)}, bf16[896,512]{1,0:T(8,128)(2,1)}, bf16[896,512]{1,0:T(8,128)(2,1)}, bf16[896,512]{1,0:T(8,128)(2,1)}) custom-call(bf16[896,512]{1,0:T(8,128)(2,1)} %get-tuple-element.41.refs_0_, bf16[896,512]{1,0:T(8,128)(2,1)} %copy-done.4, bf16[896,512]{1,0:T(8,128)(2,1)} %copy-done.2, bf16[896,512]{1,0:T(8,128)(2,1)} %copy-done.6, ...), custom_call_target="tpu_custom_call" | custom-call | flops 7516192768 | bytes 16777216 | tf_op jit(solution)/shard_map/update/pallas_call | solution.py:277
  602.2 13.0 %update.3 = (bf16[896,512]{1,0:T(8,128)(2,1)}, bf16[896,512]{1,0:T(8,128)(2,1)}, bf16[896,512]{1,0:T(8,128)(2,1)}, bf16[896,512]{1,0:T(8,128)(2,1)}) custom-call(bf16[896,512]{1,0:T(8,128)(2,1)} %get-tuple-element.59.refs_0_, bf16[896,512]{1,0:T(8,128)(2,1)} %copy-done.5, bf16[896,512]{1,0:T(8,128)(2,1)} %copy-done.3, bf16[896,512]{1,0:T(8,128)(2,1)} %copy-done.35, ...), custom_call_target="tpu_custom_call" | custom-call | flops 7516192768 | bytes 16777216 | tf_op jit(solution)/shard_map/update/pallas_call | solution.py:277
  620.8 18.8 %collective-permute-done.16.refs_2_ = bf16[896,512]{1,0:T(8,128)(2,1)S(1)} collective-permute-done((bf16[896,512]{1,0:T(8,128)(2,1)}, bf16[896,512]{1,0:T(8,128)(2,1)S(1)}, u32[]{:S(2)}, u32[]{:S(2)}) %collective-permute-start.16) | collective-permute-done | bytes 917536 | tf_op jit(solution)/shard_map/ppermute | solution.py:351
  639.7 19.2 %collective-permute-done.33.refs_5_ = bf16[896,512]{1,0:T(8,128)(2,1)S(1)} collective-permute-done((bf16[896,512]{1,0:T(8,128)(2,1)}, bf16[896,512]{1,0:T(8,128)(2,1)S(1)}, u32[]{:S(2)}, u32[]{:S(2)}) %collective-permute-start.33) | collective-permute-done | bytes 917536 | tf_op jit(solution)/shard_map/ppermute | solution.py:351
  658.9 19.7 %collective-permute-done.34.refs_6_ = bf16[896,512]{1,0:T(8,128)(2,1)S(1)} collective-permute-done((bf16[896,512]{1,0:T(8,128)(2,1)}, bf16[896,512]{1,0:T(8,128)(2,1)S(1)}, u32[]{:S(2)}, u32[]{:S(2)}) %collective-permute-start.34) | collective-permute-done | bytes 917536 | tf_op jit(solution)/shard_map/ppermute | solution.py:351
  679.9 112.3 %place_slots.1 = bf16[4,896,512]{2,1,0:T(8,128)(2,1)} custom-call(bf16[896,512]{1,0:T(8,128)(2,1)} %get-tuple-element.55.refs_0_, bf16[896,512]{1,0:T(8,128)(2,1)} %copy-done.7, bf16[896,512]{1,0:T(8,128)(2,1)} %copy-done.8, bf16[896,512]{1,0:T(8,128)(2,1)} %copy-done.9, bf16[896,512]{1,0:T(8,128)(2,1)} %get-tuple-element.73.refs_4_, ...), custom_call_target="tpu_custom_call" | custom-call | tf_op jit(solution)/shard_map/place_slots/pallas_call | solution.py:311
  (137 shorter events, 127.2 us)
Async XLA Ops:
  57.4 24.2 %collective-permute-start.1 = (bf16[896,512]{1,0:T(8,128)(2,1)}, bf16[896,512]{1,0:T(8,128)(2,1)S(1)}, u32[]{:S(2)}, u32[]{:S(2)}) collective-permute-start(bf16[896,512]{1,0:T(8,128)(2,1)} %get-tuple-element.42), channel_id=1, source_target_pairs={{0,1},{3,2},{4,5},{7,6},{8,9},{11,10},{12,13},{15,14},{16,17},{19,... | collective-permute-start | bytes 2752520 | tf_op jit(solution)/shard_map/ppermute | solution.py:337
  58.7 24.2 %collective-permute-start = (bf16[896,512]{1,0:T(8,128)(2,1)}, bf16[896,512]{1,0:T(8,128)(2,1)S(1)}, u32[]{:S(2)}, u32[]{:S(2)}) collective-permute-start(bf16[896,512]{1,0:T(8,128)(2,1)} %get-tuple-element.42), channel_id=1, source_target_pairs={{1,2},{2,1},{5,6},{6,5},{9,10},{10,9},{13,14},{14,13},{17,18},{18,... | collective-permute-start | bytes 2752520 | tf_op jit(solution)/shard_map/ppermute | solution.py:337
  113.5 24.2 %collective-permute-start.2 = (bf16[896,512]{1,0:T(8,128)(2,1)}, bf16[896,512]{1,0:T(8,128)(2,1)S(1)}, u32[]{:S(2)}, u32[]{:S(2)}) collective-permute-start(bf16[896,512]{1,0:T(8,128)(2,1)} %pick.5), channel_id=1, source_target_pairs={{0,2},{3,1},{4,6},{7,5},{8,10},{11,9},{12,14},{15,13},{16,18},{19,... | collective-permute-start | bytes 2752520 | tf_op jit(solution)/shard_map/ppermute | solution.py:337
  196.0 22.4 %collective-permute-start.19 = (bf16[896,512]{1,0:T(8,128)(2,1)}, bf16[896,512]{1,0:T(8,128)(2,1)S(1)}, u32[]{:S(2)}, u32[]{:S(2)}) collective-permute-start(bf16[896,512]{1,0:T(8,128)(2,1)} %get-tuple-element.60), channel_id=1, source_target_pairs={{0,1},{3,2},{4,5},{7,6},{8,9},{11,10},{12,13},{15,14},{16,17},{19,... | collective-permute-start | bytes 2752520 | tf_op jit(solution)/shard_map/ppermute | solution.py:337
  197.3 22.4 %collective-permute-start.18 = (bf16[896,512]{1,0:T(8,128)(2,1)}, bf16[896,512]{1,0:T(8,128)(2,1)S(1)}, u32[]{:S(2)}, u32[]{:S(2)}) collective-permute-start(bf16[896,512]{1,0:T(8,128)(2,1)} %get-tuple-element.60), channel_id=1, source_target_pairs={{1,2},{2,1},{5,6},{6,5},{9,10},{10,9},{13,14},{14,13},{17,18},{18,... | collective-permute-start | bytes 2752520 | tf_op jit(solution)/shard_map/ppermute | solution.py:337
  250.3 22.4 %collective-permute-start.20 = (bf16[896,512]{1,0:T(8,128)(2,1)}, bf16[896,512]{1,0:T(8,128)(2,1)S(1)}, u32[]{:S(2)}, u32[]{:S(2)}) collective-permute-start(bf16[896,512]{1,0:T(8,128)(2,1)} %pick.7), channel_id=1, source_target_pairs={{0,2},{3,1},{4,6},{7,5},{8,10},{11,9},{12,14},{15,13},{16,18},{19,... | collective-permute-start | bytes 2752520 | tf_op jit(solution)/shard_map/ppermute | solution.py:337
  261.6 23.9 %collective-permute-start.3 = (bf16[256,5120]{1,0:T(8,128)(2,1)}, bf16[256,5120]{1,0:T(8,128)(2,1)S(1)}, u32[]{:S(2)}, u32[]{:S(2)}) collective-permute-start(bf16[256,5120]{1,0:T(8,128)(2,1)} %get-tuple-element.44), channel_id=1, source_target_pairs={{1,5},{2,6},{5,1},{6,2},{9,13},{10,14},{13,9},{14,10},{17,21},{18,... | collective-permute-start | bytes 7864328 | tf_op jit(solution)/shard_map/ppermute | solution.py:212
  283.6 41.7 %collective-permute-start.21 = (bf16[256,5120]{1,0:T(8,128)(2,1)}, bf16[256,5120]{1,0:T(8,128)(2,1)S(1)}, u32[]{:S(2)}, u32[]{:S(2)}) collective-permute-start(bf16[256,5120]{1,0:T(8,128)(2,1)} %get-tuple-element.62), channel_id=1, source_target_pairs={{1,5},{2,6},{5,1},{6,2},{9,13},{10,14},{13,9},{14,10},{17,21},{18,... | collective-permute-start | bytes 7864328 | tf_op jit(solution)/shard_map/ppermute | solution.py:212
  292.7 19.2 %collective-permute-start.4 = (bf16[128,2560]{1,0:T(8,128)(2,1)}, bf16[128,2560]{1,0:T(8,128)(2,1)S(1)}, u32[]{:S(2)}, u32[]{:S(2)}) collective-permute-start(bf16[128,2560]{1,0:T(8,128)(2,1)} %get-tuple-element.47), channel_id=1, source_target_pairs={{1,9},{2,10},{5,13},{6,14},{9,1},{10,2},{13,5},{14,6},{17,25},{18,... | collective-permute-start | bytes 1966088 | tf_op jit(solution)/shard_map/ppermute | solution.py:212
  296.1 19.0 %collective-permute-start.5 = (bf16[128,2560]{1,0:T(8,128)(2,1)}, bf16[128,2560]{1,0:T(8,128)(2,1)S(1)}, u32[]{:S(2)}, u32[]{:S(2)}) collective-permute-start(bf16[128,2560]{1,0:T(8,128)(2,1)} %get-tuple-element.48), channel_id=1, source_target_pairs={{1,17},{2,18},{5,21},{6,22},{9,25},{10,26},{13,29},{14,30},{17,1},... | collective-permute-start | bytes 1966088 | tf_op jit(solution)/shard_map/ppermute | solution.py:212
  319.4 18.9 %collective-permute-start.6 = (bf16[64,2560]{1,0:T(8,128)(2,1)}, bf16[64,2560]{1,0:T(8,128)(2,1)S(1)}, u32[]{:S(2)}, u32[]{:S(2)}) collective-permute-start(bf16[64,2560]{1,0:T(8,128)(2,1)} %get-tuple-element.51), channel_id=1, source_target_pairs={{1,17},{2,18},{5,21},{6,22},{9,25},{10,26},{13,29},{14,30},{17,1},... | collective-permute-start | bytes 983048 | tf_op jit(solution)/shard_map/ppermute | solution.py:212
  332.5 32.6 %collective-permute-start.22 = (bf16[128,2560]{1,0:T(8,128)(2,1)}, bf16[128,2560]{1,0:T(8,128)(2,1)S(1)}, u32[]{:S(2)}, u32[]{:S(2)}) collective-permute-start(bf16[128,2560]{1,0:T(8,128)(2,1)} %get-tuple-element.65), channel_id=1, source_target_pairs={{1,9},{2,10},{5,13},{6,14},{9,1},{10,2},{13,5},{14,6},{17,25},{18,... | collective-permute-start | bytes 1966088 | tf_op jit(solution)/shard_map/ppermute | solution.py:212
  335.9 32.9 %collective-permute-start.23 = (bf16[128,2560]{1,0:T(8,128)(2,1)}, bf16[128,2560]{1,0:T(8,128)(2,1)S(1)}, u32[]{:S(2)}, u32[]{:S(2)}) collective-permute-start(bf16[128,2560]{1,0:T(8,128)(2,1)} %get-tuple-element.66), channel_id=1, source_target_pairs={{1,17},{2,18},{5,21},{6,22},{9,25},{10,26},{13,29},{14,30},{17,1},... | collective-permute-start | bytes 1966088 | tf_op jit(solution)/shard_map/ppermute | solution.py:212
  347.4 28.2 %collective-permute-start.9 = (bf16[64,2560]{1,0:T(8,128)(2,1)}, bf16[64,2560]{1,0:T(8,128)(2,1)S(1)}, u32[]{:S(2)}, u32[]{:S(2)}) collective-permute-start(bf16[64,2560]{1,0:T(8,128)(2,1)} %get-tuple-element.53.refs_0_), channel_id=1, source_target_pairs={{1,9},{2,10},{5,13},{6,14},{9,1},{10,2},{13,5},{14,6},{17,25},{18,... | collective-permute-start | bytes 983048 | tf_op jit(solution)/shard_map/ppermute | solution.py:212
  373.2 90.0 %collective-permute-start.24 = (bf16[64,2560]{1,0:T(8,128)(2,1)}, bf16[64,2560]{1,0:T(8,128)(2,1)S(1)}, u32[]{:S(2)}, u32[]{:S(2)}) collective-permute-start(bf16[64,2560]{1,0:T(8,128)(2,1)} %get-tuple-element.69), channel_id=1, source_target_pairs={{1,17},{2,18},{5,21},{6,22},{9,25},{10,26},{13,29},{14,30},{17,1},... | collective-permute-start | bytes 983048 | tf_op jit(solution)/shard_map/ppermute | solution.py:212
  375.6 87.6 %collective-permute-start.25 = (bf16[64,2560]{1,0:T(8,128)(2,1)}, bf16[64,2560]{1,0:T(8,128)(2,1)S(1)}, u32[]{:S(2)}, u32[]{:S(2)}) collective-permute-start(bf16[64,2560]{1,0:T(8,128)(2,1)} %get-tuple-element.70), channel_id=1, source_target_pairs={{1,9},{2,10},{5,13},{6,14},{9,1},{10,2},{13,5},{14,6},{17,25},{18,... | collective-permute-start | bytes 983048 | tf_op jit(solution)/shard_map/ppermute | solution.py:212
  461.2 118.5 %collective-permute-start.14 = (bf16[256,5120]{1,0:T(8,128)(2,1)}, bf16[256,5120]{1,0:T(8,128)(2,1)S(1)}, u32[]{:S(2)}, u32[]{:S(2)}) collective-permute-start(bf16[256,5120]{1,0:T(8,128)(2,1)} %join.2.refs_4_), channel_id=1, source_target_pairs={{1,5},{2,6},{5,1},{6,2},{9,13},{10,14},{13,9},{14,10},{17,21},{18,... | collective-permute-start | bytes 7864328 | tf_op jit(solution)/shard_map/ppermute | solution.py:212
  577.8 22.9 %collective-permute-start.32 = (bf16[256,5120]{1,0:T(8,128)(2,1)}, bf16[256,5120]{1,0:T(8,128)(2,1)S(1)}, u32[]{:S(2)}, u32[]{:S(2)}) collective-permute-start(bf16[256,5120]{1,0:T(8,128)(2,1)} %join.3.refs_4_), channel_id=1, source_target_pairs={{1,5},{2,6},{5,1},{6,2},{9,13},{10,14},{13,9},{14,10},{17,21},{18,... | collective-permute-start | bytes 7864328 | tf_op jit(solution)/shard_map/ppermute | solution.py:212
  594.2 25.3 %collective-permute-start.15 = (bf16[896,512]{1,0:T(8,128)(2,1)}, bf16[896,512]{1,0:T(8,128)(2,1)S(1)}, u32[]{:S(2)}, u32[]{:S(2)}) collective-permute-start(bf16[896,512]{1,0:T(8,128)(2,1)} %get-tuple-element.56), channel_id=1, source_target_pairs={{2,1},{1,2},{6,5},{5,6},{10,9},{9,10},{14,13},{13,14},{18,17},{17,... | collective-permute-start | bytes 2752520 | tf_op jit(solution)/shard_map/ppermute | solution.py:351
  597.7 41.9 %collective-permute-start.16 = (bf16[896,512]{1,0:T(8,128)(2,1)}, bf16[896,512]{1,0:T(8,128)(2,1)S(1)}, u32[]{:S(2)}, u32[]{:S(2)}) collective-permute-start(bf16[896,512]{1,0:T(8,128)(2,1)} %get-tuple-element.57), channel_id=1, source_target_pairs={{1,0},{2,3},{5,4},{6,7},{9,8},{10,11},{13,12},{14,15},{17,16},{18,... | collective-permute-start | bytes 2752520 | tf_op jit(solution)/shard_map/ppermute | solution.py:351
  599.1 40.6 %collective-permute-start.17 = (bf16[896,512]{1,0:T(8,128)(2,1)}, bf16[896,512]{1,0:T(8,128)(2,1)S(1)}, u32[]{:S(2)}, u32[]{:S(2)}) collective-permute-start(bf16[896,512]{1,0:T(8,128)(2,1)} %get-tuple-element.58), channel_id=1, source_target_pairs={{2,0},{1,3},{6,4},{5,7},{10,8},{9,11},{14,12},{13,15},{18,16},{17,... | collective-permute-start | bytes 2752520 | tf_op jit(solution)/shard_map/ppermute | solution.py:351
  615.2 43.7 %collective-permute-start.33 = (bf16[896,512]{1,0:T(8,128)(2,1)}, bf16[896,512]{1,0:T(8,128)(2,1)S(1)}, u32[]{:S(2)}, u32[]{:S(2)}) collective-permute-start(bf16[896,512]{1,0:T(8,128)(2,1)} %get-tuple-element.74), channel_id=1, source_target_pairs={{2,1},{1,2},{6,5},{5,6},{10,9},{9,10},{14,13},{13,14},{18,17},{17,... | collective-permute-start | bytes 2752520 | tf_op jit(solution)/shard_map/ppermute | solution.py:351
  617.6 61.0 %collective-permute-start.34 = (bf16[896,512]{1,0:T(8,128)(2,1)}, bf16[896,512]{1,0:T(8,128)(2,1)S(1)}, u32[]{:S(2)}, u32[]{:S(2)}) collective-permute-start(bf16[896,512]{1,0:T(8,128)(2,1)} %get-tuple-element.75), channel_id=1, source_target_pairs={{1,0},{2,3},{5,4},{6,7},{9,8},{10,11},{13,12},{14,15},{17,16},{18,... | collective-permute-start | bytes 2752520 | tf_op jit(solution)/shard_map/ppermute | solution.py:351
  619.5 59.1 %collective-permute-start.35 = (bf16[896,512]{1,0:T(8,128)(2,1)}, bf16[896,512]{1,0:T(8,128)(2,1)S(1)}, u32[]{:S(2)}, u32[]{:S(2)}) collective-permute-start(bf16[896,512]{1,0:T(8,128)(2,1)} %get-tuple-element.76), channel_id=1, source_target_pairs={{2,0},{1,3},{6,4},{5,7},{10,8},{9,11},{14,12},{13,15},{18,16},{17,... | collective-permute-start | bytes 2752520 | tf_op jit(solution)/shard_map/ppermute | solution.py:351
  (48 other events, 456.2 us)

commit v3 on v0

v3 whole, which is shorter than its diff:
```python
import jax
import jax.numpy as jnp
from jax import lax
from jax.experimental import pallas as pl
from jax.experimental.pallas import tpu as pltpu
from jax.sharding import PartitionSpec as P

D = 7168

coef_linear = 3.4445
coef_cubic = -4.775

MIB = 2**20
F32, BF16 = jnp.float32, jnp.bfloat16
ANY = pl.BlockSpec(memory_space=pl.ANY)
SMEM = pl.BlockSpec(memory_space=pltpu.SMEM)
VMEM = pl.BlockSpec(memory_space=pltpu.VMEM)


def plan(loop, fsdp):
    levels = fsdp.bit_length() - 2
    if loop == 4 and levels == 2:
        phases = [[[0, 2, 1, 3], [1, 0, 3, 2]], [[2, 0, 3, 1]]]
        order = """
            0pick0 0pick1 0gram0 0split0 0add00 1pick0 0gram1 0add01 0split1 0add10 1pick1 1gram0 0add11
            1split0 0join0 1add00 1gram1 0join1 1split1 0update31 0update20
            1add01 1add10 1add11 0need3 1join0 0need2 1join1 0need1 1update31 1update20
        """
        turns = [(int(t[0]), t[1:].rstrip("0123456789"), [int(c) for c in t[1:] if c.isdigit()]) for t in order.split()]
        return [({1: 1, 2: 2}, phases), ({1: 0, 2: 3}, phases)], turns
    rounds = [[(p + step) % loop for p in range(loop)] for step in range(1, loop)]
    turns = [(0, "pick", [0]), (0, "gram", [0]), (0, "split", [0])]
    turns += [(0, "add", [0, i]) for i in range(levels)] + [(0, "join", [i]) for i in range(levels)]
    return [({p: p for p in range(loop)}, [rounds])], turns + [(0, "update", list(range(loop)))]


def sends(owners, step):
    return {p: owners[to] for p, to in enumerate(step) if to in owners and to != p}


def merge(tables):
    merged, index = [], []
    for table in tables:
        for i, other in enumerate(merged):
            if all(other.get(key, value) == value for key, value in table.items()):
                other.update(table)
                index.append(i)
                break
        else:
            merged.append(dict(table))
            index.append(len(merged) - 1)
    return merged, index


def lookup(table, place):
    items = sorted(table.items())
    value = jnp.int32(items[0][1])
    for key, entry in items[1:]:
        value = jnp.where(place == key, jnp.int32(entry), value)
    return value


def struct(shape, dtype):
    return jax.ShapeDtypeStruct(shape, dtype)


def call(kernel, name, ins, specs, outs, mib, scratch=(), after=()):
    count, extra = len(ins), len(after)

    def wrapped(*refs):
        kernel(*refs[:count], *refs[count + extra :])

    result = pl.pallas_call(
        wrapped,
        out_shape=outs,
        in_specs=list(specs) + [ANY] * extra,
        out_specs=[VMEM] * len(outs),
        scratch_shapes=list(scratch),
        compiler_params=pltpu.CompilerParams(vmem_limit_bytes=int(mib * MIB)),
        cost_estimate=pl.CostEstimate(flops=0, bytes_accessed=1, transcendentals=0),
        name=name,
    )(*ins, *after)
    return list(result)


def run_copies(copies):
    for copy in copies:
        copy.start()
    for copy in copies:
        copy.wait()


def side_of(bit):
    return lax.rem(lax.div(lax.axis_index("fsdp"), bit), 2)


def rows_at(part, height):
    return pl.ds(pl.multiple_of(part * height, height), height)


def pick(iterate, expert_order, tables, after):
    def kernel(order, source, *rest):
        outs, sems = rest[:-1], rest[-1]
        place = lax.axis_index("loop")
        run_copies(
            [
                pltpu.make_async_copy(source.at[order[lookup(table, place)]], out, sems.at[i])
                for i, (table, out) in enumerate(zip(tables, outs))
            ]
        )

    outs = [struct(iterate.shape[1:], iterate.dtype)] * len(tables)
    sems = [pltpu.SemaphoreType.DMA((len(tables),))]
    return call(kernel, "pick", [expert_order, iterate], [SMEM, ANY], outs, 8, sems, after=after)


def gram_part(blocks, pairs, chunks, after):
    rows, width = blocks[0].shape
    half, count = width // 2, len(blocks)
    total = len(pairs) * width
    piece = total // chunks

    def kernel(*refs):
        xs, keep, sent, left = refs[:count], refs[count], refs[count + 1 : -1], refs[-1]
        side = side_of(1)
        for sending, part in ((True, 1 - side), (False, side)):
            for a in sorted({a for a, _ in pairs}):
                left[a * half : (a + 1) * half, :] = xs[a][:, rows_at(part, half)].T
            for b in sorted({b for _, b in pairs}):
                firsts = [a for a, second in pairs if second == b]
                product = jnp.dot(left[: len(firsts) * half, :], xs[b][...], preferred_element_type=F32)
                for a in firsts:
                    value = product[a * half : (a + 1) * half]
                    at = pairs.index((a, b)) * width
                    if not sending:
                        keep[:, at : at + width] = value
                        continue
                    done = 0
                    while done < width:
                        chunk, offset = divmod(at + done, piece)
                        size = min(piece - offset, width - done)
                        sent[chunk][:, offset : offset + size] = value[:, done : done + size].astype(BF16)
                        done += size

    outs = [struct((half, total), F32)] + [struct((half, piece), BF16)] * chunks
    scratch = [pltpu.VMEM((count * half, rows), BF16)]
    result = call(kernel, "gram_part", blocks, [VMEM] * count, outs, 20, scratch, after)
    return result[0], result[1:]


def first_split(keep, received, bits, after):
    rows, columns = keep.shape
    half, width = rows // 2, columns // 2
    chunks = len(received)
    piece = columns // chunks

    def kernel(kept, *refs):
        news, outs = refs[:chunks], refs[chunks:]
        for chunk, new in enumerate(news):
            i, offset = divmod(chunk * piece, width)
            side = side_of(bits[i])
            cols = slice(chunk * piece, (chunk + 1) * piece)
            for out, part in ((outs[2 + i], 1 - side), (outs[i], side)):
                at = rows_at(part, half)
                out[:, offset : offset + piece] = (kept[at, cols] + new[at, :].astype(F32)).astype(out.dtype)

    outs = [struct((half, width), F32)] * 2 + [struct((half, width), BF16)] * 2
    result = call(kernel, "first_split", [keep, *received], [VMEM] * (1 + chunks), outs, 14, after=after)
    return result[:2], result[2:]


def add_split(keeps, received, earlier, bits, after):
    count = len(keeps)
    ins_count = (2 + len(earlier)) * count
    before = sum(values[0].shape[1] for values in earlier)

    def kernel(*refs):
        ins, news, olds, outs = refs[:count], refs[count : 2 * count], refs[2 * count : ins_count], refs[ins_count:]
        for i in range(count):
            if not bits:
                done = 0
                for old in olds[i::count]:
                    outs[i][:, done : done + old.shape[1]] = old[...]
                    done += old.shape[1]
                outs[i][:, before:] = (ins[i][...] + news[i][...].astype(F32)).astype(BF16)
                continue
            half = ins[i].shape[0] // 2
            side = side_of(bits[i])
            for out, part in ((outs[count + i], 1 - side), (outs[i], side)):
                at = rows_at(part, half)
                out[...] = (ins[i][at, :] + news[i][at, :].astype(F32)).astype(out.dtype)

    if bits:
        shapes = [(k.shape[0] // 2, k.shape[1]) for k in keeps]
        outs = [struct(s, F32) for s in shapes] + [struct(s, BF16) for s in shapes]
    else:
        outs = [struct((k.shape[0], before + k.shape[1]), BF16) for k in keeps]
    ins = [*keeps, *received, *[value for values in earlier for value in values]]
    result = call(kernel, "add_split", ins, [VMEM] * ins_count, outs, 8, after=after)
    return result[:count], result[count:]


def join(values, received, bits, chunks, after):
    count = len(values)
    rows, width = values[0].shape

    def kernel(*refs):
        ins, news, outs = refs[:count], refs[count : 2 * count], refs[2 * count :]
        for i, bit in enumerate(bits):
            side = side_of(bit)
            for source, part in ((ins[i], side), (news[i], 1 - side)):
                at = rows_at(part, rows)
                if not chunks:
                    outs[i][at, :] = source[...]
                    continue
                piece = count * width // chunks
                for chunk in range(chunks):
                    low, high = max(chunk * piece, i * width), min((chunk + 1) * piece, (i + 1) * width)
                    if low < high:
                        outs[chunk][at, low - chunk * piece : high - chunk * piece] = source[
                            :, low - i * width : high - i * width
                        ]

    if chunks:
        outs = [struct((2 * rows, count * width // chunks), BF16)] * chunks
    else:
        outs = [struct((2 * rows, width), BF16)] * count
    return call(kernel, "join", [*values, *received], [VMEM] * (2 * count), outs, 8, after=after)


def swap(value, bit, fsdp):
    return lax.ppermute(value, "fsdp", [(i, i ^ bit) for i in range(fsdp)])


def update_blocks(blocks, places, own, other, wanted, after):
    rows, width = blocks[0].shape
    half, count = width // 2, len(blocks)
    total, chunks, piece = count * width, len(own), own[0].shape[1]
    factor = 0.2 * D**0.5

    def kernel(*refs):
        xs, strips = refs[:count], (refs[count : count + chunks], refs[count + chunks : count + 2 * chunks])
        refs = refs[count + 2 * chunks :]
        outs, (x, g) = refs[: len(wanted)], refs[len(wanted) :]
        side = side_of(1)
        for a in range(count):
            x[:, a * width : (a + 1) * width] = xs[a][...]
        for part, strip in zip((side, 1 - side), strips):
            for (a, b), column in places.items():
                if a not in wanted and b not in wanted:
                    continue
                where = pl.ds(pl.multiple_of(a * width + part * half, half), half)
                done = 0
                while done < width:
                    chunk, offset = divmod(column + done, piece)
                    size = min(piece - offset, width - done)
                    at = b * width + done
                    g[where, at : at + size] = strip[chunk][:, offset : offset + size]
                    done += size
        for out, b in zip(outs, wanted):
            low, high = b * width, (b + 1) * width
            product = jnp.dot(x[:, :high], g[:high, low:high], preferred_element_type=F32)
            if b < count - 1:
                product += lax.dot_general(
                    x[:, high:], g[low:high, high:], (((1,), (1,)), ((), ())), preferred_element_type=F32
                )
            out[...] = (factor * (coef_linear * x[:, low:high].astype(F32) + coef_cubic * product)).astype(BF16)

    scratch = [pltpu.VMEM((rows, total), BF16), pltpu.VMEM((total, total), BF16)]
    outs = [struct((rows, width), BF16)] * len(wanted)
    ins = [*blocks, *own, *other]
    return call(kernel, "update", ins, [VMEM] * len(ins), outs, 30, scratch, after)


def place_slots(candidates, slots, like, after):
    flat = [value for wave in candidates for value in wave]

    def kernel(*refs):
        ins, out, sems = refs[: len(flat)], refs[-2], refs[-1]
        place = lax.axis_index("loop")
        base = 0
        for wave, tables in enumerate(slots):
            for index, table in enumerate(tables):
                for key, slot in table.items():

                    @pl.when(place == key)
                    def _(source=ins[base + index], slot=slot):
                        pltpu.make_async_copy(source, out.at[slot], sems.at[slot]).start()

            base += len(tables)
        for slot in range(like.shape[0]):
            pltpu.make_async_copy(ins[0], out.at[slot], sems.at[slot]).wait()

    sems = [pltpu.SemaphoreType.DMA((like.shape[0],))]
    outs = [struct(like.shape, like.dtype)]
    return call(kernel, "place_slots", flat, [ANY] * len(flat), outs, 8, sems, after=after)[0]


class Wave:
    def __init__(self, iterate, expert_order, owners, phases, fsdp, chunks, shared):
        self.iterate, self.expert_order, self.owners, self.phases = iterate, expert_order, owners, phases
        self.fsdp, self.chunks, self.shared = fsdp, chunks, shared
        self.bits = [1 << i for i in range(1, fsdp.bit_length() - 1)]
        self.orders = [self.bits, self.bits[::-1]]
        self.blocks, self.groups, self.state, self.gathered = [], [], {}, None
        self.rounds = [step for rounds in phases for step in rounds]
        self.updates = {}

    def move(self, values, bits):
        return [swap(value, bit, self.fsdp) for value, bit in zip(values, bits)]

    def pick(self, phase):
        rounds, first = self.phases[phase], len(self.blocks)
        tables = [sends(self.owners, step) for step in rounds]
        merged, index = merge(tables if phase else tables + [self.owners])
        picked = pick(self.iterate, self.expert_order, merged, self.shared["last"] + self.shared["arrived"])
        if not phase:
            self.blocks.append(picked[index[-1]])
        arrived = [lax.ppermute(picked[i], "loop", list(enumerate(step))) for i, step in zip(index, rounds)]
        self.blocks.extend(arrived)
        count = len(self.blocks)
        self.groups.append([(a, b) for b in range(first, count) for a in range(b + 1)])
        self.shared["last"], self.shared["arrived"] = picked[:1], arrived

    def gram(self, group):
        pairs = self.groups[group]
        blocks = self.blocks[: 1 + max(b for _, b in pairs)]
        keep, out = gram_part(blocks, pairs, self.chunks, self.shared["last"])
        self.shared["last"] = [keep]
        self.state[group] = keep, self.move(out, [1] * self.chunks)

    def split(self, group):
        keep, received = self.state[group]
        firsts = [order[0] for order in self.orders]
        keeps, out = first_split(keep, received, firsts, self.shared["last"])
        self.shared["last"] = keeps[:1]
        self.state[group] = keeps, self.move(out, firsts)

    def add(self, group, level):
        keeps, received = self.state[group]
        bits = [order[level + 1] for order in self.orders if level + 1 < len(order)]
        last = not bits and group == len(self.phases) - 1
        earlier = [self.state[g] for g in range(group)] if last else []
        keeps, out = add_split(keeps, received, earlier, bits, self.shared["last"])
        self.shared["last"] = keeps[:1]
        self.state[group] = (keeps, self.move(out, bits)) if bits else keeps
        if last:
            self.gathered = keeps, self.move(keeps, [order[-1] for order in self.orders])

    def join(self, level):
        left = len(self.bits) - 1 - level
        bits = [order[left] for order in self.orders]
        values = join(*self.gathered, bits, 0 if left else self.chunks, self.shared["last"])
        self.shared["last"] = values[:1]
        bits = [order[left - 1] for order in self.orders] if left else [1] * self.chunks
        self.gathered = values, self.move(values, bits)

    def places(self):
        width, found, column = self.blocks[0].shape[1], {}, 0
        for part in range(2):
            for pairs in self.groups:
                half = len(pairs) // 2
                for pair in pairs[part * half : (part + 1) * half]:
                    found[pair] = column
                    column += width
        return found

    def update(self, *wanted):
        values = update_blocks(self.blocks, self.places(), *self.gathered, wanted, self.shared["last"])
        self.shared["last"] = values[:1]
        for b, value in zip(wanted, values):
            if b:
                back = [(to, source) for source, to in enumerate(self.rounds[b - 1])]
                value = lax.ppermute(value, "loop", back)
            self.updates[b] = value

    def need(self, b):
        self.shared["last"] = self.shared["last"] + [self.updates[b]]

    def result(self):
        tables = [self.owners] + [sends(self.owners, step) for step in self.rounds]
        return [self.updates[b] for b in range(len(tables))], tables


def body(iterate, expert_order, fsdp, loop):
    waves, turns = plan(loop, fsdp)
    shared = {"last": [], "arrived": []}
    waves = [Wave(iterate, expert_order, owners, phases, fsdp, 4, shared) for owners, phases in waves]
    for turn, step, arguments in turns:
        getattr(waves[turn], step)(*arguments)
    results = [wave.result() for wave in waves]
    return place_slots([found for found, _ in results], [tables for _, tables in results], iterate, shared["last"])


def solution(mesh):
    fsdp, loop = mesh.shape["fsdp"], mesh.shape["loop"]
    placed = (P(None, "fsdp", "loop"), P())

    def step(iterate, expert_order):
        return body(iterate, expert_order, fsdp, loop)

    return jax.shard_map(
        step, mesh=mesh, in_specs=placed, out_specs=P(None, "fsdp", "loop"), check_vma=False
    )
```

time: 642 us -> 247 us (0.38)
  blocking collectives: 329 us -> 0 us
  waiting for transfers between devices: 251 us -> 153 us
  starting transfers between devices: 0.01 us -> 49.1 us
  Pallas kernels: 0 us -> 37.3 us
  matrix products: 33.8 us -> 0 us
  between operations: 13.4 us -> 0.58 us
    psum x1 -> x0, blocking collectives: 329 us -> none  [half_step(): summed = lax.psum(partial_gram, 'fsdp')]
    all_gather x1 -> x0, waiting for transfers between devices: 251 us -> none  [body(): gathered = lax.all_gather(chosen, 'loop', axis=2, tiled=True)]
    ppermute x0 -> x60, waiting for transfers between devices: none -> 153 us  [the longest x48 79.5 us: swap(): return lax.ppermute(value, 'fsdp', [(i, i ^ bit) for i in range(fsdp)])]
    ppermute x0 -> x60, starting transfers between devices: none -> 49.1 us  [the longest x48 31.1 us: swap(): return lax.ppermute(value, 'fsdp', [(i, i ^ bit) for i in range(fsdp)])]
    pallas_call x0 -> x29, Pallas kernels: none -> 37.3 us  [call(): pl.pallas_call(wrapped, out_shape=outs, in_specs=list(specs) + [ANY] * ex...]
    dot_general x2 -> x0, matrix products: 33.8 us -> none  [the longest x1 18 us: half_step(): jnp.einsum('eic,eik->eck', left, right, preferred_element_type=jnp.float32)]
  transfers between devices with their start and end apart: 1 -> 60, of which waited for: 1 -> 35; matrix products, arithmetic and copies ran while one was open for 0% -> 0% of each run, Pallas kernels for 0% -> 6%
where the time goes in v3:
time: 247 us; the launch traced here: 243 us
  waiting for transfers between devices  153 us (62%)
  starting transfers between devices  49.1 us (20%)
  Pallas kernels  37.3 us (15%)
  local copies, waits for them, and re-layouts  2.7 us (1%)
    ppermute x48, waiting for transfers between devices, swap(): return lax.ppermute(value, 'fsdp', [(i, i ^ bit) for i in range(fsdp)])  79.5 us
    ppermute x6, waiting for transfers between devices, update(): value = lax.ppermute(value, 'loop', back)  51.1 us
    pallas_call x29, Pallas kernels, call(): pl.pallas_call(wrapped, out_shape=outs, in_specs=list(specs) + [ANY] * ex...  37.3 us
    ppermute x48, starting transfers between devices, swap(): return lax.ppermute(value, 'fsdp', [(i, i ^ bit) for i in range(fsdp)])  31.1 us
    ppermute x6, waiting for transfers between devices, pick(): lax.ppermute(picked[i], 'loop', list(enumerate(step)))  22.4 us
    ppermute x6, starting transfers between devices, update(): value = lax.ppermute(value, 'loop', back)  9.5 us
    ppermute x6, starting transfers between devices, pick(): lax.ppermute(picked[i], 'loop', list(enumerate(step)))  8.57 us
  transfers between devices with their start and end apart: 60, of which 35 were waited for; matrix products, arithmetic and copies ran while one was open for 0% of the time, Pallas kernels for 6%

profile of v3, /device:TPU:8, one launch (start us, length us, event | category | flops | bytes accessed | tf_op | source)
XLA Modules:
  0.0 242.7 jit_solution(456303439038117854)
XLA Ops:
  3.8 5.0 %collective-permute-start = (bf16[896,512]{1,0:T(8,128)(2,1)S(1)}, bf16[896,512]{1,0:T(8,128)(2,1)S(1)}, u32[]{:S(2)}, u32[]{:S(2)}) collective-permute-start(bf16[896,512]{1,0:T(8,128)(2,1)S(1)} %get-tuple-element.90.refs_2_), channel_id=1, source_target_pairs={{0,0},{1,2},{2,1},{3,3},{4,4},{5,6},{6,5},{7,7},{8,8},{9,10},{10,9... | collective-permute-start | bytes 2752520 | tf_op jit(solution)/shard_map/ppermute | solution.py:319
  8.8 17.0 %collective-permute-done.1.refs_4_.refs_2_ = bf16[896,512]{1,0:T(8,128)(2,1)S(1)} collective-permute-done((bf16[896,512]{1,0:T(8,128)(2,1)S(1)}, bf16[896,512]{1,0:T(8,128)(2,1)S(1)}, u32[]{:S(2)}, u32[]{:S(2)}) %collective-permute-start.1) | collective-permute-done | bytes 917536 | tf_op jit(solution)/shard_map/ppermute | solution.py:319
  29.8 3.5 %gram_part.4 = (f32[256,3072]{1,0:T(8,128)S(1)}, bf16[256,768]{1,0:T(8,128)(2,1)S(1)}, bf16[256,768]{1,0:T(8,128)(2,1)S(1)}, bf16[256,768]{1,0:T(8,128)(2,1)S(1)}, bf16[256,768]{1,0:T(8,128)(2,1)S(1)}) custom-call(bf16[896,512]{1,0:T(8,128)(2,1)S(1)} %get-tuple-element.89.refs_0_, bf16[896,512]{1,0:T(8,128)(2,1)S(1)} %collective-permute-done.refs_3_.refs_1_, ...), custom_call_target="tpu_custom_call" | custom-call | bytes 1 | tf_op jit(solution)/shard_map/gram_part/pallas_call | solution.py:73
  40.1 8.1 %collective-permute-done.7.refs_2_ = bf16[128,1536]{1,0:T(8,128)(2,1)S(1)} collective-permute-done((bf16[128,1536]{1,0:T(8,128)(2,1)S(1)}, bf16[128,1536]{1,0:T(8,128)(2,1)S(1)}, u32[]{:S(2)}, u32[]{:S(2)}) %collective-permute-start.7) | collective-permute-done | bytes 393248 | tf_op jit(solution)/shard_map/ppermute | solution.py:232
  61.9 4.2 %collective-permute-done.13.refs_2_ = bf16[64,1536]{1,0:T(8,128)(2,1)S(1)} collective-permute-done((bf16[64,1536]{1,0:T(8,128)(2,1)S(1)}, bf16[64,1536]{1,0:T(8,128)(2,1)S(1)}, u32[]{:S(2)}, u32[]{:S(2)}) %collective-permute-start.13) | collective-permute-done | bytes 196640 | tf_op jit(solution)/shard_map/ppermute | solution.py:232
  71.6 6.2 %collective-permute-done.15.refs_2_ = bf16[128,1024]{1,0:T(8,128)(2,1)S(1)} collective-permute-done((bf16[128,1024]{1,0:T(8,128)(2,1)S(1)}, bf16[128,1024]{1,0:T(8,128)(2,1)S(1)}, u32[]{:S(2)}, u32[]{:S(2)}) %collective-permute-start.15) | collective-permute-done | bytes 262176 | tf_op jit(solution)/shard_map/ppermute | solution.py:232
  79.9 3.5 %gram_part.6 = (f32[256,3072]{1,0:T(8,128)S(1)}, bf16[256,768]{1,0:T(8,128)(2,1)S(1)}, bf16[256,768]{1,0:T(8,128)(2,1)S(1)}, bf16[256,768]{1,0:T(8,128)(2,1)S(1)}, bf16[256,768]{1,0:T(8,128)(2,1)S(1)}) custom-call(bf16[896,512]{1,0:T(8,128)(2,1)S(1)} %get-tuple-element.120.refs_0_, bf16[896,512]{1,0:T(8,128)(2,1)S(1)} %collective-permute-done.19.refs_3_.refs_1_, ...), custom_call_target="tpu_custom_call" | custom-call | bytes 1 | tf_op jit(solution)/shard_map/gram_part/pallas_call | solution.py:73
  85.2 4.3 %collective-permute-done.17.refs_2_ = bf16[64,1024]{1,0:T(8,128)(2,1)S(1)} collective-permute-done((bf16[64,1024]{1,0:T(8,128)(2,1)S(1)}, bf16[64,1024]{1,0:T(8,128)(2,1)S(1)}, u32[]{:S(2)}, u32[]{:S(2)}) %collective-permute-start.17) | collective-permute-done | bytes 131104 | tf_op jit(solution)/shard_map/ppermute | solution.py:232
  93.7 7.0 %collective-permute-done.22.refs_3_ = bf16[64,2560]{1,0:T(8,128)(2,1)S(1)} collective-permute-done((bf16[64,2560]{1,0:T(8,128)(2,1)S(1)}, bf16[64,2560]{1,0:T(8,128)(2,1)S(1)}, u32[]{:S(2)}, u32[]{:S(2)}) %collective-permute-start.22) | collective-permute-done | bytes 327712 | tf_op jit(solution)/shard_map/ppermute | solution.py:232
  104.1 5.0 %collective-permute-done.30.refs_2_ = bf16[128,1536]{1,0:T(8,128)(2,1)S(1)} collective-permute-done((bf16[128,1536]{1,0:T(8,128)(2,1)S(1)}, bf16[128,1536]{1,0:T(8,128)(2,1)S(1)}, u32[]{:S(2)}, u32[]{:S(2)}) %collective-permute-start.30) | collective-permute-done | bytes 393248 | tf_op jit(solution)/shard_map/ppermute | solution.py:232
  109.1 15.8 %collective-permute-done.31.refs_3_ = bf16[128,1536]{1,0:T(8,128)(2,1)S(1)} collective-permute-done((bf16[128,1536]{1,0:T(8,128)(2,1)S(1)}, bf16[128,1536]{1,0:T(8,128)(2,1)S(1)}, u32[]{:S(2)}, u32[]{:S(2)}) %collective-permute-start.31) | collective-permute-done | bytes 393248 | tf_op jit(solution)/shard_map/ppermute | solution.py:232
  129.6 4.0 %collective-permute-done.38.refs_3_ = bf16[256,512]{1,0:T(8,128)(2,1)S(1)} collective-permute-done((bf16[256,512]{1,0:T(8,128)(2,1)S(1)}, bf16[256,512]{1,0:T(8,128)(2,1)S(1)}, u32[]{:S(2)}, u32[]{:S(2)}) %collective-permute-start.38) | collective-permute-done | bytes 262176 | tf_op jit(solution)/shard_map/ppermute | solution.py:232
  135.3 4.3 %update.4 = (bf16[896,512]{1,0:T(8,128)(2,1)S(1)}, bf16[896,512]{1,0:T(8,128)(2,1)S(1)}) custom-call(bf16[896,512]{1,0:T(8,128)(2,1)S(1)} %get-tuple-element.89.refs_0_, bf16[896,512]{1,0:T(8,128)(2,1)S(1)} %collective-permute-done.refs_3_.refs_1_, bf16[896,512]{1,0:T(8,128)(2,1)S(1)} %collective-permute-done.1.refs_4_.refs_2_, ...), custom_call_target="tpu_custom_call" | custom-call | bytes 1 | tf_op jit(solution)/shard_map/update/pallas_call | solution.py:73
  143.9 4.3 %update.5 = (bf16[896,512]{1,0:T(8,128)(2,1)S(1)}, bf16[896,512]{1,0:T(8,128)(2,1)S(1)}) custom-call(bf16[896,512]{1,0:T(8,128)(2,1)S(1)} %get-tuple-element.89.refs_0_, bf16[896,512]{1,0:T(8,128)(2,1)S(1)} %collective-permute-done.refs_3_.refs_1_, bf16[896,512]{1,0:T(8,128)(2,1)S(1)} %collective-permute-done.1.refs_4_.refs_2_, ...), custom_call_target="tpu_custom_call" | custom-call | bytes 1 | tf_op jit(solution)/shard_map/update/pallas_call | solution.py:73
  148.2 5.3 %collective-permute-done.45.refs_2_ = bf16[64,1536]{1,0:T(8,128)(2,1)S(1)} collective-permute-done((bf16[64,1536]{1,0:T(8,128)(2,1)S(1)}, bf16[64,1536]{1,0:T(8,128)(2,1)S(1)}, u32[]{:S(2)}, u32[]{:S(2)}) %collective-permute-start.45) | collective-permute-done | bytes 196640 | tf_op jit(solution)/shard_map/ppermute | solution.py:232
  163.2 4.6 %collective-permute-done.49.refs_2_ = bf16[64,2560]{1,0:T(8,128)(2,1)S(1)} collective-permute-done((bf16[64,2560]{1,0:T(8,128)(2,1)S(1)}, bf16[64,2560]{1,0:T(8,128)(2,1)S(1)}, u32[]{:S(2)}, u32[]{:S(2)}) %collective-permute-start.49) | collective-permute-done | bytes 327712 | tf_op jit(solution)/shard_map/ppermute | solution.py:232
  170.9 3.6 %collective-permute-start.40 = (bf16[896,512]{1,0:T(8,128)(2,1)S(1)}, bf16[896,512]{1,0:T(8,128)(2,1)S(1)}, u32[]{:S(2)}, u32[]{:S(2)}) collective-permute-start(bf16[896,512]{1,0:T(8,128)(2,1)S(1)} %get-tuple-element.147), channel_id=1, source_target_pairs={{0,0},{2,1},{1,2},{3,3},{4,4},{6,5},{5,6},{7,7},{8,8},{10,9},{9,10... | collective-permute-start | bytes 2752520 | tf_op jit(solution)/shard_map/ppermute | solution.py:374
  174.4 7.3 %collective-permute-done.41.refs_5_.refs_2_ = bf16[896,512]{1,0:T(8,128)(2,1)S(1)} collective-permute-done((bf16[896,512]{1,0:T(8,128)(2,1)S(1)}, bf16[896,512]{1,0:T(8,128)(2,1)S(1)}, u32[]{:S(2)}, u32[]{:S(2)}) %collective-permute-start.41) | collective-permute-done | bytes 917536 | tf_op jit(solution)/shard_map/ppermute | solution.py:374
  183.3 7.2 %collective-permute-done.40.refs_13_.refs_1_ = bf16[896,512]{1,0:T(8,128)(2,1)S(1)} collective-permute-done((bf16[896,512]{1,0:T(8,128)(2,1)S(1)}, bf16[896,512]{1,0:T(8,128)(2,1)S(1)}, u32[]{:S(2)}, u32[]{:S(2)}) %collective-permute-start.40) | collective-permute-done | bytes 917536 | tf_op jit(solution)/shard_map/ppermute | solution.py:374
  190.5 4.2 %update.6 = (bf16[896,512]{1,0:T(8,128)(2,1)S(1)}, bf16[896,512]{1,0:T(8,128)(2,1)S(1)}) custom-call(bf16[896,512]{1,0:T(8,128)(2,1)S(1)} %get-tuple-element.120.refs_0_, bf16[896,512]{1,0:T(8,128)(2,1)S(1)} %collective-permute-done.19.refs_3_.refs_1_, bf16[896,512]{1,0:T(8,128)(2,1)S(1)} %collective-permute-done.20.refs_4_.refs_2_, ...), custom_call_target="tpu_custom_call" | custom-call | bytes 1 | tf_op jit(solution)/shard_map/update/pallas_call | solution.py:73
  194.8 4.3 %update.7 = (bf16[896,512]{1,0:T(8,128)(2,1)S(1)}, bf16[896,512]{1,0:T(8,128)(2,1)S(1)}) custom-call(bf16[896,512]{1,0:T(8,128)(2,1)S(1)} %get-tuple-element.120.refs_0_, bf16[896,512]{1,0:T(8,128)(2,1)S(1)} %collective-permute-done.19.refs_3_.refs_1_, bf16[896,512]{1,0:T(8,128)(2,1)S(1)} %collective-permute-done.20.refs_4_.refs_2_, ...), custom_call_target="tpu_custom_call" | custom-call | bytes 1 | tf_op jit(solution)/shard_map/update/pallas_call | solution.py:73
  199.1 3.6 %collective-permute-start.57 = (bf16[896,512]{1,0:T(8,128)(2,1)S(1)}, bf16[896,512]{1,0:T(8,128)(2,1)S(1)}, u32[]{:S(2)}, u32[]{:S(2)}) collective-permute-start(bf16[896,512]{1,0:T(8,128)(2,1)S(1)} %get-tuple-element.171), channel_id=1, source_target_pairs={{0,0},{2,1},{1,2},{3,3},{4,4},{6,5},{5,6},{7,7},{8,8},{10,9},{9,10... | collective-permute-start | bytes 2752520 | tf_op jit(solution)/shard_map/ppermute | solution.py:374
  203.1 19.3 %collective-permute-done.58.refs_6_ = bf16[896,512]{1,0:T(8,128)(2,1)S(1)} collective-permute-done((bf16[896,512]{1,0:T(8,128)(2,1)S(1)}, bf16[896,512]{1,0:T(8,128)(2,1)S(1)}, u32[]{:S(2)}, u32[]{:S(2)}) %collective-permute-start.58) | collective-permute-done | bytes 917536 | tf_op jit(solution)/shard_map/ppermute | solution.py:374
  224.3 15.4 %collective-permute-done.59.refs_7_ = bf16[896,512]{1,0:T(8,128)(2,1)S(1)} collective-permute-done((bf16[896,512]{1,0:T(8,128)(2,1)S(1)}, bf16[896,512]{1,0:T(8,128)(2,1)S(1)}, u32[]{:S(2)}, u32[]{:S(2)}) %collective-permute-start.59) | collective-permute-done | bytes 917536 | tf_op jit(solution)/shard_map/ppermute | solution.py:374
  (133 shorter events, 75.1 us)
Async XLA Ops:
  3.7 22.2 %collective-permute-start.1 = (bf16[896,512]{1,0:T(8,128)(2,1)S(1)}, bf16[896,512]{1,0:T(8,128)(2,1)S(1)}, u32[]{:S(2)}, u32[]{:S(2)}) collective-permute-start(bf16[896,512]{1,0:T(8,128)(2,1)S(1)} %get-tuple-element.90.refs_2_), channel_id=1, source_target_pairs={{0,1},{1,0},{2,3},{3,2},{4,5},{5,4},{6,7},{7,6},{8,9},{9,8},{10,11... | collective-permute-start | bytes 2752520 | tf_op jit(solution)/shard_map/ppermute | solution.py:319
  3.8 25.1 %collective-permute-start = (bf16[896,512]{1,0:T(8,128)(2,1)S(1)}, bf16[896,512]{1,0:T(8,128)(2,1)S(1)}, u32[]{:S(2)}, u32[]{:S(2)}) collective-permute-start(bf16[896,512]{1,0:T(8,128)(2,1)S(1)} %get-tuple-element.90.refs_2_), channel_id=1, source_target_pairs={{0,0},{1,2},{2,1},{3,3},{4,4},{5,6},{6,5},{7,7},{8,8},{9,10},{10,9... | collective-permute-start | bytes 2752520 | tf_op jit(solution)/shard_map/ppermute | solution.py:319
  29.7 22.2 %collective-permute-start.2 = (bf16[896,512]{1,0:T(8,128)(2,1)S(1)}, bf16[896,512]{1,0:T(8,128)(2,1)S(1)}, u32[]{:S(2)}, u32[]{:S(2)}) collective-permute-start(bf16[896,512]{1,0:T(8,128)(2,1)S(1)} %pick.5.refs_3_), channel_id=1, source_target_pairs={{0,2},{1,0},{2,3},{3,1},{4,6},{5,4},{6,7},{7,5},{8,10},{9,8},{10,1... | collective-permute-start | bytes 2752520 | tf_op jit(solution)/shard_map/ppermute | solution.py:319
  37.0 11.2 %collective-permute-start.7 = (bf16[128,1536]{1,0:T(8,128)(2,1)S(1)}, bf16[128,1536]{1,0:T(8,128)(2,1)S(1)}, u32[]{:S(2)}, u32[]{:S(2)}) collective-permute-start(bf16[128,1536]{1,0:T(8,128)(2,1)S(1)} %get-tuple-element.98), channel_id=1, source_target_pairs={{0,8},{4,12},{8,0},{12,4},{16,24},{20,28},{24,16},{28,20},{1,9},{5... | collective-permute-start | bytes 1179656 | tf_op jit(solution)/shard_map/ppermute | solution.py:232
  38.5 10.9 %collective-permute-start.8 = (bf16[128,1536]{1,0:T(8,128)(2,1)S(1)}, bf16[128,1536]{1,0:T(8,128)(2,1)S(1)}, u32[]{:S(2)}, u32[]{:S(2)}) collective-permute-start(bf16[128,1536]{1,0:T(8,128)(2,1)S(1)} %get-tuple-element.99), channel_id=1, source_target_pairs={{0,16},{4,20},{8,24},{12,28},{16,0},{20,4},{24,8},{28,12},{1,17},{... | collective-permute-start | bytes 1179656 | tf_op jit(solution)/shard_map/ppermute | solution.py:232
  52.9 26.2 %collective-permute-start.20 = (bf16[896,512]{1,0:T(8,128)(2,1)S(1)}, bf16[896,512]{1,0:T(8,128)(2,1)S(1)}, u32[]{:S(2)}, u32[]{:S(2)}) collective-permute-start(bf16[896,512]{1,0:T(8,128)(2,1)S(1)} %get-tuple-element.101.refs_4_), channel_id=1, source_target_pairs={{0,1},{1,0},{2,3},{3,2},{4,5},{5,4},{6,7},{7,6},{8,9},{9,8},{10,11... | collective-permute-start | bytes 2752520 | tf_op jit(solution)/shard_map/ppermute | solution.py:319
  53.8 25.3 %collective-permute-start.19 = (bf16[896,512]{1,0:T(8,128)(2,1)S(1)}, bf16[896,512]{1,0:T(8,128)(2,1)S(1)}, u32[]{:S(2)}, u32[]{:S(2)}) collective-permute-start(bf16[896,512]{1,0:T(8,128)(2,1)S(1)} %get-tuple-element.101.refs_4_), channel_id=1, source_target_pairs={{0,0},{1,2},{2,1},{3,3},{4,4},{5,6},{6,5},{7,7},{8,8},{9,10},{10,9... | collective-permute-start | bytes 2752520 | tf_op jit(solution)/shard_map/ppermute | solution.py:319
  85.2 39.9 %collective-permute-start.29 = (bf16[896,512]{1,0:T(8,128)(2,1)S(1)}, bf16[896,512]{1,0:T(8,128)(2,1)S(1)}, u32[]{:S(2)}, u32[]{:S(2)}) collective-permute-start(bf16[896,512]{1,0:T(8,128)(2,1)S(1)} %pick.7.refs_3_), channel_id=1, source_target_pairs={{0,2},{1,0},{2,3},{3,1},{4,6},{5,4},{6,7},{7,5},{8,10},{9,8},{10,1... | collective-permute-start | bytes 2752520 | tf_op jit(solution)/shard_map/ppermute | solution.py:319
  90.1 10.6 %collective-permute-start.22 = (bf16[64,2560]{1,0:T(8,128)(2,1)S(1)}, bf16[64,2560]{1,0:T(8,128)(2,1)S(1)}, u32[]{:S(2)}, u32[]{:S(2)}) collective-permute-start(bf16[64,2560]{1,0:T(8,128)(2,1)S(1)} %get-tuple-element.123.refs_1_), channel_id=1, source_target_pairs={{0,8},{4,12},{8,0},{12,4},{16,24},{20,28},{24,16},{28,20},{1,9},{5... | collective-permute-start | bytes 983048 | tf_op jit(solution)/shard_map/ppermute | solution.py:232
  92.2 16.9 %collective-permute-start.30 = (bf16[128,1536]{1,0:T(8,128)(2,1)S(1)}, bf16[128,1536]{1,0:T(8,128)(2,1)S(1)}, u32[]{:S(2)}, u32[]{:S(2)}) collective-permute-start(bf16[128,1536]{1,0:T(8,128)(2,1)S(1)} %get-tuple-element.132), channel_id=1, source_target_pairs={{0,8},{4,12},{8,0},{12,4},{16,24},{20,28},{24,16},{28,20},{1,9},{5... | collective-permute-start | bytes 1179656 | tf_op jit(solution)/shard_map/ppermute | solution.py:232
  100.8 27.2 %collective-permute-start.28 = (bf16[128,2560]{1,0:T(8,128)(2,1)S(1)}, bf16[128,2560]{1,0:T(8,128)(2,1)S(1)}, u32[]{:S(2)}, u32[]{:S(2)}) collective-permute-start(bf16[128,2560]{1,0:T(8,128)(2,1)S(1)} %get-tuple-element.130.refs_1_), channel_id=1, source_target_pairs={{0,16},{4,20},{8,24},{12,28},{16,0},{20,4},{24,8},{28,12},{1,17},{... | collective-permute-start | bytes 1966088 | tf_op jit(solution)/shard_map/ppermute | solution.py:232
  102.1 26.0 %collective-permute-start.27 = (bf16[128,2560]{1,0:T(8,128)(2,1)S(1)}, bf16[128,2560]{1,0:T(8,128)(2,1)S(1)}, u32[]{:S(2)}, u32[]{:S(2)}) collective-permute-start(bf16[128,2560]{1,0:T(8,128)(2,1)S(1)} %get-tuple-element.129.refs_4_.refs_0_), channel_id=1, source_target_pairs={{0,8},{4,12},{8,0},{12,4},{16,24},{20,28},{24,16},{28,20},{1,9},{5... | collective-permute-start | bytes 1966088 | tf_op jit(solution)/shard_map/ppermute | solution.py:232
  103.4 21.5 %collective-permute-start.31 = (bf16[128,1536]{1,0:T(8,128)(2,1)S(1)}, bf16[128,1536]{1,0:T(8,128)(2,1)S(1)}, u32[]{:S(2)}, u32[]{:S(2)}) collective-permute-start(bf16[128,1536]{1,0:T(8,128)(2,1)S(1)} %get-tuple-element.133), channel_id=1, source_target_pairs={{0,16},{4,20},{8,24},{12,28},{16,0},{20,4},{24,8},{28,12},{1,17},{... | collective-permute-start | bytes 1179656 | tf_op jit(solution)/shard_map/ppermute | solution.py:232
  139.6 29.0 %collective-permute-start.42 = (bf16[896,512]{1,0:T(8,128)(2,1)S(1)}, bf16[896,512]{1,0:T(8,128)(2,1)S(1)}, u32[]{:S(2)}, u32[]{:S(2)}) collective-permute-start(bf16[896,512]{1,0:T(8,128)(2,1)S(1)} %get-tuple-element.145.refs_12_), channel_id=1, source_target_pairs={{2,0},{0,1},{3,2},{1,3},{6,4},{4,5},{7,6},{5,7},{10,8},{8,9},{11,1... | collective-permute-start | bytes 2752520 | tf_op jit(solution)/shard_map/ppermute | solution.py:374
  139.9 13.7 %collective-permute-start.43 = (bf16[128,1024]{1,0:T(8,128)(2,1)S(1)}, bf16[128,1024]{1,0:T(8,128)(2,1)S(1)}, u32[]{:S(2)}, u32[]{:S(2)}) collective-permute-start(bf16[128,1024]{1,0:T(8,128)(2,1)S(1)} %get-tuple-element.150), channel_id=1, source_target_pairs={{0,8},{4,12},{8,0},{12,4},{16,24},{20,28},{24,16},{28,20},{1,9},{5... | collective-permute-start | bytes 786440 | tf_op jit(solution)/shard_map/ppermute | solution.py:232
  141.3 12.3 %collective-permute-start.44 = (bf16[128,1024]{1,0:T(8,128)(2,1)S(1)}, bf16[128,1024]{1,0:T(8,128)(2,1)S(1)}, u32[]{:S(2)}, u32[]{:S(2)}) collective-permute-start(bf16[128,1024]{1,0:T(8,128)(2,1)S(1)} %get-tuple-element.151), channel_id=1, source_target_pairs={{0,16},{4,20},{8,24},{12,28},{16,0},{20,4},{24,8},{28,12},{1,17},{... | collective-permute-start | bytes 786440 | tf_op jit(solution)/shard_map/ppermute | solution.py:232
  142.8 10.7 %collective-permute-start.45 = (bf16[64,1536]{1,0:T(8,128)(2,1)S(1)}, bf16[64,1536]{1,0:T(8,128)(2,1)S(1)}, u32[]{:S(2)}, u32[]{:S(2)}) collective-permute-start(bf16[64,1536]{1,0:T(8,128)(2,1)S(1)} %get-tuple-element.153), channel_id=1, source_target_pairs={{0,16},{4,20},{8,24},{12,28},{16,0},{20,4},{24,8},{28,12},{1,17},{... | collective-permute-start | bytes 589832 | tf_op jit(solution)/shard_map/ppermute | solution.py:232
  161.5 20.3 %collective-permute-start.41 = (bf16[896,512]{1,0:T(8,128)(2,1)S(1)}, bf16[896,512]{1,0:T(8,128)(2,1)S(1)}, u32[]{:S(2)}, u32[]{:S(2)}) collective-permute-start(bf16[896,512]{1,0:T(8,128)(2,1)S(1)} %get-tuple-element.148.refs_4_), channel_id=1, source_target_pairs={{1,0},{0,1},{3,2},{2,3},{5,4},{4,5},{7,6},{6,7},{9,8},{8,9},{11,10... | collective-permute-start | bytes 2752520 | tf_op jit(solution)/shard_map/ppermute | solution.py:374
  168.7 13.4 %collective-permute-start.51 = (bf16[128,2560]{1,0:T(8,128)(2,1)S(1)}, bf16[128,2560]{1,0:T(8,128)(2,1)S(1)}, u32[]{:S(2)}, u32[]{:S(2)}) collective-permute-start(bf16[128,2560]{1,0:T(8,128)(2,1)S(1)} %get-tuple-element.163.refs_0_.refs_4_), channel_id=1, source_target_pairs={{0,8},{4,12},{8,0},{12,4},{16,24},{20,28},{24,16},{28,20},{1,9},{5... | collective-permute-start | bytes 1966088 | tf_op jit(solution)/shard_map/ppermute | solution.py:232
  169.3 12.7 %collective-permute-start.52 = (bf16[128,2560]{1,0:T(8,128)(2,1)S(1)}, bf16[128,2560]{1,0:T(8,128)(2,1)S(1)}, u32[]{:S(2)}, u32[]{:S(2)}) collective-permute-start(bf16[128,2560]{1,0:T(8,128)(2,1)S(1)} %get-tuple-element.164.refs_1_), channel_id=1, source_target_pairs={{0,16},{4,20},{8,24},{12,28},{16,0},{20,4},{24,8},{28,12},{1,17},{... | collective-permute-start | bytes 1966088 | tf_op jit(solution)/shard_map/ppermute | solution.py:232
  170.9 19.6 %collective-permute-start.40 = (bf16[896,512]{1,0:T(8,128)(2,1)S(1)}, bf16[896,512]{1,0:T(8,128)(2,1)S(1)}, u32[]{:S(2)}, u32[]{:S(2)}) collective-permute-start(bf16[896,512]{1,0:T(8,128)(2,1)S(1)} %get-tuple-element.147), channel_id=1, source_target_pairs={{0,0},{2,1},{1,2},{3,3},{4,4},{6,5},{5,6},{7,7},{8,8},{10,9},{9,10... | collective-permute-start | bytes 2752520 | tf_op jit(solution)/shard_map/ppermute | solution.py:374
  199.1 23.4 %collective-permute-start.58 = (bf16[896,512]{1,0:T(8,128)(2,1)S(1)}, bf16[896,512]{1,0:T(8,128)(2,1)S(1)}, u32[]{:S(2)}, u32[]{:S(2)}) collective-permute-start(bf16[896,512]{1,0:T(8,128)(2,1)S(1)} %get-tuple-element.172.refs_8_), channel_id=1, source_target_pairs={{1,0},{0,1},{3,2},{2,3},{5,4},{4,5},{7,6},{6,7},{9,8},{8,9},{11,10... | collective-permute-start | bytes 2752520 | tf_op jit(solution)/shard_map/ppermute | solution.py:374
  199.1 25.2 %collective-permute-start.57 = (bf16[896,512]{1,0:T(8,128)(2,1)S(1)}, bf16[896,512]{1,0:T(8,128)(2,1)S(1)}, u32[]{:S(2)}, u32[]{:S(2)}) collective-permute-start(bf16[896,512]{1,0:T(8,128)(2,1)S(1)} %get-tuple-element.171), channel_id=1, source_target_pairs={{0,0},{2,1},{1,2},{3,3},{4,4},{6,5},{5,6},{7,7},{8,8},{10,9},{9,10... | collective-permute-start | bytes 2752520 | tf_op jit(solution)/shard_map/ppermute | solution.py:374
  202.8 36.9 %collective-permute-start.59 = (bf16[896,512]{1,0:T(8,128)(2,1)S(1)}, bf16[896,512]{1,0:T(8,128)(2,1)S(1)}, u32[]{:S(2)}, u32[]{:S(2)}) collective-permute-start(bf16[896,512]{1,0:T(8,128)(2,1)S(1)} %get-tuple-element.169.refs_12_), channel_id=1, source_target_pairs={{2,0},{0,1},{3,2},{1,3},{6,4},{4,5},{7,6},{5,7},{10,8},{8,9},{11,1... | collective-permute-start | bytes 2752520 | tf_op jit(solution)/shard_map/ppermute | solution.py:374
  (40 other events, 228.6 us)

commit v4 on v3

--- a/solution.py
+++ b/solution.py
@@ -1,3 +1,5 @@
+import functools
+
 import jax
 import jax.numpy as jnp
 from jax import lax
@@ -10,6 +12,8 @@
 coef_linear = 3.4445
 coef_cubic = -4.775
 
+CHUNKS = 4, 2
+
 MIB = 2**20
 F32, BF16 = jnp.float32, jnp.bfloat16
 ANY = pl.BlockSpec(memory_space=pl.ANY)
@@ -20,18 +24,22 @@
 def plan(loop, fsdp):
     levels = fsdp.bit_length() - 2
     if loop == 4 and levels == 2:
-        phases = [[[0, 2, 1, 3], [1, 0, 3, 2]], [[2, 0, 3, 1]]]
-        order = """
-            0pick0 0pick1 0gram0 0split0 0add00 1pick0 0gram1 0add01 0split1 0add10 1pick1 1gram0 0add11
-            1split0 0join0 1add00 1gram1 0join1 1split1 0update31 0update20
-            1add01 1add10 1add11 0need3 1join0 0need2 1join1 0need1 1update31 1update20
-        """
-        turns = [(int(t[0]), t[1:].rstrip("0123456789"), [int(c) for c in t[1:] if c.isdigit()]) for t in order.split()]
-        return [({1: 1, 2: 2}, phases), ({1: 0, 2: 3}, phases)], turns
+        phases = [[[1, 0, 3, 2], [0, 2, 1, 3]], [[2, 0, 3, 1]], [[1, 3, 0, 2]], [[3, 1, 2, 0]]]
+        waves = [({0: 0, 3: 3}, [[0], [3], [4]], [[0], [1, 2]]), ({1: 1, 2: 2}, [[0, 1], [2]], [[0, 1]])]
+        order = [
+            "0send0", "0send1", "1gram0", "1split0", "0gram0", "1add00", "0send2", "1gram1", "1add01", "1split1",
+            "0split0", "1add10", "0add00", "0send3", "1add11", "0add01", "0gram1", "1join00", "0split1", "0join00",
+            "0gram2", "1join01", "0add10", "0join01", "0split2", "1update32", "0add11", "0add20", "1update10",
+            "0add21", "0join10", "1need3", "0join11", "0update12", "0update30", "1place203", "0place120", "1place1",
+            "0place3",
+        ]
+        turns = [(int(t[0]), t[1:].rstrip("0123456789"), [int(c) for c in t[1:] if c.isdigit()]) for t in order]
+        return phases, waves, {(0, 2): (1, 1)}, turns
     rounds = [[(p + step) % loop for p in range(loop)] for step in range(1, loop)]
-    turns = [(0, "pick", [0]), (0, "gram", [0]), (0, "split", [0])]
-    turns += [(0, "add", [0, i]) for i in range(levels)] + [(0, "join", [i]) for i in range(levels)]
-    return [({p: p for p in range(loop)}, [rounds])], turns + [(0, "update", list(range(loop)))]
+    turns = [(0, "send", [0]), (0, "gram", [0]), (0, "split", [0])]
+    turns += [(0, step, [0, i]) for step in ("add", "join") for i in range(levels)]
+    turns += [(0, "update", list(range(loop))), (0, "place", list(range(loop)))]
+    return [rounds], [({p: p for p in range(loop)}, [list(range(len(rounds)))], [[0]])], {}, turns
 
 
 def sends(owners, step):
@@ -94,6 +102,11 @@
     return lax.rem(lax.div(lax.axis_index("fsdp"), bit), 2)
 
 
+def is_one_of(places):
+    here = lax.axis_index("loop")
+    return functools.reduce(jnp.logical_or, [here == place for place in places])
+
+
 def rows_at(part, height):
     return pl.ds(pl.multiple_of(part * height, height), height)
 
@@ -114,7 +127,7 @@
     return call(kernel, "pick", [expert_order, iterate], [SMEM, ANY], outs, 8, sems, after=after)
 
 
-def gram_part(blocks, pairs, chunks, after):
+def gram_part(blocks, pairs, chunks, owners, after):
     rows, width = blocks[0].shape
     half, count = width // 2, len(blocks)
     total = len(pairs) * width
@@ -123,6 +136,9 @@
     def kernel(*refs):
         xs, keep, sent, left = refs[:count], refs[count], refs[count + 1 : -1], refs[-1]
         side = side_of(1)
+        pl.when(is_one_of(owners))(lambda: multiply(xs, keep, sent, left, side))
+
+    def multiply(xs, keep, sent, left, side):
         for sending, part in ((True, 1 - side), (False, side)):
             for a in sorted({a for a, _ in pairs}):
                 left[a * half : (a + 1) * half, :] = xs[a][:, rows_at(part, half)].T
@@ -228,35 +244,48 @@
     return call(kernel, "join", [*values, *received], [VMEM] * (2 * count), outs, 8, after=after)
 
 
-def swap(value, bit, fsdp):
-    return lax.ppermute(value, "fsdp", [(i, i ^ bit) for i in range(fsdp)])
-
-
-def update_blocks(blocks, places, own, other, wanted, after):
+def swap(value, bit, fsdp, loop, places):
+    pairs = [(i * loop + p, (i ^ (bit if p in places else 1)) * loop + p) for i in range(fsdp) for p in range(loop)]
+    return lax.ppermute(value, ("fsdp", "loop"), pairs)
+
+
+def shift(value, step, fsdp):
+    loop = len(step)
+    pairs = [(i * loop + p, (i ^ (to == p)) * loop + to) for i in range(fsdp) for p, to in enumerate(step)]
+    return lax.ppermute(value, ("fsdp", "loop"), pairs)
+
+
+def update_blocks(blocks, places, own, other, wanted, instead, owners, after):
     rows, width = blocks[0].shape
     half, count = width // 2, len(blocks)
-    total, chunks, piece = count * width, len(own), own[0].shape[1]
+    total, chunks = count * width, len(own)
     factor = 0.2 * D**0.5
 
     def kernel(*refs):
         xs, strips = refs[:count], (refs[count : count + chunks], refs[count + chunks : count + 2 * chunks])
         refs = refs[count + 2 * chunks :]
+        given, refs = refs[: len(instead)], refs[len(instead) :]
         outs, (x, g) = refs[: len(wanted)], refs[len(wanted) :]
+        mine = is_one_of(owners)
+        pl.when(mine)(lambda: multiply(xs, strips, outs, x, g))
+        for b, value in zip(instead, given):
+
+            @pl.when(jnp.logical_not(mine))
+            def _(out=outs[wanted.index(b)], value=value):
+                out[...] = value[...]
+
+    def multiply(xs, strips, outs, x, g):
         side = side_of(1)
         for a in range(count):
             x[:, a * width : (a + 1) * width] = xs[a][...]
         for part, strip in zip((side, 1 - side), strips):
-            for (a, b), column in places.items():
+            for (a, b), pieces in places.items():
                 if a not in wanted and b not in wanted:
                     continue
                 where = pl.ds(pl.multiple_of(a * width + part * half, half), half)
-                done = 0
-                while done < width:
-                    chunk, offset = divmod(column + done, piece)
-                    size = min(piece - offset, width - done)
-                    at = b * width + done
+                for chunk, offset, first, size in pieces:
+                    at = b * width + first
                     g[where, at : at + size] = strip[chunk][:, offset : offset + size]
-                    done += size
         for out, b in zip(outs, wanted):
             low, high = b * width, (b + 1) * width
             product = jnp.dot(x[:, :high], g[:high, low:high], preferred_element_type=F32)
@@ -268,128 +297,169 @@
 
     scratch = [pltpu.VMEM((rows, total), BF16), pltpu.VMEM((total, total), BF16)]
     outs = [struct((rows, width), BF16)] * len(wanted)
-    ins = [*blocks, *own, *other]
+    ins = [*blocks, *own, *other, *instead.values()]
     return call(kernel, "update", ins, [VMEM] * len(ins), outs, 30, scratch, after)
 
 
-def place_slots(candidates, slots, like, after):
-    flat = [value for wave in candidates for value in wave]
+def place_slots(out, found, like, after):
+    old = [] if out is None else [out]
+    ins = [value for value, _ in found]
+    cases = [(i, place, slot) for i, (_, table) in enumerate(found) for place, slot in table.items()]
 
     def kernel(*refs):
-        ins, out, sems = refs[: len(flat)], refs[-2], refs[-1]
-        place = lax.axis_index("loop")
-        base = 0
-        for wave, tables in enumerate(slots):
-            for index, table in enumerate(tables):
-                for key, slot in table.items():
-
-                    @pl.when(place == key)
-                    def _(source=ins[base + index], slot=slot):
-                        pltpu.make_async_copy(source, out.at[slot], sems.at[slot]).start()
-
-            base += len(tables)
-        for slot in range(like.shape[0]):
-            pltpu.make_async_copy(ins[0], out.at[slot], sems.at[slot]).wait()
-
-    sems = [pltpu.SemaphoreType.DMA((like.shape[0],))]
-    outs = [struct(like.shape, like.dtype)]
-    return call(kernel, "place_slots", flat, [ANY] * len(flat), outs, 8, sems, after=after)[0]
+        values, target, sems = refs[: len(ins)], refs[-2], refs[-1]
+        here = lax.axis_index("loop")
+        for wait in (False, True):
+            for i, place, slot in cases:
+
+                @pl.when(here == place)
+                def _(i=i, slot=slot):
+                    copy = pltpu.make_async_copy(values[i], target.at[slot], sems.at[i])
+                    copy.wait() if wait else copy.start()
+
+    return pl.pallas_call(
+        kernel,
+        out_shape=struct(like.shape, like.dtype),
+        in_specs=[VMEM] * len(ins) + [ANY] * (len(old) + len(after)),
+        out_specs=ANY,
+        scratch_shapes=[pltpu.SemaphoreType.DMA((len(ins),))],
+        input_output_aliases={len(ins): 0} if old else {},
+        compiler_params=pltpu.CompilerParams(vmem_limit_bytes=8 * MIB),
+        cost_estimate=pl.CostEstimate(flops=0, bytes_accessed=1, transcendentals=0),
+        name="place_slots",
+    )(*ins, *old, *after)
+
+
+class Columns:
+    def __init__(self, iterate, expert_order, phases, fsdp):
+        self.iterate, self.expert_order, self.phases, self.fsdp = iterate, expert_order, phases, fsdp
+        self.rounds = [step for rounds in phases for step in rounds]
+        self.own, self.arrived, self.last, self.out = None, [], [], None
+
+    def send(self, phase):
+        rounds = self.phases[phase]
+        tables = [{p: to for p, to in enumerate(step) if p != to} for step in rounds]
+        places = {p: p for p in range(len(rounds[0]))}
+        merged, index = merge(tables if phase else tables + [places])
+        before = self.arrived[len(self.arrived) - len(self.phases[phase - 1]) :] if phase else []
+        picked = pick(self.iterate, self.expert_order, merged, self.last + before)
+        if not phase:
+            self.own = picked[index[-1]]
+        self.arrived += [shift(picked[i], step, self.fsdp) for i, step in zip(index, rounds)]
+        self.last = picked[:1]
 
 
 class Wave:
-    def __init__(self, iterate, expert_order, owners, phases, fsdp, chunks, shared):
-        self.iterate, self.expert_order, self.owners, self.phases = iterate, expert_order, owners, phases
-        self.fsdp, self.chunks, self.shared = fsdp, chunks, shared
-        self.bits = [1 << i for i in range(1, fsdp.bit_length() - 1)]
+    def __init__(self, columns, owners, groups, gathers, shares, loop, chunks):
+        self.columns, self.owners, self.loop, self.chunks = columns, owners, loop, chunks
+        self.fsdp = columns.fsdp
+        self.bits = [1 << i for i in range(1, self.fsdp.bit_length() - 1)]
         self.orders = [self.bits, self.bits[::-1]]
-        self.blocks, self.groups, self.state, self.gathered = [], [], {}, None
-        self.rounds = [step for rounds in phases for step in rounds]
-        self.updates = {}
+        self.rounds = [number for group in groups for number in group]
+        self.groups, self.gathers, self.state, self.gathered, first = [], gathers, {}, {}, 0
+        for group in groups:
+            count = first + len(group) + 1
+            self.groups.append([(a, b) for b in range(first + 1 if first else 0, count) for a in range(b + 1)])
+            first += len(group)
+        self.updates, self.shares = {}, shares
+
+    def blocks(self, count):
+        return [self.columns.own] + [self.columns.arrived[number] for number in self.rounds[: count - 1]]
 
     def move(self, values, bits):
-        return [swap(value, bit, self.fsdp) for value, bit in zip(values, bits)]
-
-    def pick(self, phase):
-        rounds, first = self.phases[phase], len(self.blocks)
-        tables = [sends(self.owners, step) for step in rounds]
-        merged, index = merge(tables if phase else tables + [self.owners])
-        picked = pick(self.iterate, self.expert_order, merged, self.shared["last"] + self.shared["arrived"])
-        if not phase:
-            self.blocks.append(picked[index[-1]])
-        arrived = [lax.ppermute(picked[i], "loop", list(enumerate(step))) for i, step in zip(index, rounds)]
-        self.blocks.extend(arrived)
-        count = len(self.blocks)
-        self.groups.append([(a, b) for b in range(first, count) for a in range(b + 1)])
-        self.shared["last"], self.shared["arrived"] = picked[:1], arrived
+        return [swap(value, bit, self.fsdp, self.loop, self.owners) for value, bit in zip(values, bits)]
 
     def gram(self, group):
         pairs = self.groups[group]
-        blocks = self.blocks[: 1 + max(b for _, b in pairs)]
-        keep, out = gram_part(blocks, pairs, self.chunks, self.shared["last"])
-        self.shared["last"] = [keep]
-        self.state[group] = keep, self.move(out, [1] * self.chunks)
+        blocks = self.blocks(1 + max(b for _, b in pairs))
+        keep, out = gram_part(blocks, pairs, self.chunks[0], self.owners, self.columns.last)
+        self.columns.last = [keep]
+        self.state[group] = keep, self.move(out, [1] * self.chunks[0])
 
     def split(self, group):
         keep, received = self.state[group]
         firsts = [order[0] for order in self.orders]
-        keeps, out = first_split(keep, received, firsts, self.shared["last"])
-        self.shared["last"] = keeps[:1]
+        keeps, out = first_split(keep, received, firsts, self.columns.last)
+        self.columns.last = keeps[:1]
         self.state[group] = keeps, self.move(out, firsts)
 
     def add(self, group, level):
         keeps, received = self.state[group]
         bits = [order[level + 1] for order in self.orders if level + 1 < len(order)]
-        last = not bits and group == len(self.phases) - 1
-        earlier = [self.state[g] for g in range(group)] if last else []
-        keeps, out = add_split(keeps, received, earlier, bits, self.shared["last"])
-        self.shared["last"] = keeps[:1]
+        last = [] if bits else [i for i, groups in enumerate(self.gathers) if groups[-1] == group]
+        earlier = [self.state[g] for i in last for g in self.gathers[i][:-1]]
+        keeps, out = add_split(keeps, received, earlier, bits, self.columns.last)
+        self.columns.last = keeps[:1]
         self.state[group] = (keeps, self.move(out, bits)) if bits else keeps
-        if last:
-            self.gathered = keeps, self.move(keeps, [order[-1] for order in self.orders])
-
-    def join(self, level):
+        for i in last:
+            self.gathered[i] = keeps, self.move(keeps, [order[-1] for order in self.orders])
+
+    def join(self, gather, level):
         left = len(self.bits) - 1 - level
         bits = [order[left] for order in self.orders]
-        values = join(*self.gathered, bits, 0 if left else self.chunks, self.shared["last"])
-        self.shared["last"] = values[:1]
-        bits = [order[left - 1] for order in self.orders] if left else [1] * self.chunks
-        self.gathered = values, self.move(values, bits)
+        values = join(*self.gathered[gather], bits, 0 if left else self.chunks[1], self.columns.last)
+        self.columns.last = values[:1]
+        bits = [order[left - 1] for order in self.orders] if left else [1] * self.chunks[1]
+        self.gathered[gather] = values, self.move(values, bits)
 
     def places(self):
-        width, found, column = self.blocks[0].shape[1], {}, 0
-        for part in range(2):
-            for pairs in self.groups:
-                half = len(pairs) // 2
-                for pair in pairs[part * half : (part + 1) * half]:
-                    found[pair] = column
-                    column += width
+        width, found, base = self.columns.own.shape[1], {}, 0
+        for gather, groups in enumerate(self.gathers):
+            sizes = [len(self.groups[g]) * width // 2 for g in groups]
+            piece = self.gathered[gather][0][0].shape[1]
+            for which, g in enumerate(groups):
+                for index, pair in enumerate(self.groups[g]):
+                    found[pair], done = [], 0
+                    while done < width:
+                        part, inside = divmod(index * width + done, sizes[which])
+                        flat = part * sum(sizes) + sum(sizes[:which]) + inside
+                        chunk, offset = divmod(flat, piece)
+                        size = min(piece - offset, sizes[which] - inside, width - done)
+                        found[pair].append((base + chunk, offset, done, size))
+                        done += size
+            base += self.chunks[1]
         return found
 
     def update(self, *wanted):
-        values = update_blocks(self.blocks, self.places(), *self.gathered, wanted, self.shared["last"])
-        self.shared["last"] = values[:1]
+        blocks = self.blocks(1 + len(self.rounds))
+        own, other = ([v for i in range(len(self.gathers)) for v in self.gathered[i][core]] for core in range(2))
+        instead = {b: self.shares[b][0].updates[self.shares[b][1]] for b in wanted if self.shares.get(b)}
+        values = update_blocks(
+            blocks, self.places(), own, other, wanted, instead, self.owners, self.columns.last
+        )
+        self.columns.last = values[:1]
         for b, value in zip(wanted, values):
-            if b:
-                back = [(to, source) for source, to in enumerate(self.rounds[b - 1])]
-                value = lax.ppermute(value, "loop", back)
+            if b and b not in self.shares or b in instead:
+                step = self.columns.rounds[self.rounds[b - 1]]
+                value = shift(value, [step.index(p) for p in range(self.loop)], self.fsdp)
+            if b in instead:
+                wave, block = self.shares[b]
+                wave.updates[block] = value
             self.updates[b] = value
 
     def need(self, b):
-        self.shared["last"] = self.shared["last"] + [self.updates[b]]
-
-    def result(self):
-        tables = [self.owners] + [sends(self.owners, step) for step in self.rounds]
-        return [self.updates[b] for b in range(len(tables))], tables
+        self.columns.last = self.columns.last + [self.updates[b]]
+
+    def place(self, *wanted):
+        steps = [self.columns.rounds[self.rounds[b - 1]] if b else None for b in wanted]
+        tables = [sends(self.owners, step) if step else self.owners for step in steps]
+        found = [(self.updates[b], table) for b, table in zip(wanted, tables)]
+        columns = self.columns
+        after = [value for value in columns.last if value is not columns.out]
+        columns.out = place_slots(columns.out, found, columns.iterate, after)
+        columns.last = [columns.out]
 
 
 def body(iterate, expert_order, fsdp, loop):
-    waves, turns = plan(loop, fsdp)
-    shared = {"last": [], "arrived": []}
-    waves = [Wave(iterate, expert_order, owners, phases, fsdp, 4, shared) for owners, phases in waves]
+    phases, waves, shares, turns = plan(loop, fsdp)
+    columns = Columns(iterate, expert_order, phases, fsdp)
+    waves = [Wave(columns, *wave, {}, loop, CHUNKS) for wave in waves]
+    for (wave, block), (other, given) in shares.items():
+        waves[wave].shares[block] = waves[other], given
+        waves[other].shares[given] = None
     for turn, step, arguments in turns:
-        getattr(waves[turn], step)(*arguments)
-    results = [wave.result() for wave in waves]
-    return place_slots([found for found, _ in results], [tables for _, tables in results], iterate, shared["last"])
+        getattr(columns if step == "send" else waves[turn], step)(*arguments)
+    return columns.out
 
 
 def solution(mesh):

time: 247 us -> 226 us (0.915)
  the two profiles are of different devices: /device:TPU:8 before, /device:TPU:0 now
where the time goes in v4:
time: 226 us
  waiting for transfers between devices  147 us (65%)
  starting transfers between devices  51.3 us (23%)
  Pallas kernels  24.2 us (11%)
  local copies, waits for them, and re-layouts  2.71 us (1%)
    ppermute x10, waiting for transfers between devices, shift(): return lax.ppermute(value, ('fsdp', 'loop'), pairs)  93 us
    ppermute x58, waiting for transfers between devices, swap(): return lax.ppermute(value, ('fsdp', 'loop'), pairs)  53.9 us
    ppermute x58, starting transfers between devices, swap(): return lax.ppermute(value, ('fsdp', 'loop'), pairs)  35.1 us
    pallas_call x34, Pallas kernels, call(): pl.pallas_call(wrapped, out_shape=outs, in_specs=list(specs) + [ANY] * ex...  20.5 us
    ppermute x10, starting transfers between devices, shift(): return lax.ppermute(value, ('fsdp', 'loop'), pairs)  16.2 us
  transfers between devices with their start and end apart: 68, of which 42 were waited for; matrix products, arithmetic and copies ran while one was open for 0% of the time, Pallas kernels for 9%

profile of v4, /device:TPU:0, one launch (start us, length us, event | category | flops | bytes accessed | tf_op | source)
XLA Modules:
  0.0 225.7 jit_solution(11709486681391523676)
XLA Ops:
  4.0 3.1 %collective-permute-start = (bf16[896,512]{1,0:T(8,128)(2,1)S(1)}, bf16[896,512]{1,0:T(8,128)(2,1)S(1)}, u32[]{:S(2)}, u32[]{:S(2)}) collective-permute-start(bf16[896,512]{1,0:T(8,128)(2,1)S(1)} %get-tuple-element.104.refs_2_), channel_id=1, source_target_pairs={{0,1},{1,0},{2,3},{3,2},{4,5},{5,4},{6,7},{7,6},{8,9},{9,8},{10,11... | collective-permute-start | bytes 2752520 | tf_op jit(solution)/shard_map/ppermute | solution.py:255
  7.1 20.3 %collective-permute-done.refs_3_.refs_1_ = bf16[896,512]{1,0:T(8,128)(2,1)S(1)} collective-permute-done((bf16[896,512]{1,0:T(8,128)(2,1)S(1)}, bf16[896,512]{1,0:T(8,128)(2,1)S(1)}, u32[]{:S(2)}, u32[]{:S(2)}) %collective-permute-start) | collective-permute-done | bytes 917536 | tf_op jit(solution)/shard_map/ppermute | solution.py:255
  28.2 4.1 %collective-permute-start.8 = (bf16[896,512]{1,0:T(8,128)(2,1)S(1)}, bf16[896,512]{1,0:T(8,128)(2,1)S(1)}, u32[]{:S(2)}, u32[]{:S(2)}) collective-permute-start(bf16[896,512]{1,0:T(8,128)(2,1)S(1)} %pick.5.refs_3_), channel_id=1, source_target_pairs={{0,2},{1,0},{2,3},{3,1},{4,6},{5,4},{6,7},{7,5},{8,10},{9,8},{10,1... | collective-permute-start | bytes 2752520 | tf_op jit(solution)/shard_map/ppermute | solution.py:255
  38.6 12.1 %collective-permute-done.8.refs_3_ = bf16[896,512]{1,0:T(8,128)(2,1)S(1)} collective-permute-done((bf16[896,512]{1,0:T(8,128)(2,1)S(1)}, bf16[896,512]{1,0:T(8,128)(2,1)S(1)}, u32[]{:S(2)}, u32[]{:S(2)}) %collective-permute-start.8) | collective-permute-done | bytes 917536 | tf_op jit(solution)/shard_map/ppermute | solution.py:255
  51.5 2.6 %collective-permute-start.9 = (bf16[896,512]{1,0:T(8,128)(2,1)S(1)}, bf16[896,512]{1,0:T(8,128)(2,1)S(1)}, u32[]{:S(2)}, u32[]{:S(2)}) collective-permute-start(bf16[896,512]{1,0:T(8,128)(2,1)S(1)} %pick.6.refs_4_), channel_id=1, source_target_pairs={{0,1},{1,3},{2,0},{3,2},{4,5},{5,7},{6,4},{7,6},{8,9},{9,11},{10,8... | collective-permute-start | bytes 2752520 | tf_op jit(solution)/shard_map/ppermute | solution.py:255
  62.8 3.3 %collective-permute-done.20.refs_2_ = bf16[128,768]{1,0:T(8,128)(2,1)S(1)} collective-permute-done((bf16[128,768]{1,0:T(8,128)(2,1)S(1)}, bf16[128,768]{1,0:T(8,128)(2,1)S(1)}, u32[]{:S(2)}, u32[]{:S(2)}) %collective-permute-start.20) | collective-permute-done | bytes 196640 | tf_op jit(solution)/shard_map/ppermute | solution.py:249
  67.3 5.9 %collective-permute-done.9.refs_3_.refs_2_ = bf16[896,512]{1,0:T(8,128)(2,1)S(1)} collective-permute-done((bf16[896,512]{1,0:T(8,128)(2,1)S(1)}, bf16[896,512]{1,0:T(8,128)(2,1)S(1)}, u32[]{:S(2)}, u32[]{:S(2)}) %collective-permute-start.9) | collective-permute-done | bytes 917536 | tf_op jit(solution)/shard_map/ppermute | solution.py:255
  74.7 2.1 collective-permute-start.24
  86.0 2.3 %collective-permute-done.31.refs_1_ = bf16[256,384]{1,0:T(8,128)(2,1)S(1)} collective-permute-done((bf16[256,384]{1,0:T(8,128)(2,1)S(1)}, bf16[256,384]{1,0:T(8,128)(2,1)S(1)}, u32[]{:S(2)}, u32[]{:S(2)}) %collective-permute-start.31) | collective-permute-done | bytes 196640 | tf_op jit(solution)/shard_map/ppermute | solution.py:249
  91.9 2.7 %collective-permute-done.29.refs_2_ = bf16[64,768]{1,0:T(8,128)(2,1)S(1)} collective-permute-done((bf16[64,768]{1,0:T(8,128)(2,1)S(1)}, bf16[64,768]{1,0:T(8,128)(2,1)S(1)}, u32[]{:S(2)}, u32[]{:S(2)}) %collective-permute-start.29) | collective-permute-done | bytes 98336 | tf_op jit(solution)/shard_map/ppermute | solution.py:249
  95.0 3.8 %collective-permute-done.24.refs_3_ = bf16[896,512]{1,0:T(8,128)(2,1)S(1)} collective-permute-done((bf16[896,512]{1,0:T(8,128)(2,1)S(1)}, bf16[896,512]{1,0:T(8,128)(2,1)S(1)}, u32[]{:S(2)}, u32[]{:S(2)}) %collective-permute-start.24) | collective-permute-done | bytes 917536 | tf_op jit(solution)/shard_map/ppermute | solution.py:255
  98.8 2.4 %gram_part.9 = (f32[256,2048]{1,0:T(8,128)S(1)}, bf16[256,512]{1,0:T(8,128)(2,1)S(1)}, bf16[256,512]{1,0:T(8,128)(2,1)S(1)}, bf16[256,512]{1,0:T(8,128)(2,1)S(1)}, bf16[256,512]{1,0:T(8,128)(2,1)S(1)}) custom-call(bf16[896,512]{1,0:T(8,128)(2,1)S(1)} %get-tuple-element.103.refs_0_, bf16[896,512]{1,0:T(8,128)(2,1)S(1)} %collective-permute-done.refs_3_.refs_1_, ...), custom_call_target="tpu_custom_call" | custom-call | bytes 1 | tf_op jit(solution)/shard_map/gram_part/pallas_call | solution.py:81
  105.0 3.9 %collective-permute-done.37.refs_2_ = bf16[128,768]{1,0:T(8,128)(2,1)S(1)} collective-permute-done((bf16[128,768]{1,0:T(8,128)(2,1)S(1)}, bf16[128,768]{1,0:T(8,128)(2,1)S(1)}, u32[]{:S(2)}, u32[]{:S(2)}) %collective-permute-start.37) | collective-permute-done | bytes 196640 | tf_op jit(solution)/shard_map/ppermute | solution.py:249
  111.9 3.0 %collective-permute-done.39.refs_2_ = bf16[128,768]{1,0:T(8,128)(2,1)S(1)} collective-permute-done((bf16[128,768]{1,0:T(8,128)(2,1)S(1)}, bf16[128,768]{1,0:T(8,128)(2,1)S(1)}, u32[]{:S(2)}, u32[]{:S(2)}) %collective-permute-start.39) | collective-permute-done | bytes 196640 | tf_op jit(solution)/shard_map/ppermute | solution.py:249
  122.3 6.8 %collective-permute-done.49.refs_2_ = bf16[64,768]{1,0:T(8,128)(2,1)S(1)} collective-permute-done((bf16[64,768]{1,0:T(8,128)(2,1)S(1)}, bf16[64,768]{1,0:T(8,128)(2,1)S(1)}, u32[]{:S(2)}, u32[]{:S(2)}) %collective-permute-start.49) | collective-permute-done | bytes 98336 | tf_op jit(solution)/shard_map/ppermute | solution.py:249
  137.8 4.1 %collective-permute-done.55.refs_2_ = bf16[64,1792]{1,0:T(8,128)(2,1)S(1)} collective-permute-done((bf16[64,1792]{1,0:T(8,128)(2,1)S(1)}, bf16[64,1792]{1,0:T(8,128)(2,1)S(1)}, u32[]{:S(2)}, u32[]{:S(2)}) %collective-permute-start.55) | collective-permute-done | bytes 229408 | tf_op jit(solution)/shard_map/ppermute | solution.py:249
  146.0 6.3 %collective-permute-done.57.refs_2_ = bf16[128,1792]{1,0:T(8,128)(2,1)S(1)} collective-permute-done((bf16[128,1792]{1,0:T(8,128)(2,1)S(1)}, bf16[128,1792]{1,0:T(8,128)(2,1)S(1)}, u32[]{:S(2)}, u32[]{:S(2)}) %collective-permute-start.57) | collective-permute-done | bytes 458784 | tf_op jit(solution)/shard_map/ppermute | solution.py:249
  154.3 3.2 %collective-permute-done.60.refs_8_ = bf16[256,768]{1,0:T(8,128)(2,1)S(1)} collective-permute-done((bf16[256,768]{1,0:T(8,128)(2,1)S(1)}, bf16[256,768]{1,0:T(8,128)(2,1)S(1)}, u32[]{:S(2)}, u32[]{:S(2)}) %collective-permute-start.60) | collective-permute-done | bytes 393248 | tf_op jit(solution)/shard_map/ppermute | solution.py:249
  158.1 4.3 %update.6 = (bf16[896,512]{1,0:T(8,128)(2,1)S(1)}, bf16[896,512]{1,0:T(8,128)(2,1)S(1)}) custom-call(bf16[896,512]{1,0:T(8,128)(2,1)S(1)} %get-tuple-element.103.refs_0_, bf16[896,512]{1,0:T(8,128)(2,1)S(1)} %collective-permute-done.refs_3_.refs_1_, bf16[896,512]{1,0:T(8,128)(2,1)S(1)} %collective-permute-done.9.refs_3_.refs_2_, ...), custom_call_target="tpu_custom_call" | custom-call | bytes 1 | tf_op jit(solution)/shard_map/update/pallas_call | solution.py:81
  164.5 4.3 %update.7 = (bf16[896,512]{1,0:T(8,128)(2,1)S(1)}, bf16[896,512]{1,0:T(8,128)(2,1)S(1)}) custom-call(bf16[896,512]{1,0:T(8,128)(2,1)S(1)} %get-tuple-element.103.refs_0_, bf16[896,512]{1,0:T(8,128)(2,1)S(1)} %collective-permute-done.refs_3_.refs_1_, bf16[896,512]{1,0:T(8,128)(2,1)S(1)} %collective-permute-done.9.refs_3_.refs_2_, ...), custom_call_target="tpu_custom_call" | custom-call | bytes 1 | tf_op jit(solution)/shard_map/update/pallas_call | solution.py:81
  168.8 2.2 collective-permute-start.64
  171.9 13.8 %collective-permute-done.65.refs_1_.refs_0_ = bf16[896,512]{1,0:T(8,128)(2,1)S(1)} collective-permute-done((bf16[896,512]{1,0:T(8,128)(2,1)S(1)}, bf16[896,512]{1,0:T(8,128)(2,1)S(1)}, u32[]{:S(2)}, u32[]{:S(2)}) %collective-permute-start.65) | collective-permute-done | bytes 917536 | tf_op jit(solution)/shard_map/ppermute | solution.py:255
  185.7 18.9 %collective-permute-done.66.refs_0_ = bf16[896,512]{1,0:T(8,128)(2,1)S(1)} collective-permute-done((bf16[896,512]{1,0:T(8,128)(2,1)S(1)}, bf16[896,512]{1,0:T(8,128)(2,1)S(1)}, u32[]{:S(2)}, u32[]{:S(2)}) %collective-permute-start.66) | collective-permute-done | bytes 917536 | tf_op jit(solution)/shard_map/ppermute | solution.py:255
  206.5 18.1 %collective-permute-done.64.refs_0_ = bf16[896,512]{1,0:T(8,128)(2,1)S(1)} collective-permute-done((bf16[896,512]{1,0:T(8,128)(2,1)S(1)}, bf16[896,512]{1,0:T(8,128)(2,1)S(1)}, u32[]{:S(2)}, u32[]{:S(2)}) %collective-permute-start.64) | collective-permute-done | bytes 917536 | tf_op jit(solution)/shard_map/ppermute | solution.py:255
  (158 shorter events, 71.5 us)
Async XLA Ops:
  4.0 23.4 %collective-permute-start = (bf16[896,512]{1,0:T(8,128)(2,1)S(1)}, bf16[896,512]{1,0:T(8,128)(2,1)S(1)}, u32[]{:S(2)}, u32[]{:S(2)}) collective-permute-start(bf16[896,512]{1,0:T(8,128)(2,1)S(1)} %get-tuple-element.104.refs_2_), channel_id=1, source_target_pairs={{0,1},{1,0},{2,3},{3,2},{4,5},{5,4},{6,7},{7,6},{8,9},{9,8},{10,11... | collective-permute-start | bytes 2752520 | tf_op jit(solution)/shard_map/ppermute | solution.py:255
  7.0 20.4 %collective-permute-start.1 = (bf16[896,512]{1,0:T(8,128)(2,1)S(1)}, bf16[896,512]{1,0:T(8,128)(2,1)S(1)}, u32[]{:S(2)}, u32[]{:S(2)}) collective-permute-start(bf16[896,512]{1,0:T(8,128)(2,1)S(1)} %get-tuple-element.105), channel_id=1, source_target_pairs={{0,4},{1,2},{2,1},{3,7},{4,0},{5,6},{6,5},{7,3},{8,12},{9,10},{10,... | collective-permute-start | bytes 2752520 | tf_op jit(solution)/shard_map/ppermute | solution.py:255
  28.2 22.5 %collective-permute-start.8 = (bf16[896,512]{1,0:T(8,128)(2,1)S(1)}, bf16[896,512]{1,0:T(8,128)(2,1)S(1)}, u32[]{:S(2)}, u32[]{:S(2)}) collective-permute-start(bf16[896,512]{1,0:T(8,128)(2,1)S(1)} %pick.5.refs_3_), channel_id=1, source_target_pairs={{0,2},{1,0},{2,3},{3,1},{4,6},{5,4},{6,7},{7,5},{8,10},{9,8},{10,1... | collective-permute-start | bytes 2752520 | tf_op jit(solution)/shard_map/ppermute | solution.py:255
  51.5 21.7 %collective-permute-start.9 = (bf16[896,512]{1,0:T(8,128)(2,1)S(1)}, bf16[896,512]{1,0:T(8,128)(2,1)S(1)}, u32[]{:S(2)}, u32[]{:S(2)}) collective-permute-start(bf16[896,512]{1,0:T(8,128)(2,1)S(1)} %pick.6.refs_4_), channel_id=1, source_target_pairs={{0,1},{1,3},{2,0},{3,2},{4,5},{5,7},{6,4},{7,6},{8,9},{9,11},{10,8... | collective-permute-start | bytes 2752520 | tf_op jit(solution)/shard_map/ppermute | solution.py:255
  62.2 11.8 %collective-permute-start.27 = (bf16[64,1024]{1,0:T(8,128)(2,1)S(1)}, bf16[64,1024]{1,0:T(8,128)(2,1)S(1)}, u32[]{:S(2)}, u32[]{:S(2)}) collective-permute-start(bf16[64,1024]{1,0:T(8,128)(2,1)S(1)} %get-tuple-element.144), channel_id=1, source_target_pairs={{0,4},{1,17},{2,18},{3,7},{4,0},{5,21},{6,22},{7,3},{8,12},{9,25},... | collective-permute-start | bytes 393224 | tf_op jit(solution)/shard_map/ppermute | solution.py:249
  62.3 11.7 %collective-permute-start.28 = (bf16[64,1024]{1,0:T(8,128)(2,1)S(1)}, bf16[64,1024]{1,0:T(8,128)(2,1)S(1)}, u32[]{:S(2)}, u32[]{:S(2)}) collective-permute-start(bf16[64,1024]{1,0:T(8,128)(2,1)S(1)} %get-tuple-element.145), channel_id=1, source_target_pairs={{0,4},{1,9},{2,10},{3,7},{4,0},{5,13},{6,14},{7,3},{8,12},{9,1},{1... | collective-permute-start | bytes 393224 | tf_op jit(solution)/shard_map/ppermute | solution.py:249
  74.1 10.7 %collective-permute-start.35 = (bf16[64,2560]{1,0:T(8,128)(2,1)S(1)}, bf16[64,2560]{1,0:T(8,128)(2,1)S(1)}, u32[]{:S(2)}, u32[]{:S(2)}) collective-permute-start(bf16[64,2560]{1,0:T(8,128)(2,1)S(1)} %get-tuple-element.147.refs_4_.refs_0_), channel_id=1, source_target_pairs={{0,4},{1,17},{2,18},{3,7},{4,0},{5,21},{6,22},{7,3},{8,12},{9,25},... | collective-permute-start | bytes 983048 | tf_op jit(solution)/shard_map/ppermute | solution.py:249
  74.2 10.6 %collective-permute-start.36 = (bf16[64,2560]{1,0:T(8,128)(2,1)S(1)}, bf16[64,2560]{1,0:T(8,128)(2,1)S(1)}, u32[]{:S(2)}, u32[]{:S(2)}) collective-permute-start(bf16[64,2560]{1,0:T(8,128)(2,1)S(1)} %get-tuple-element.155.refs_1_), channel_id=1, source_target_pairs={{0,4},{1,9},{2,10},{3,7},{4,0},{5,13},{6,14},{7,3},{8,12},{9,1},{1... | collective-permute-start | bytes 983048 | tf_op jit(solution)/shard_map/ppermute | solution.py:249
  74.7 24.1 %collective-permute-start.24 = (bf16[896,512]{1,0:T(8,128)(2,1)S(1)}, bf16[896,512]{1,0:T(8,128)(2,1)S(1)}, u32[]{:S(2)}, u32[]{:S(2)}) collective-permute-start(bf16[896,512]{1,0:T(8,128)(2,1)S(1)} %pick.7.refs_6_), channel_id=1, source_target_pairs={{0,3},{1,5},{2,6},{3,0},{4,7},{5,1},{6,2},{7,4},{8,11},{9,13},{10,... | collective-permute-start | bytes 2752520 | tf_op jit(solution)/shard_map/ppermute | solution.py:255
  84.9 16.3 %collective-permute-start.41 = (bf16[128,2560]{1,0:T(8,128)(2,1)S(1)}, bf16[128,2560]{1,0:T(8,128)(2,1)S(1)}, u32[]{:S(2)}, u32[]{:S(2)}) collective-permute-start(bf16[128,2560]{1,0:T(8,128)(2,1)S(1)} %get-tuple-element.156.refs_5_.refs_0_), channel_id=1, source_target_pairs={{0,4},{1,9},{2,10},{3,7},{4,0},{5,13},{6,14},{7,3},{8,12},{9,1},{1... | collective-permute-start | bytes 1966088 | tf_op jit(solution)/shard_map/ppermute | solution.py:249
  85.0 16.2 %collective-permute-start.42 = (bf16[128,2560]{1,0:T(8,128)(2,1)S(1)}, bf16[128,2560]{1,0:T(8,128)(2,1)S(1)}, u32[]{:S(2)}, u32[]{:S(2)}) collective-permute-start(bf16[128,2560]{1,0:T(8,128)(2,1)S(1)} %get-tuple-element.163.refs_1_), channel_id=1, source_target_pairs={{0,4},{1,17},{2,18},{3,7},{4,0},{5,21},{6,22},{7,3},{8,12},{9,25},... | collective-permute-start | bytes 1966088 | tf_op jit(solution)/shard_map/ppermute | solution.py:249
  101.4 19.5 %collective-permute-start.51 = (bf16[256,2560]{1,0:T(8,128)(2,1)S(1)}, bf16[256,2560]{1,0:T(8,128)(2,1)S(1)}, u32[]{:S(2)}, u32[]{:S(2)}) collective-permute-start(bf16[256,2560]{1,0:T(8,128)(2,1)S(1)} %get-tuple-element.165.refs_4_), channel_id=1, source_target_pairs={{0,4},{1,5},{2,6},{3,7},{4,0},{5,1},{6,2},{7,3},{8,12},{9,13},{10,... | collective-permute-start | bytes 3932168 | tf_op jit(solution)/shard_map/ppermute | solution.py:249
  101.5 20.8 %collective-permute-start.52 = (bf16[256,2560]{1,0:T(8,128)(2,1)S(1)}, bf16[256,2560]{1,0:T(8,128)(2,1)S(1)}, u32[]{:S(2)}, u32[]{:S(2)}) collective-permute-start(bf16[256,2560]{1,0:T(8,128)(2,1)S(1)} %get-tuple-element.180.refs_5_), channel_id=1, source_target_pairs={{0,4},{1,5},{2,6},{3,7},{4,0},{5,1},{6,2},{7,3},{8,12},{9,13},{10,... | collective-permute-start | bytes 3932168 | tf_op jit(solution)/shard_map/ppermute | solution.py:249
  105.0 11.1 %collective-permute-start.43 = (bf16[256,512]{1,0:T(8,128)(2,1)S(1)}, bf16[256,512]{1,0:T(8,128)(2,1)S(1)}, u32[]{:S(2)}, u32[]{:S(2)}) collective-permute-start(bf16[256,512]{1,0:T(8,128)(2,1)S(1)} %get-tuple-element.169), channel_id=1, source_target_pairs={{0,4},{1,5},{2,6},{3,7},{4,0},{5,1},{6,2},{7,3},{8,12},{9,13},{10,... | collective-permute-start | bytes 786440 | tf_op jit(solution)/shard_map/ppermute | solution.py:249
  118.2 10.9 %collective-permute-start.47 = (bf16[128,1024]{1,0:T(8,128)(2,1)S(1)}, bf16[128,1024]{1,0:T(8,128)(2,1)S(1)}, u32[]{:S(2)}, u32[]{:S(2)}) collective-permute-start(bf16[128,1024]{1,0:T(8,128)(2,1)S(1)} %get-tuple-element.175), channel_id=1, source_target_pairs={{0,8},{1,5},{2,6},{3,11},{4,12},{5,1},{6,2},{7,15},{8,0},{9,13},{1... | collective-permute-start | bytes 786440 | tf_op jit(solution)/shard_map/ppermute | solution.py:249
  118.9 10.2 %collective-permute-start.48 = (bf16[128,1024]{1,0:T(8,128)(2,1)S(1)}, bf16[128,1024]{1,0:T(8,128)(2,1)S(1)}, u32[]{:S(2)}, u32[]{:S(2)}) collective-permute-start(bf16[128,1024]{1,0:T(8,128)(2,1)S(1)} %get-tuple-element.176), channel_id=1, source_target_pairs={{0,16},{1,5},{2,6},{3,19},{4,20},{5,1},{6,2},{7,23},{8,24},{9,13},... | collective-permute-start | bytes 786440 | tf_op jit(solution)/shard_map/ppermute | solution.py:249
  120.4 8.7 %collective-permute-start.49 = (bf16[64,768]{1,0:T(8,128)(2,1)S(1)}, bf16[64,768]{1,0:T(8,128)(2,1)S(1)}, u32[]{:S(2)}, u32[]{:S(2)}) collective-permute-start(bf16[64,768]{1,0:T(8,128)(2,1)S(1)} %get-tuple-element.178), channel_id=1, source_target_pairs={{0,16},{1,5},{2,6},{3,19},{4,20},{5,1},{6,2},{7,23},{8,24},{9,13},... | collective-permute-start | bytes 294920 | tf_op jit(solution)/shard_map/ppermute | solution.py:249
  122.3 30.6 %collective-permute-start.59 = (bf16[896,512]{1,0:T(8,128)(2,1)S(1)}, bf16[896,512]{1,0:T(8,128)(2,1)S(1)}, u32[]{:S(2)}, u32[]{:S(2)}) collective-permute-start(bf16[896,512]{1,0:T(8,128)(2,1)S(1)} %get-tuple-element.181.refs_4_), channel_id=1, source_target_pairs={{0,1},{1,3},{2,0},{3,2},{4,5},{5,7},{6,4},{7,6},{8,9},{9,11},{10,8... | collective-permute-start | bytes 2752520 | tf_op jit(solution)/shard_map/ppermute | solution.py:255
  143.0 9.3 %collective-permute-start.57 = (bf16[128,1792]{1,0:T(8,128)(2,1)S(1)}, bf16[128,1792]{1,0:T(8,128)(2,1)S(1)}, u32[]{:S(2)}, u32[]{:S(2)}) collective-permute-start(bf16[128,1792]{1,0:T(8,128)(2,1)S(1)} %get-tuple-element.191.refs_0_.refs_4_), channel_id=1, source_target_pairs={{0,8},{1,5},{2,6},{3,11},{4,12},{5,1},{6,2},{7,15},{8,0},{9,13},{1... | collective-permute-start | bytes 1376264 | tf_op jit(solution)/shard_map/ppermute | solution.py:249
  144.5 8.5 %collective-permute-start.58 = (bf16[128,1792]{1,0:T(8,128)(2,1)S(1)}, bf16[128,1792]{1,0:T(8,128)(2,1)S(1)}, u32[]{:S(2)}, u32[]{:S(2)}) collective-permute-start(bf16[128,1792]{1,0:T(8,128)(2,1)S(1)} %get-tuple-element.192.refs_1_), channel_id=1, source_target_pairs={{0,16},{1,5},{2,6},{3,19},{4,20},{5,1},{6,2},{7,23},{8,24},{9,13},... | collective-permute-start | bytes 1376264 | tf_op jit(solution)/shard_map/ppermute | solution.py:249
  154.2 16.7 %collective-permute-start.67 = (bf16[896,512]{1,0:T(8,128)(2,1)S(1)}, bf16[896,512]{1,0:T(8,128)(2,1)S(1)}, u32[]{:S(2)}, u32[]{:S(2)}) collective-permute-start(bf16[896,512]{1,0:T(8,128)(2,1)S(1)} %get-tuple-element.199), channel_id=1, source_target_pairs={{0,4},{1,2},{2,1},{3,7},{4,0},{5,6},{6,5},{7,3},{8,12},{9,10},{10,... | collective-permute-start | bytes 2752520 | tf_op jit(solution)/shard_map/ppermute | solution.py:255
  162.4 23.2 %collective-permute-start.65 = (bf16[896,512]{1,0:T(8,128)(2,1)S(1)}, bf16[896,512]{1,0:T(8,128)(2,1)S(1)}, u32[]{:S(2)}, u32[]{:S(2)}) collective-permute-start(bf16[896,512]{1,0:T(8,128)(2,1)S(1)} %get-tuple-element.197), channel_id=1, source_target_pairs={{0,2},{1,0},{2,3},{3,1},{4,6},{5,4},{6,7},{7,5},{8,10},{9,8},{10,1... | collective-permute-start | bytes 2752520 | tf_op jit(solution)/shard_map/ppermute | solution.py:255
  162.5 42.1 %collective-permute-start.66 = (bf16[896,512]{1,0:T(8,128)(2,1)S(1)}, bf16[896,512]{1,0:T(8,128)(2,1)S(1)}, u32[]{:S(2)}, u32[]{:S(2)}) collective-permute-start(bf16[896,512]{1,0:T(8,128)(2,1)S(1)} %get-tuple-element.195.refs_12_), channel_id=1, source_target_pairs={{0,1},{1,0},{2,3},{3,2},{4,5},{5,4},{6,7},{7,6},{8,9},{9,8},{10,11... | collective-permute-start | bytes 2752520 | tf_op jit(solution)/shard_map/ppermute | solution.py:255
  168.8 55.9 %collective-permute-start.64 = (bf16[896,512]{1,0:T(8,128)(2,1)S(1)}, bf16[896,512]{1,0:T(8,128)(2,1)S(1)}, u32[]{:S(2)}, u32[]{:S(2)}) collective-permute-start(bf16[896,512]{1,0:T(8,128)(2,1)S(1)} %get-tuple-element.196.refs_3_), channel_id=1, source_target_pairs={{0,3},{1,5},{2,6},{3,0},{4,7},{5,1},{6,2},{7,4},{8,11},{9,13},{10,... | collective-permute-start | bytes 2752520 | tf_op jit(solution)/shard_map/ppermute | solution.py:255
  (48 other events, 186.5 us)

commit v5 on v4

--- a/solution.py
+++ b/solution.py
@@ -12,7 +12,7 @@
 coef_linear = 3.4445
 coef_cubic = -4.775
 
-CHUNKS = 4, 2
+CHUNKS = 2, 2
 
 MIB = 2**20
 F32, BF16 = jnp.float32, jnp.bfloat16
@@ -24,40 +24,26 @@
 def plan(loop, fsdp):
     levels = fsdp.bit_length() - 2
     if loop == 4 and levels == 2:
-        phases = [[[1, 0, 3, 2], [0, 2, 1, 3]], [[2, 0, 3, 1]], [[1, 3, 0, 2]], [[3, 1, 2, 0]]]
-        waves = [({0: 0, 3: 3}, [[0], [3], [4]], [[0], [1, 2]]), ({1: 1, 2: 2}, [[0, 1], [2]], [[0, 1]])]
+        phases = [[[1, 3, 0, 2]], [[2, 0, 3, 1]], [[3, 1, 2, 0]], [[0, 2, 1, 3]]]
+        waves = [({0: 0, 3: 3}, [[0], [1], [2]], [[0], [1, 2]], {}), ({1: 1, 2: 2}, [[0, 1], [3]], [[0, 1]], {})]
         order = [
-            "0send0", "0send1", "1gram0", "1split0", "0gram0", "1add00", "0send2", "1gram1", "1add01", "1split1",
-            "0split0", "1add10", "0add00", "0send3", "1add11", "0add01", "0gram1", "1join00", "0split1", "0join00",
-            "0gram2", "1join01", "0add10", "0join01", "0split2", "1update32", "0add11", "0add20", "1update10",
-            "0add21", "0join10", "1need3", "0join11", "0update12", "0update30", "1place203", "0place120", "1place1",
-            "0place3",
+            "0pick00", "0send0", "0pick13", "0send1", "0gram0", "0split0", "0add00", "0add01", "0send2", "0gram1",
+            "0split1", "0join00", "0add10", "0join01", "0add11", "0gram2", "0send3", "0split2", "1gram0", "0add20",
+            "1split0", "0add21", "1add00", "0join10", "1add01", "1gram1", "0join11", "1split1", "0update3", "1add10",
+            "1add11", "1join00", "1join01", "0update120", "1update12", "0need3", "1update30", "0place0003",
+            "0place0102101112", "0place13",
         ]
         turns = [(int(t[0]), t[1:].rstrip("0123456789"), [int(c) for c in t[1:] if c.isdigit()]) for t in order]
-        return phases, waves, {(0, 2): (1, 1)}, turns
+        return phases, waves, {(1, 1): (0, 1), (1, 2): (0, 2)}, turns
     rounds = [[(p + step) % loop for p in range(loop)] for step in range(1, loop)]
-    turns = [(0, "send", [0]), (0, "gram", [0]), (0, "split", [0])]
+    turns = [(0, "pick", [0, 0]), (0, "send", [0]), (0, "gram", [0]), (0, "split", [0])]
     turns += [(0, step, [0, i]) for step in ("add", "join") for i in range(levels)]
-    turns += [(0, "update", list(range(loop))), (0, "place", list(range(loop)))]
-    return [rounds], [({p: p for p in range(loop)}, [list(range(len(rounds)))], [[0]])], {}, turns
+    turns += [(0, "update", list(range(loop))), (0, "place", [i for b in range(loop) for i in (0, b)])]
+    return [rounds], [({p: p for p in range(loop)}, [list(range(len(rounds)))], [[0]], {})], {}, turns
 
 
 def sends(owners, step):
     return {p: owners[to] for p, to in enumerate(step) if to in owners and to != p}
-
-
-def merge(tables):
-    merged, index = [], []
-    for table in tables:
-        for i, other in enumerate(merged):
-            if all(other.get(key, value) == value for key, value in table.items()):
-                other.update(table)
-                index.append(i)
-                break
-        else:
-            merged.append(dict(table))
-            index.append(len(merged) - 1)
-    return merged, index
 
 
 def lookup(table, place):
@@ -111,7 +97,7 @@
     return pl.ds(pl.multiple_of(part * height, height), height)
 
 
-def pick(iterate, expert_order, tables, after):
+def pick(iterate, expert_order, tables, after, alone):
     def kernel(order, source, *rest):
         outs, sems = rest[:-1], rest[-1]
         place = lax.axis_index("loop")
@@ -124,7 +110,20 @@
 
     outs = [struct(iterate.shape[1:], iterate.dtype)] * len(tables)
     sems = [pltpu.SemaphoreType.DMA((len(tables),))]
-    return call(kernel, "pick", [expert_order, iterate], [SMEM, ANY], outs, 8, sems, after=after)
+    return call(kernel, "pick", [expert_order, iterate], [SMEM, ANY], outs, 62 if alone else 8, sems, after=after)
+
+
+def gate(value, after):
+    return pl.pallas_call(
+        lambda *refs: None,
+        out_shape=struct(value.shape, value.dtype),
+        in_specs=[ANY] * (1 + len(after)),
+        out_specs=ANY,
+        input_output_aliases={0: 0},
+        compiler_params=pltpu.CompilerParams(vmem_limit_bytes=MIB),
+        cost_estimate=pl.CostEstimate(flops=0, bytes_accessed=1, transcendentals=0),
+        name="gate",
+    )(value, *after)
 
 
 def gram_part(blocks, pairs, chunks, owners, after):
@@ -255,23 +254,29 @@
     return lax.ppermute(value, ("fsdp", "loop"), pairs)
 
 
-def update_blocks(blocks, places, own, other, wanted, instead, owners, after):
+def update_blocks(blocks, places, own, other, wanted, pieces, instead, owners, after):
     rows, width = blocks[0].shape
     half, count = width // 2, len(blocks)
     total, chunks = count * width, len(own)
     factor = 0.2 * D**0.5
+    parts = []
+    for b in wanted:
+        weights, row = pieces.get(b, (1,)), 0
+        for weight in weights:
+            parts.append((b, row, rows * weight // sum(weights)))
+            row += parts[-1][2]
 
     def kernel(*refs):
         xs, strips = refs[:count], (refs[count : count + chunks], refs[count + chunks : count + 2 * chunks])
         refs = refs[count + 2 * chunks :]
         given, refs = refs[: len(instead)], refs[len(instead) :]
-        outs, (x, g) = refs[: len(wanted)], refs[len(wanted) :]
+        outs, (x, g) = refs[: len(parts)], refs[len(parts) :]
         mine = is_one_of(owners)
         pl.when(mine)(lambda: multiply(xs, strips, outs, x, g))
         for b, value in zip(instead, given):
 
             @pl.when(jnp.logical_not(mine))
-            def _(out=outs[wanted.index(b)], value=value):
+            def _(out=outs[parts.index((b, 0, rows))], value=value):
                 out[...] = value[...]
 
     def multiply(xs, strips, outs, x, g):
@@ -286,35 +291,43 @@
                 for chunk, offset, first, size in pieces:
                     at = b * width + first
                     g[where, at : at + size] = strip[chunk][:, offset : offset + size]
-        for out, b in zip(outs, wanted):
+        for b in wanted:
             low, high = b * width, (b + 1) * width
             product = jnp.dot(x[:, :high], g[:high, low:high], preferred_element_type=F32)
             if b < count - 1:
                 product += lax.dot_general(
                     x[:, high:], g[low:high, high:], (((1,), (1,)), ((), ())), preferred_element_type=F32
                 )
-            out[...] = (factor * (coef_linear * x[:, low:high].astype(F32) + coef_cubic * product)).astype(BF16)
+            result = (factor * (coef_linear * x[:, low:high].astype(F32) + coef_cubic * product)).astype(BF16)
+            for out, (block, row, height) in zip(outs, parts):
+                if block == b:
+                    out[...] = result[row : row + height]
 
     scratch = [pltpu.VMEM((rows, total), BF16), pltpu.VMEM((total, total), BF16)]
-    outs = [struct((rows, width), BF16)] * len(wanted)
+    outs = [struct((height, width), BF16) for _, _, height in parts]
     ins = [*blocks, *own, *other, *instead.values()]
     return call(kernel, "update", ins, [VMEM] * len(ins), outs, 30, scratch, after)
 
 
 def place_slots(out, found, like, after):
     old = [] if out is None else [out]
-    ins = [value for value, _ in found]
-    cases = [(i, place, slot) for i, (_, table) in enumerate(found) for place, slot in table.items()]
+    ins, cases = [], []
+    for values, table in found:
+        row = 0
+        for value in values:
+            cases += [(len(ins), place, slot, pl.ds(row, value.shape[0])) for place, slot in table.items()]
+            ins.append(value)
+            row += value.shape[0]
 
     def kernel(*refs):
         values, target, sems = refs[: len(ins)], refs[-2], refs[-1]
         here = lax.axis_index("loop")
         for wait in (False, True):
-            for i, place, slot in cases:
+            for i, place, slot, rows in cases:
 
                 @pl.when(here == place)
-                def _(i=i, slot=slot):
-                    copy = pltpu.make_async_copy(values[i], target.at[slot], sems.at[i])
+                def _(i=i, slot=slot, rows=rows):
+                    copy = pltpu.make_async_copy(values[i], target.at[slot, rows], sems.at[i])
                     copy.wait() if wait else copy.start()
 
     return pl.pallas_call(
@@ -330,27 +343,43 @@
     )(*ins, *old, *after)
 
 
+def back(returns):
+    to = {owner: p for owners, step in returns for p, owner in enumerate(step) if owner in owners}
+    places = range(len(returns[0][1]))
+    rest = iter([p for p in places if p not in to.values()])
+    return [to[p] if p in to else next(rest) for p in places]
+
+
 class Columns:
     def __init__(self, iterate, expert_order, phases, fsdp):
         self.iterate, self.expert_order, self.phases, self.fsdp = iterate, expert_order, phases, fsdp
         self.rounds = [step for rounds in phases for step in rounds]
-        self.own, self.arrived, self.last, self.out = None, [], [], None
+        self.own, self.picked, self.arrived, self.ends, self.last, self.out = None, {}, [], [0], [], None
+
+    def pick(self, first, last):
+        steps = [step for rounds in self.phases[first : last + 1] for step in rounds]
+        tables = [{p: to for p, to in enumerate(step) if p != to} for step in steps]
+        places = {p: p for p in range(len(steps[0]))}
+        picked = pick(self.iterate, self.expert_order, tables if first else tables + [places], self.last, not first)
+        if not first:
+            self.own = picked.pop()
+        for phase in range(first, last + 1):
+            count = len(self.phases[phase])
+            self.picked[phase], picked = picked[:count], picked[count:]
+            self.last = self.picked[phase][:1]
 
     def send(self, phase):
-        rounds = self.phases[phase]
-        tables = [{p: to for p, to in enumerate(step) if p != to} for step in rounds]
-        places = {p: p for p in range(len(rounds[0]))}
-        merged, index = merge(tables if phase else tables + [places])
-        before = self.arrived[len(self.arrived) - len(self.phases[phase - 1]) :] if phase else []
-        picked = pick(self.iterate, self.expert_order, merged, self.last + before)
-        if not phase:
-            self.own = picked[index[-1]]
-        self.arrived += [shift(picked[i], step, self.fsdp) for i, step in zip(index, rounds)]
+        picked = self.picked[phase]
+        if phase:
+            before = self.arrived[self.ends[phase - 1] : self.ends[phase]]
+            picked = [gate(value, self.last + before) for value in picked]
+        self.arrived += [shift(value, step, self.fsdp) for value, step in zip(picked, self.phases[phase])]
+        self.ends.append(len(self.arrived))
         self.last = picked[:1]
 
 
 class Wave:
-    def __init__(self, columns, owners, groups, gathers, shares, loop, chunks):
+    def __init__(self, columns, owners, groups, gathers, pieces, shares, loop, chunks):
         self.columns, self.owners, self.loop, self.chunks = columns, owners, loop, chunks
         self.fsdp = columns.fsdp
         self.bits = [1 << i for i in range(1, self.fsdp.bit_length() - 1)]
@@ -361,7 +390,7 @@
             count = first + len(group) + 1
             self.groups.append([(a, b) for b in range(first + 1 if first else 0, count) for a in range(b + 1)])
             first += len(group)
-        self.updates, self.shares = {}, shares
+        self.updates, self.shares, self.pieces = {b: [] for b in pieces}, shares, pieces
 
     def blocks(self, count):
         return [self.columns.own] + [self.columns.arrived[number] for number in self.rounds[: count - 1]]
@@ -425,29 +454,29 @@
         own, other = ([v for i in range(len(self.gathers)) for v in self.gathered[i][core]] for core in range(2))
         instead = {b: self.shares[b][0].updates[self.shares[b][1]] for b in wanted if self.shares.get(b)}
         values = update_blocks(
-            blocks, self.places(), own, other, wanted, instead, self.owners, self.columns.last
+            blocks, self.places(), own, other, wanted, self.pieces, instead, self.owners, self.columns.last
         )
         self.columns.last = values[:1]
-        for b, value in zip(wanted, values):
+        for b, value in zip([b for b in wanted for _ in self.pieces.get(b, (1,))], values):
             if b and b not in self.shares or b in instead:
-                step = self.columns.rounds[self.rounds[b - 1]]
-                value = shift(value, [step.index(p) for p in range(self.loop)], self.fsdp)
+                returns = [self.returned(b)]
+                if b in instead:
+                    returns.append(self.shares[b][0].returned(self.shares[b][1]))
+                value = shift(value, back(returns), self.fsdp)
             if b in instead:
                 wave, block = self.shares[b]
                 wave.updates[block] = value
-            self.updates[b] = value
+            self.updates[b] = self.updates[b] + [value] if b in self.pieces else value
 
     def need(self, b):
-        self.columns.last = self.columns.last + [self.updates[b]]
-
-    def place(self, *wanted):
-        steps = [self.columns.rounds[self.rounds[b - 1]] if b else None for b in wanted]
-        tables = [sends(self.owners, step) if step else self.owners for step in steps]
-        found = [(self.updates[b], table) for b, table in zip(wanted, tables)]
-        columns = self.columns
-        after = [value for value in columns.last if value is not columns.out]
-        columns.out = place_slots(columns.out, found, columns.iterate, after)
-        columns.last = [columns.out]
+        self.columns.last = self.columns.last + self.found(b)[0]
+
+    def returned(self, b):
+        return self.owners, self.columns.rounds[self.rounds[b - 1]]
+
+    def found(self, b):
+        value = self.updates[b]
+        return value if isinstance(value, list) else [value], sends(*self.returned(b)) if b else self.owners
 
 
 def body(iterate, expert_order, fsdp, loop):
@@ -457,8 +486,14 @@
     for (wave, block), (other, given) in shares.items():
         waves[wave].shares[block] = waves[other], given
         waves[other].shares[given] = None
-    for turn, step, arguments in turns:
-        getattr(columns if step == "send" else waves[turn], step)(*arguments)
+    for turn, step, numbers in turns:
+        if step == "place":
+            found = [waves[wave].found(b) for wave, b in zip(numbers[::2], numbers[1::2])]
+            after = [value for value in columns.last if value is not columns.out]
+            columns.out = place_slots(columns.out, found, iterate, after)
+            columns.last = [columns.out]
+        else:
+            getattr(columns if step in ("send", "pick") else waves[turn], step)(*numbers)
     return columns.out
 
 

time: 226 us -> 212 us (0.938)
  the two profiles are of different devices: /device:TPU:0 before, /device:TPU:8 now
where the time goes in v5:
time: 212 us
  waiting for transfers between devices  151 us (71%)
  starting transfers between devices  32.8 us (15%)
  Pallas kernels  23.9 us (11%)
  local copies, waits for them, and re-layouts  3.22 us (2%)
    ppermute x8, waiting for transfers between devices, shift(): return lax.ppermute(value, ('fsdp', 'loop'), pairs)  87.4 us
    ppermute x48, waiting for transfers between devices, swap(): return lax.ppermute(value, ('fsdp', 'loop'), pairs)  63.8 us
    ppermute x48, starting transfers between devices, swap(): return lax.ppermute(value, ('fsdp', 'loop'), pairs)  23.6 us
    pallas_call x32, Pallas kernels, call(): pl.pallas_call(wrapped, out_shape=outs, in_specs=list(specs) + [ANY] * ex...  21.4 us
    ppermute x8, starting transfers between devices, shift(): return lax.ppermute(value, ('fsdp', 'loop'), pairs)  9.15 us
  transfers between devices with their start and end apart: 56, of which 40 were waited for; matrix products, arithmetic and copies ran while one was open for 0% of the time, Pallas kernels for 7%

profile of v5, /device:TPU:8, one launch (start us, length us, event | category | flops | bytes accessed | tf_op | source)
XLA Modules:
  0.0 211.6 jit_solution(8400443130809848724)
XLA Ops:
  0.0 3.5 %pick.2 = (bf16[896,512]{1,0:T(8,128)(2,1)}, bf16[896,512]{1,0:T(8,128)(2,1)}) custom-call(s32[4]{0:T(128)} %refs_0_.3, bf16[4,896,512]{2,1,0:T(8,128)(2,1)} %refs_1_.3), custom_call_target="tpu_custom_call" | custom-call | bytes 1 | tf_op jit(solution)/shard_map/pick/pallas_call | solution.py:67
  3.5 2.6 %collective-permute-start = (bf16[896,512]{1,0:T(8,128)(2,1)}, bf16[896,512]{1,0:T(8,128)(2,1)S(1)}, u32[]{:S(2)}, u32[]{:S(2)}) collective-permute-start(bf16[896,512]{1,0:T(8,128)(2,1)} %get-tuple-element.95.refs_2_), channel_id=1, source_target_pairs={{0,1},{1,3},{2,0},{3,2},{4,5},{5,7},{6,4},{7,6},{8,9},{9,11},{10,8... | collective-permute-start | bytes 2752520 | tf_op jit(solution)/shard_map/ppermute | solution.py:254
  6.2 2.0 copy-done.1
  10.7 15.4 %collective-permute-done.refs_2_.refs_1_ = bf16[896,512]{1,0:T(8,128)(2,1)S(1)} collective-permute-done((bf16[896,512]{1,0:T(8,128)(2,1)}, bf16[896,512]{1,0:T(8,128)(2,1)S(1)}, u32[]{:S(2)}, u32[]{:S(2)}) %collective-permute-start) | collective-permute-done | bytes 917536 | tf_op jit(solution)/shard_map/ppermute | solution.py:254
  33.1 15.8 %collective-permute-done.1.refs_2_ = bf16[896,512]{1,0:T(8,128)(2,1)S(1)} collective-permute-done((bf16[896,512]{1,0:T(8,128)(2,1)S(1)}, bf16[896,512]{1,0:T(8,128)(2,1)S(1)}, u32[]{:S(2)}, u32[]{:S(2)}) %collective-permute-start.1) | collective-permute-done | bytes 917536 | tf_op jit(solution)/shard_map/ppermute | solution.py:254
  49.9 2.0 collective-permute-done.9.refs_1_
  59.0 3.5 %gram_part.8 = (f32[256,3072]{1,0:T(8,128)S(1)}, bf16[256,1536]{1,0:T(8,128)(2,1)S(1)}, bf16[256,1536]{1,0:T(8,128)(2,1)S(1)}) custom-call(bf16[896,512]{1,0:T(8,128)(2,1)S(1)} %copy-done, bf16[896,512]{1,0:T(8,128)(2,1)S(1)} %collective-permute-done.refs_2_.refs_1_, bf16[896,512]{1,0:T(8,128)(2,1)S(1)} %collective-permute-done.1.refs_2_, ...), custom_call_target="tpu_custom_call" | custom-call | bytes 1 | tf_op jit(solution)/shard_map/gram_part/pallas_call | solution.py:67
  64.3 2.0 collective-permute-done.24.refs_2_
  72.3 6.1 %collective-permute-done.26.refs_2_ = bf16[128,1536]{1,0:T(8,128)(2,1)S(1)} collective-permute-done((bf16[128,1536]{1,0:T(8,128)(2,1)S(1)}, bf16[128,1536]{1,0:T(8,128)(2,1)S(1)}, u32[]{:S(2)}, u32[]{:S(2)}) %collective-permute-start.26) | collective-permute-done | bytes 393248 | tf_op jit(solution)/shard_map/ppermute | solution.py:248
  82.5 4.8 %collective-permute-done.30.refs_2_ = bf16[64,1536]{1,0:T(8,128)(2,1)S(1)} collective-permute-done((bf16[64,1536]{1,0:T(8,128)(2,1)S(1)}, bf16[64,1536]{1,0:T(8,128)(2,1)S(1)}, u32[]{:S(2)}, u32[]{:S(2)}) %collective-permute-start.30) | collective-permute-done | bytes 196640 | tf_op jit(solution)/shard_map/ppermute | solution.py:248
  89.3 2.4 %gram_part.9 = (f32[256,2048]{1,0:T(8,128)S(1)}, bf16[256,1024]{1,0:T(8,128)(2,1)S(1)}, bf16[256,1024]{1,0:T(8,128)(2,1)S(1)}) custom-call(bf16[896,512]{1,0:T(8,128)(2,1)S(1)} %copy-done, bf16[896,512]{1,0:T(8,128)(2,1)S(1)} %collective-permute-done.refs_2_.refs_1_, bf16[896,512]{1,0:T(8,128)(2,1)S(1)} %collective-permute-done.1.refs_2_, ...), custom_call_target="tpu_custom_call" | custom-call | bytes 1 | tf_op jit(solution)/shard_map/gram_part/pallas_call | solution.py:67
  93.8 3.2 %collective-permute-done.35.refs_2_ = bf16[256,1024]{1,0:T(8,128)(2,1)S(1)} collective-permute-done((bf16[256,1024]{1,0:T(8,128)(2,1)S(1)}, bf16[256,1024]{1,0:T(8,128)(2,1)S(1)}, u32[]{:S(2)}, u32[]{:S(2)}) %collective-permute-start.35) | collective-permute-done | bytes 524320 | tf_op jit(solution)/shard_map/ppermute | solution.py:248
  100.0 5.7 %collective-permute-done.38.refs_2_ = bf16[128,1024]{1,0:T(8,128)(2,1)S(1)} collective-permute-done((bf16[128,1024]{1,0:T(8,128)(2,1)S(1)}, bf16[128,1024]{1,0:T(8,128)(2,1)S(1)}, u32[]{:S(2)}, u32[]{:S(2)}) %collective-permute-start.38) | collective-permute-done | bytes 262176 | tf_op jit(solution)/shard_map/ppermute | solution.py:248
  108.8 2.8 %collective-permute-done.44.refs_2_ = bf16[64,1024]{1,0:T(8,128)(2,1)S(1)} collective-permute-done((bf16[64,1024]{1,0:T(8,128)(2,1)S(1)}, bf16[64,1024]{1,0:T(8,128)(2,1)S(1)}, u32[]{:S(2)}, u32[]{:S(2)}) %collective-permute-start.44) | collective-permute-done | bytes 131104 | tf_op jit(solution)/shard_map/ppermute | solution.py:248
  114.7 6.1 %collective-permute-done.46.refs_2_ = bf16[64,2560]{1,0:T(8,128)(2,1)S(1)} collective-permute-done((bf16[64,2560]{1,0:T(8,128)(2,1)S(1)}, bf16[64,2560]{1,0:T(8,128)(2,1)S(1)}, u32[]{:S(2)}, u32[]{:S(2)}) %collective-permute-start.46) | collective-permute-done | bytes 327712 | tf_op jit(solution)/shard_map/ppermute | solution.py:248
  123.8 11.1 %collective-permute-done.48.refs_2_ = bf16[128,2560]{1,0:T(8,128)(2,1)S(1)} collective-permute-done((bf16[128,2560]{1,0:T(8,128)(2,1)S(1)}, bf16[128,2560]{1,0:T(8,128)(2,1)S(1)}, u32[]{:S(2)}, u32[]{:S(2)}) %collective-permute-start.48) | collective-permute-done | bytes 655392 | tf_op jit(solution)/shard_map/ppermute | solution.py:248
  135.8 2.4 %collective-permute-done.51.refs_7_ = bf16[256,2560]{1,0:T(8,128)(2,1)S(1)} collective-permute-done((bf16[256,2560]{1,0:T(8,128)(2,1)S(1)}, bf16[256,2560]{1,0:T(8,128)(2,1)S(1)}, u32[]{:S(2)}, u32[]{:S(2)}) %collective-permute-start.51) | collective-permute-done | bytes 1310752 | tf_op jit(solution)/shard_map/ppermute | solution.py:248
  140.1 4.3 %update.6 = (bf16[896,512]{1,0:T(8,128)(2,1)S(1)}, bf16[896,512]{1,0:T(8,128)(2,1)S(1)}) custom-call(bf16[896,512]{1,0:T(8,128)(2,1)S(1)} %copy-done, bf16[896,512]{1,0:T(8,128)(2,1)S(1)} %collective-permute-done.refs_2_.refs_1_, bf16[896,512]{1,0:T(8,128)(2,1)S(1)} %collective-permute-done.1.refs_2_, bf16[896,512]{1,0:T(8,128)(2,1)S(1)} %collective-permute-done.19.refs_3_, ...), custom_call_target="tpu_custom_call" | custom-call | bytes 1 | tf_op jit(solution)/shard_map/update/pallas_call | solution.py:67
  144.5 2.0 collective-permute-start.54
  146.6 4.3 %update.7 = (bf16[896,512]{1,0:T(8,128)(2,1)S(1)}, bf16[896,512]{1,0:T(8,128)(2,1)S(1)}) custom-call(bf16[896,512]{1,0:T(8,128)(2,1)S(1)} %copy-done, bf16[896,512]{1,0:T(8,128)(2,1)S(1)} %collective-permute-done.refs_2_.refs_1_, bf16[896,512]{1,0:T(8,128)(2,1)S(1)} %collective-permute-done.1.refs_2_, bf16[896,512]{1,0:T(8,128)(2,1)S(1)} %collective-permute-done.19.refs_3_, ...), custom_call_target="tpu_custom_call" | custom-call | bytes 1 | tf_op jit(solution)/shard_map/update/pallas_call | solution.py:67
  150.8 2.5 %collective-permute-start.53 = (bf16[896,512]{1,0:T(8,128)(2,1)S(1)}, bf16[896,512]{1,0:T(8,128)(2,1)S(1)}, u32[]{:S(2)}, u32[]{:S(2)}) collective-permute-start(bf16[896,512]{1,0:T(8,128)(2,1)S(1)} %get-tuple-element.179.refs_2_), channel_id=1, source_target_pairs={{0,4},{1,2},{2,1},{3,7},{4,0},{5,6},{6,5},{7,3},{8,12},{9,10},{10,... | collective-permute-start | bytes 2752520 | tf_op jit(solution)/shard_map/ppermute | solution.py:254
  153.4 18.4 %collective-permute-done.55.refs_1_.refs_4_ = bf16[896,512]{1,0:T(8,128)(2,1)S(1)} collective-permute-done((bf16[896,512]{1,0:T(8,128)(2,1)S(1)}, bf16[896,512]{1,0:T(8,128)(2,1)S(1)}, u32[]{:S(2)}, u32[]{:S(2)}) %collective-permute-start.55) | collective-permute-done | bytes 917536 | tf_op jit(solution)/shard_map/ppermute | solution.py:254
  171.8 19.2 %collective-permute-done.54.refs_0_.refs_3_ = bf16[896,512]{1,0:T(8,128)(2,1)S(1)} collective-permute-done((bf16[896,512]{1,0:T(8,128)(2,1)S(1)}, bf16[896,512]{1,0:T(8,128)(2,1)S(1)}, u32[]{:S(2)}, u32[]{:S(2)}) %collective-permute-start.54) | collective-permute-done | bytes 917536 | tf_op jit(solution)/shard_map/ppermute | solution.py:254
  192.6 17.9 %collective-permute-done.53.refs_0_ = bf16[896,512]{1,0:T(8,128)(2,1)S(1)} collective-permute-done((bf16[896,512]{1,0:T(8,128)(2,1)S(1)}, bf16[896,512]{1,0:T(8,128)(2,1)S(1)}, u32[]{:S(2)}, u32[]{:S(2)}) %collective-permute-start.53) | collective-permute-done | bytes 917536 | tf_op jit(solution)/shard_map/ppermute | solution.py:254
  (134 shorter events, 50.9 us)
Async XLA Ops:
  3.5 22.6 %collective-permute-start = (bf16[896,512]{1,0:T(8,128)(2,1)}, bf16[896,512]{1,0:T(8,128)(2,1)S(1)}, u32[]{:S(2)}, u32[]{:S(2)}) collective-permute-start(bf16[896,512]{1,0:T(8,128)(2,1)} %get-tuple-element.95.refs_2_), channel_id=1, source_target_pairs={{0,1},{1,3},{2,0},{3,2},{4,5},{5,7},{6,4},{7,6},{8,9},{9,11},{10,8... | collective-permute-start | bytes 2752520 | tf_op jit(solution)/shard_map/ppermute | solution.py:254
  26.1 22.8 %collective-permute-start.1 = (bf16[896,512]{1,0:T(8,128)(2,1)S(1)}, bf16[896,512]{1,0:T(8,128)(2,1)S(1)}, u32[]{:S(2)}, u32[]{:S(2)}) collective-permute-start(bf16[896,512]{1,0:T(8,128)(2,1)S(1)} %gate.3.refs_2_), channel_id=1, source_target_pairs={{0,2},{1,0},{2,3},{3,1},{4,6},{5,4},{6,7},{7,5},{8,10},{9,8},{10,1... | collective-permute-start | bytes 2752520 | tf_op jit(solution)/shard_map/ppermute | solution.py:254
  48.8 7.2 %collective-permute-start.8 = (bf16[896,512]{1,0:T(8,128)(2,1)S(1)}, bf16[896,512]{1,0:T(8,128)(2,1)S(1)}, u32[]{:S(2)}, u32[]{:S(2)}) collective-permute-start(bf16[896,512]{1,0:T(8,128)(2,1)S(1)} %gate.4.refs_3_), channel_id=1, source_target_pairs={{0,3},{1,5},{2,6},{3,0},{4,7},{5,1},{6,2},{7,4},{8,11},{9,13},{10,... | collective-permute-start | bytes 2752520 | tf_op jit(solution)/shard_map/ppermute | solution.py:254
  63.6 25.8 %collective-permute-start.19 = (bf16[896,512]{1,0:T(8,128)(2,1)S(1)}, bf16[896,512]{1,0:T(8,128)(2,1)S(1)}, u32[]{:S(2)}, u32[]{:S(2)}) collective-permute-start(bf16[896,512]{1,0:T(8,128)(2,1)S(1)} %gate.5.refs_3_), channel_id=1, source_target_pairs={{0,4},{1,2},{2,1},{3,7},{4,0},{5,6},{6,5},{7,3},{8,12},{9,10},{10,... | collective-permute-start | bytes 2752520 | tf_op jit(solution)/shard_map/ppermute | solution.py:254
  67.1 11.4 %collective-permute-start.26 = (bf16[128,1536]{1,0:T(8,128)(2,1)S(1)}, bf16[128,1536]{1,0:T(8,128)(2,1)S(1)}, u32[]{:S(2)}, u32[]{:S(2)}) collective-permute-start(bf16[128,1536]{1,0:T(8,128)(2,1)S(1)} %get-tuple-element.140), channel_id=1, source_target_pairs={{0,4},{1,9},{2,10},{3,7},{4,0},{5,13},{6,14},{7,3},{8,12},{9,1},{1... | collective-permute-start | bytes 1179656 | tf_op jit(solution)/shard_map/ppermute | solution.py:248
  68.6 11.0 %collective-permute-start.27 = (bf16[128,1536]{1,0:T(8,128)(2,1)S(1)}, bf16[128,1536]{1,0:T(8,128)(2,1)S(1)}, u32[]{:S(2)}, u32[]{:S(2)}) collective-permute-start(bf16[128,1536]{1,0:T(8,128)(2,1)S(1)} %get-tuple-element.141), channel_id=1, source_target_pairs={{0,4},{1,17},{2,18},{3,7},{4,0},{5,21},{6,22},{7,3},{8,12},{9,25},... | collective-permute-start | bytes 1179656 | tf_op jit(solution)/shard_map/ppermute | solution.py:248
  71.8 8.0 %collective-permute-start.33 = (bf16[64,1792]{1,0:T(8,128)(2,1)S(1)}, bf16[64,1792]{1,0:T(8,128)(2,1)S(1)}, u32[]{:S(2)}, u32[]{:S(2)}) collective-permute-start(bf16[64,1792]{1,0:T(8,128)(2,1)S(1)} %get-tuple-element.151.refs_1_), channel_id=1, source_target_pairs={{0,8},{1,5},{2,6},{3,11},{4,12},{5,1},{6,2},{7,15},{8,0},{9,13},{1... | collective-permute-start | bytes 688136 | tf_op jit(solution)/shard_map/ppermute | solution.py:248
  72.2 7.7 %collective-permute-start.32 = (bf16[64,1792]{1,0:T(8,128)(2,1)S(1)}, bf16[64,1792]{1,0:T(8,128)(2,1)S(1)}, u32[]{:S(2)}, u32[]{:S(2)}) collective-permute-start(bf16[64,1792]{1,0:T(8,128)(2,1)S(1)} %get-tuple-element.146.refs_4_.refs_0_), channel_id=1, source_target_pairs={{0,16},{1,5},{2,6},{3,19},{4,20},{5,1},{6,2},{7,23},{8,24},{9,13},... | collective-permute-start | bytes 688136 | tf_op jit(solution)/shard_map/ppermute | solution.py:248
  79.9 11.9 %collective-permute-start.37 = (bf16[128,1792]{1,0:T(8,128)(2,1)S(1)}, bf16[128,1792]{1,0:T(8,128)(2,1)S(1)}, u32[]{:S(2)}, u32[]{:S(2)}) collective-permute-start(bf16[128,1792]{1,0:T(8,128)(2,1)S(1)} %get-tuple-element.157.refs_1_), channel_id=1, source_target_pairs={{0,16},{1,5},{2,6},{3,19},{4,20},{5,1},{6,2},{7,23},{8,24},{9,13},... | collective-permute-start | bytes 1376264 | tf_op jit(solution)/shard_map/ppermute | solution.py:248
  80.0 11.9 %collective-permute-start.36 = (bf16[128,1792]{1,0:T(8,128)(2,1)S(1)}, bf16[128,1792]{1,0:T(8,128)(2,1)S(1)}, u32[]{:S(2)}, u32[]{:S(2)}) collective-permute-start(bf16[128,1792]{1,0:T(8,128)(2,1)S(1)} %get-tuple-element.152.refs_4_.refs_0_), channel_id=1, source_target_pairs={{0,8},{1,5},{2,6},{3,11},{4,12},{5,1},{6,2},{7,15},{8,0},{9,13},{1... | collective-permute-start | bytes 1376264 | tf_op jit(solution)/shard_map/ppermute | solution.py:248
  80.5 6.9 %collective-permute-start.30 = (bf16[64,1536]{1,0:T(8,128)(2,1)S(1)}, bf16[64,1536]{1,0:T(8,128)(2,1)S(1)}, u32[]{:S(2)}, u32[]{:S(2)}) collective-permute-start(bf16[64,1536]{1,0:T(8,128)(2,1)S(1)} %get-tuple-element.149), channel_id=1, source_target_pairs={{0,4},{1,17},{2,18},{3,7},{4,0},{5,21},{6,22},{7,3},{8,12},{9,25},... | collective-permute-start | bytes 589832 | tf_op jit(solution)/shard_map/ppermute | solution.py:248
  82.0 6.6 %collective-permute-start.31 = (bf16[64,1536]{1,0:T(8,128)(2,1)S(1)}, bf16[64,1536]{1,0:T(8,128)(2,1)S(1)}, u32[]{:S(2)}, u32[]{:S(2)}) collective-permute-start(bf16[64,1536]{1,0:T(8,128)(2,1)S(1)} %get-tuple-element.150), channel_id=1, source_target_pairs={{0,4},{1,9},{2,10},{3,7},{4,0},{5,13},{6,14},{7,3},{8,12},{9,1},{1... | collective-permute-start | bytes 589832 | tf_op jit(solution)/shard_map/ppermute | solution.py:248
  92.0 8.0 %collective-permute-start.43 = (bf16[256,1792]{1,0:T(8,128)(2,1)S(1)}, bf16[256,1792]{1,0:T(8,128)(2,1)S(1)}, u32[]{:S(2)}, u32[]{:S(2)}) collective-permute-start(bf16[256,1792]{1,0:T(8,128)(2,1)S(1)} %get-tuple-element.164.refs_7_), channel_id=1, source_target_pairs={{0,4},{1,5},{2,6},{3,7},{4,0},{5,1},{6,2},{7,3},{8,12},{9,13},{10,... | collective-permute-start | bytes 2752520 | tf_op jit(solution)/shard_map/ppermute | solution.py:248
  92.5 7.5 %collective-permute-start.42 = (bf16[256,1792]{1,0:T(8,128)(2,1)S(1)}, bf16[256,1792]{1,0:T(8,128)(2,1)S(1)}, u32[]{:S(2)}, u32[]{:S(2)}) collective-permute-start(bf16[256,1792]{1,0:T(8,128)(2,1)S(1)} %get-tuple-element.158.refs_3_.refs_6_), channel_id=1, source_target_pairs={{0,4},{1,5},{2,6},{3,7},{4,0},{5,1},{6,2},{7,3},{8,12},{9,13},{10,... | collective-permute-start | bytes 2752520 | tf_op jit(solution)/shard_map/ppermute | solution.py:248
  97.2 8.4 %collective-permute-start.38 = (bf16[128,1024]{1,0:T(8,128)(2,1)S(1)}, bf16[128,1024]{1,0:T(8,128)(2,1)S(1)}, u32[]{:S(2)}, u32[]{:S(2)}) collective-permute-start(bf16[128,1024]{1,0:T(8,128)(2,1)S(1)} %get-tuple-element.161), channel_id=1, source_target_pairs={{0,4},{1,9},{2,10},{3,7},{4,0},{5,13},{6,14},{7,3},{8,12},{9,1},{1... | collective-permute-start | bytes 786440 | tf_op jit(solution)/shard_map/ppermute | solution.py:248
  98.4 8.1 %collective-permute-start.39 = (bf16[128,1024]{1,0:T(8,128)(2,1)S(1)}, bf16[128,1024]{1,0:T(8,128)(2,1)S(1)}, u32[]{:S(2)}, u32[]{:S(2)}) collective-permute-start(bf16[128,1024]{1,0:T(8,128)(2,1)S(1)} %get-tuple-element.162), channel_id=1, source_target_pairs={{0,4},{1,17},{2,18},{3,7},{4,0},{5,21},{6,22},{7,3},{8,12},{9,25},... | collective-permute-start | bytes 786440 | tf_op jit(solution)/shard_map/ppermute | solution.py:248
  113.2 7.5 %collective-permute-start.46 = (bf16[64,2560]{1,0:T(8,128)(2,1)S(1)}, bf16[64,2560]{1,0:T(8,128)(2,1)S(1)}, u32[]{:S(2)}, u32[]{:S(2)}) collective-permute-start(bf16[64,2560]{1,0:T(8,128)(2,1)S(1)} %get-tuple-element.170.refs_0_.refs_4_), channel_id=1, source_target_pairs={{0,4},{1,17},{2,18},{3,7},{4,0},{5,21},{6,22},{7,3},{8,12},{9,25},... | collective-permute-start | bytes 983048 | tf_op jit(solution)/shard_map/ppermute | solution.py:248
  113.8 7.4 %collective-permute-start.47 = (bf16[64,2560]{1,0:T(8,128)(2,1)S(1)}, bf16[64,2560]{1,0:T(8,128)(2,1)S(1)}, u32[]{:S(2)}, u32[]{:S(2)}) collective-permute-start(bf16[64,2560]{1,0:T(8,128)(2,1)S(1)} %get-tuple-element.171.refs_1_), channel_id=1, source_target_pairs={{0,4},{1,9},{2,10},{3,7},{4,0},{5,13},{6,14},{7,3},{8,12},{9,1},{1... | collective-permute-start | bytes 983048 | tf_op jit(solution)/shard_map/ppermute | solution.py:248
  121.3 13.6 %collective-permute-start.48 = (bf16[128,2560]{1,0:T(8,128)(2,1)S(1)}, bf16[128,2560]{1,0:T(8,128)(2,1)S(1)}, u32[]{:S(2)}, u32[]{:S(2)}) collective-permute-start(bf16[128,2560]{1,0:T(8,128)(2,1)S(1)} %get-tuple-element.172.refs_0_.refs_4_), channel_id=1, source_target_pairs={{0,4},{1,9},{2,10},{3,7},{4,0},{5,13},{6,14},{7,3},{8,12},{9,1},{1... | collective-permute-start | bytes 1966088 | tf_op jit(solution)/shard_map/ppermute | solution.py:248
  122.4 12.6 %collective-permute-start.49 = (bf16[128,2560]{1,0:T(8,128)(2,1)S(1)}, bf16[128,2560]{1,0:T(8,128)(2,1)S(1)}, u32[]{:S(2)}, u32[]{:S(2)}) collective-permute-start(bf16[128,2560]{1,0:T(8,128)(2,1)S(1)} %get-tuple-element.173.refs_1_), channel_id=1, source_target_pairs={{0,4},{1,17},{2,18},{3,7},{4,0},{5,21},{6,22},{7,3},{8,12},{9,25},... | collective-permute-start | bytes 1966088 | tf_op jit(solution)/shard_map/ppermute | solution.py:248
  135.7 10.8 %collective-permute-start.52 = (bf16[896,512]{1,0:T(8,128)(2,1)S(1)}, bf16[896,512]{1,0:T(8,128)(2,1)S(1)}, u32[]{:S(2)}, u32[]{:S(2)}) collective-permute-start(bf16[896,512]{1,0:T(8,128)(2,1)S(1)} %update.4.refs_4_), channel_id=1, source_target_pairs={{0,3},{1,5},{2,6},{3,0},{4,7},{5,1},{6,2},{7,4},{8,11},{9,13},{10,... | collective-permute-start | bytes 2752520 | tf_op jit(solution)/shard_map/ppermute | solution.py:254
  144.5 27.3 %collective-permute-start.55 = (bf16[896,512]{1,0:T(8,128)(2,1)S(1)}, bf16[896,512]{1,0:T(8,128)(2,1)S(1)}, u32[]{:S(2)}, u32[]{:S(2)}) collective-permute-start(bf16[896,512]{1,0:T(8,128)(2,1)S(1)} %get-tuple-element.180), channel_id=1, source_target_pairs={{0,1},{1,3},{2,0},{3,2},{4,5},{5,7},{6,4},{7,6},{8,9},{9,11},{10,8... | collective-permute-start | bytes 2752520 | tf_op jit(solution)/shard_map/ppermute | solution.py:254
  144.5 46.4 %collective-permute-start.54 = (bf16[896,512]{1,0:T(8,128)(2,1)S(1)}, bf16[896,512]{1,0:T(8,128)(2,1)S(1)}, u32[]{:S(2)}, u32[]{:S(2)}) collective-permute-start(bf16[896,512]{1,0:T(8,128)(2,1)S(1)} %get-tuple-element.178.refs_8_), channel_id=1, source_target_pairs={{0,2},{1,0},{2,3},{3,1},{4,6},{5,4},{6,7},{7,5},{8,10},{9,8},{10,1... | collective-permute-start | bytes 2752520 | tf_op jit(solution)/shard_map/ppermute | solution.py:254
  150.8 59.7 %collective-permute-start.53 = (bf16[896,512]{1,0:T(8,128)(2,1)S(1)}, bf16[896,512]{1,0:T(8,128)(2,1)S(1)}, u32[]{:S(2)}, u32[]{:S(2)}) collective-permute-start(bf16[896,512]{1,0:T(8,128)(2,1)S(1)} %get-tuple-element.179.refs_2_), channel_id=1, source_target_pairs={{0,4},{1,2},{2,1},{3,7},{4,0},{5,6},{6,5},{7,3},{8,12},{9,10},{10,... | collective-permute-start | bytes 2752520 | tf_op jit(solution)/shard_map/ppermute | solution.py:254
  (36 other events, 116.3 us)

commit v6 on v5

--- a/solution.py
+++ b/solution.py
@@ -12,8 +12,6 @@
 coef_linear = 3.4445
 coef_cubic = -4.775
 
-CHUNKS = 2, 2
-
 MIB = 2**20
 F32, BF16 = jnp.float32, jnp.bfloat16
 ANY = pl.BlockSpec(memory_space=pl.ANY)
@@ -25,7 +23,7 @@
     levels = fsdp.bit_length() - 2
     if loop == 4 and levels == 2:
         phases = [[[1, 3, 0, 2]], [[2, 0, 3, 1]], [[3, 1, 2, 0]], [[0, 2, 1, 3]]]
-        waves = [({0: 0, 3: 3}, [[0], [1], [2]], [[0], [1, 2]], {}), ({1: 1, 2: 2}, [[0, 1], [3]], [[0, 1]], {})]
+        waves = [({0: 0, 3: 3}, [[0], [1], [2]], [[0], [1, 2]], (2, 2)), ({1: 1, 2: 2}, [[0, 1], [3]], [[0, 1]], (2, 4))]
         order = [
             "0pick00", "0send0", "0pick13", "0send1", "0gram0", "0split0", "0add00", "0add01", "0send2", "0gram1",
             "0split1", "0join00", "0add10", "0join01", "0add11", "0gram2", "0send3", "0split2", "1gram0", "0add20",
@@ -39,7 +37,7 @@
     turns = [(0, "pick", [0, 0]), (0, "send", [0]), (0, "gram", [0]), (0, "split", [0])]
     turns += [(0, step, [0, i]) for step in ("add", "join") for i in range(levels)]
     turns += [(0, "update", list(range(loop))), (0, "place", [i for b in range(loop) for i in (0, b)])]
-    return [rounds], [({p: p for p in range(loop)}, [list(range(len(rounds)))], [[0]], {})], {}, turns
+    return [rounds], [({p: p for p in range(loop)}, [list(range(len(rounds)))], [[0]], (4, 4))], {}, turns
 
 
 def sends(owners, step):
@@ -254,29 +252,23 @@
     return lax.ppermute(value, ("fsdp", "loop"), pairs)
 
 
-def update_blocks(blocks, places, own, other, wanted, pieces, instead, owners, after):
+def update_blocks(blocks, places, own, other, wanted, instead, owners, after):
     rows, width = blocks[0].shape
     half, count = width // 2, len(blocks)
     total, chunks = count * width, len(own)
     factor = 0.2 * D**0.5
-    parts = []
-    for b in wanted:
-        weights, row = pieces.get(b, (1,)), 0
-        for weight in weights:
-            parts.append((b, row, rows * weight // sum(weights)))
-            row += parts[-1][2]
 
     def kernel(*refs):
         xs, strips = refs[:count], (refs[count : count + chunks], refs[count + chunks : count + 2 * chunks])
         refs = refs[count + 2 * chunks :]
         given, refs = refs[: len(instead)], refs[len(instead) :]
-        outs, (x, g) = refs[: len(parts)], refs[len(parts) :]
+        outs, (x, g) = refs[: len(wanted)], refs[len(wanted) :]
         mine = is_one_of(owners)
         pl.when(mine)(lambda: multiply(xs, strips, outs, x, g))
         for b, value in zip(instead, given):
 
             @pl.when(jnp.logical_not(mine))
-            def _(out=outs[parts.index((b, 0, rows))], value=value):
+            def _(out=outs[wanted.index(b)], value=value):
                 out[...] = value[...]
 
     def multiply(xs, strips, outs, x, g):
@@ -291,43 +283,35 @@
                 for chunk, offset, first, size in pieces:
                     at = b * width + first
                     g[where, at : at + size] = strip[chunk][:, offset : offset + size]
-        for b in wanted:
+        for out, b in zip(outs, wanted):
             low, high = b * width, (b + 1) * width
             product = jnp.dot(x[:, :high], g[:high, low:high], preferred_element_type=F32)
             if b < count - 1:
                 product += lax.dot_general(
                     x[:, high:], g[low:high, high:], (((1,), (1,)), ((), ())), preferred_element_type=F32
                 )
-            result = (factor * (coef_linear * x[:, low:high].astype(F32) + coef_cubic * product)).astype(BF16)
-            for out, (block, row, height) in zip(outs, parts):
-                if block == b:
-                    out[...] = result[row : row + height]
+            out[...] = (factor * (coef_linear * x[:, low:high].astype(F32) + coef_cubic * product)).astype(BF16)
 
     scratch = [pltpu.VMEM((rows, total), BF16), pltpu.VMEM((total, total), BF16)]
-    outs = [struct((height, width), BF16) for _, _, height in parts]
+    outs = [struct((rows, width), BF16)] * len(wanted)
     ins = [*blocks, *own, *other, *instead.values()]
     return call(kernel, "update", ins, [VMEM] * len(ins), outs, 30, scratch, after)
 
 
 def place_slots(out, found, like, after):
     old = [] if out is None else [out]
-    ins, cases = [], []
-    for values, table in found:
-        row = 0
-        for value in values:
-            cases += [(len(ins), place, slot, pl.ds(row, value.shape[0])) for place, slot in table.items()]
-            ins.append(value)
-            row += value.shape[0]
+    ins = [value for value, _ in found]
+    cases = [(i, place, slot) for i, (_, table) in enumerate(found) for place, slot in table.items()]
 
     def kernel(*refs):
         values, target, sems = refs[: len(ins)], refs[-2], refs[-1]
         here = lax.axis_index("loop")
         for wait in (False, True):
-            for i, place, slot, rows in cases:
+            for i, place, slot in cases:
 
                 @pl.when(here == place)
-                def _(i=i, slot=slot, rows=rows):
-                    copy = pltpu.make_async_copy(values[i], target.at[slot, rows], sems.at[i])
+                def _(i=i, slot=slot):
+                    copy = pltpu.make_async_copy(values[i], target.at[slot], sems.at[i])
                     copy.wait() if wait else copy.start()
 
     return pl.pallas_call(
@@ -379,7 +363,7 @@
 
 
 class Wave:
-    def __init__(self, columns, owners, groups, gathers, pieces, shares, loop, chunks):
+    def __init__(self, columns, owners, groups, gathers, chunks, loop):
         self.columns, self.owners, self.loop, self.chunks = columns, owners, loop, chunks
         self.fsdp = columns.fsdp
         self.bits = [1 << i for i in range(1, self.fsdp.bit_length() - 1)]
@@ -390,7 +374,7 @@
             count = first + len(group) + 1
             self.groups.append([(a, b) for b in range(first + 1 if first else 0, count) for a in range(b + 1)])
             first += len(group)
-        self.updates, self.shares, self.pieces = {b: [] for b in pieces}, shares, pieces
+        self.updates, self.shares = {}, {}
 
     def blocks(self, count):
         return [self.columns.own] + [self.columns.arrived[number] for number in self.rounds[: count - 1]]
@@ -454,10 +438,10 @@
         own, other = ([v for i in range(len(self.gathers)) for v in self.gathered[i][core]] for core in range(2))
         instead = {b: self.shares[b][0].updates[self.shares[b][1]] for b in wanted if self.shares.get(b)}
         values = update_blocks(
-            blocks, self.places(), own, other, wanted, self.pieces, instead, self.owners, self.columns.last
+            blocks, self.places(), own, other, wanted, instead, self.owners, self.columns.last
         )
         self.columns.last = values[:1]
-        for b, value in zip([b for b in wanted for _ in self.pieces.get(b, (1,))], values):
+        for b, value in zip(wanted, values):
             if b and b not in self.shares or b in instead:
                 returns = [self.returned(b)]
                 if b in instead:
@@ -466,23 +450,22 @@
             if b in instead:
                 wave, block = self.shares[b]
                 wave.updates[block] = value
-            self.updates[b] = self.updates[b] + [value] if b in self.pieces else value
+            self.updates[b] = value
 
     def need(self, b):
-        self.columns.last = self.columns.last + self.found(b)[0]
+        self.columns.last = self.columns.last + [self.updates[b]]
 
     def returned(self, b):
         return self.owners, self.columns.rounds[self.rounds[b - 1]]
 
     def found(self, b):
-        value = self.updates[b]
-        return value if isinstance(value, list) else [value], sends(*self.returned(b)) if b else self.owners
+        return self.updates[b], sends(*self.returned(b)) if b else self.owners
 
 
 def body(iterate, expert_order, fsdp, loop):
     phases, waves, shares, turns = plan(loop, fsdp)
     columns = Columns(iterate, expert_order, phases, fsdp)
-    waves = [Wave(columns, *wave, {}, loop, CHUNKS) for wave in waves]
+    waves = [Wave(columns, *wave, loop) for wave in waves]
     for (wave, block), (other, given) in shares.items():
         waves[wave].shares[block] = waves[other], given
         waves[other].shares[given] = None

time: 212 us -> 209 us (0.986)
  waiting for transfers between devices: 151 us -> 147 us
    ppermute x8, waiting for transfers between devices: 87.4 us -> 84.1 us  [shift(): return lax.ppermute(value, ('fsdp', 'loop'), pairs)]
    ppermute x48 -> x50, starting transfers between devices: 23.6 us -> 24.2 us  [swap(): return lax.ppermute(value, ('fsdp', 'loop'), pairs)]
    ppermute x48 -> x50, waiting for transfers between devices: 63.8 us -> 63.4 us  [swap(): return lax.ppermute(value, ('fsdp', 'loop'), pairs)]
  transfers between devices with their start and end apart: 56 -> 58, of which waited for: 40 -> 42; matrix products, arithmetic and copies ran while one was open for 0% -> 0% of each run, Pallas kernels for 7% -> 7%
where the time goes in v6:
time: 209 us; the launch traced here: 208 us
  waiting for transfers between devices  147 us (70%)
  starting transfers between devices  33.2 us (16%)
  Pallas kernels  23.9 us (11%)
  local copies, waits for them, and re-layouts  3.22 us (2%)
    ppermute x8, waiting for transfers between devices, shift(): return lax.ppermute(value, ('fsdp', 'loop'), pairs)  84.1 us
    ppermute x50, waiting for transfers between devices, swap(): return lax.ppermute(value, ('fsdp', 'loop'), pairs)  63.4 us
    ppermute x50, starting transfers between devices, swap(): return lax.ppermute(value, ('fsdp', 'loop'), pairs)  24.2 us
    pallas_call x32, Pallas kernels, call(): pl.pallas_call(wrapped, out_shape=outs, in_specs=list(specs) + [ANY] * ex...  21.4 us
    ppermute x8, starting transfers between devices, shift(): return lax.ppermute(value, ('fsdp', 'loop'), pairs)  9.08 us
  transfers between devices with their start and end apart: 58, of which 42 were waited for; matrix products, arithmetic and copies ran while one was open for 0% of the time, Pallas kernels for 7%

profile of v6, /device:TPU:8, one launch (start us, length us, event | category | flops | bytes accessed | tf_op | source)
XLA Modules:
  0.0 208.3 jit_solution(12665276143005697612)
XLA Ops:
  0.0 3.5 %pick.2 = (bf16[896,512]{1,0:T(8,128)(2,1)}, bf16[896,512]{1,0:T(8,128)(2,1)}) custom-call(s32[4]{0:T(128)} %refs_0_.3, bf16[4,896,512]{2,1,0:T(8,128)(2,1)} %refs_1_.3), custom_call_target="tpu_custom_call" | custom-call | bytes 1 | tf_op jit(solution)/shard_map/pick/pallas_call | solution.py:65
  3.5 2.6 %collective-permute-start = (bf16[896,512]{1,0:T(8,128)(2,1)}, bf16[896,512]{1,0:T(8,128)(2,1)S(1)}, u32[]{:S(2)}, u32[]{:S(2)}) collective-permute-start(bf16[896,512]{1,0:T(8,128)(2,1)} %get-tuple-element.97.refs_2_), channel_id=1, source_target_pairs={{0,1},{1,3},{2,0},{3,2},{4,5},{5,7},{6,4},{7,6},{8,9},{9,11},{10,8... | collective-permute-start | bytes 2752520 | tf_op jit(solution)/shard_map/ppermute | solution.py:252
  6.2 2.0 copy-done.1
  10.7 15.4 %collective-permute-done.refs_2_.refs_1_ = bf16[896,512]{1,0:T(8,128)(2,1)S(1)} collective-permute-done((bf16[896,512]{1,0:T(8,128)(2,1)}, bf16[896,512]{1,0:T(8,128)(2,1)S(1)}, u32[]{:S(2)}, u32[]{:S(2)}) %collective-permute-start) | collective-permute-done | bytes 917536 | tf_op jit(solution)/shard_map/ppermute | solution.py:252
  33.1 15.8 %collective-permute-done.1.refs_2_ = bf16[896,512]{1,0:T(8,128)(2,1)S(1)} collective-permute-done((bf16[896,512]{1,0:T(8,128)(2,1)S(1)}, bf16[896,512]{1,0:T(8,128)(2,1)S(1)}, u32[]{:S(2)}, u32[]{:S(2)}) %collective-permute-start.1) | collective-permute-done | bytes 917536 | tf_op jit(solution)/shard_map/ppermute | solution.py:252
  49.9 2.0 collective-permute-done.9.refs_1_
  59.0 3.5 %gram_part.8 = (f32[256,3072]{1,0:T(8,128)S(1)}, bf16[256,1536]{1,0:T(8,128)(2,1)S(1)}, bf16[256,1536]{1,0:T(8,128)(2,1)S(1)}) custom-call(bf16[896,512]{1,0:T(8,128)(2,1)S(1)} %copy-done, bf16[896,512]{1,0:T(8,128)(2,1)S(1)} %collective-permute-done.refs_2_.refs_1_, bf16[896,512]{1,0:T(8,128)(2,1)S(1)} %collective-permute-done.1.refs_2_, ...), custom_call_target="tpu_custom_call" | custom-call | bytes 1 | tf_op jit(solution)/shard_map/gram_part/pallas_call | solution.py:65
  64.3 2.0 collective-permute-done.24.refs_2_
  72.4 6.1 %collective-permute-done.26.refs_2_ = bf16[128,1536]{1,0:T(8,128)(2,1)S(1)} collective-permute-done((bf16[128,1536]{1,0:T(8,128)(2,1)S(1)}, bf16[128,1536]{1,0:T(8,128)(2,1)S(1)}, u32[]{:S(2)}, u32[]{:S(2)}) %collective-permute-start.26) | collective-permute-done | bytes 393248 | tf_op jit(solution)/shard_map/ppermute | solution.py:246
  82.5 4.8 %collective-permute-done.30.refs_2_ = bf16[64,1536]{1,0:T(8,128)(2,1)S(1)} collective-permute-done((bf16[64,1536]{1,0:T(8,128)(2,1)S(1)}, bf16[64,1536]{1,0:T(8,128)(2,1)S(1)}, u32[]{:S(2)}, u32[]{:S(2)}) %collective-permute-start.30) | collective-permute-done | bytes 196640 | tf_op jit(solution)/shard_map/ppermute | solution.py:246
  89.3 2.4 %gram_part.9 = (f32[256,2048]{1,0:T(8,128)S(1)}, bf16[256,1024]{1,0:T(8,128)(2,1)S(1)}, bf16[256,1024]{1,0:T(8,128)(2,1)S(1)}) custom-call(bf16[896,512]{1,0:T(8,128)(2,1)S(1)} %copy-done, bf16[896,512]{1,0:T(8,128)(2,1)S(1)} %collective-permute-done.refs_2_.refs_1_, bf16[896,512]{1,0:T(8,128)(2,1)S(1)} %collective-permute-done.1.refs_2_, ...), custom_call_target="tpu_custom_call" | custom-call | bytes 1 | tf_op jit(solution)/shard_map/gram_part/pallas_call | solution.py:65
  93.8 3.2 %collective-permute-done.35.refs_2_ = bf16[256,1024]{1,0:T(8,128)(2,1)S(1)} collective-permute-done((bf16[256,1024]{1,0:T(8,128)(2,1)S(1)}, bf16[256,1024]{1,0:T(8,128)(2,1)S(1)}, u32[]{:S(2)}, u32[]{:S(2)}) %collective-permute-start.35) | collective-permute-done | bytes 524320 | tf_op jit(solution)/shard_map/ppermute | solution.py:246
  100.0 5.6 %collective-permute-done.38.refs_2_ = bf16[128,1024]{1,0:T(8,128)(2,1)S(1)} collective-permute-done((bf16[128,1024]{1,0:T(8,128)(2,1)S(1)}, bf16[128,1024]{1,0:T(8,128)(2,1)S(1)}, u32[]{:S(2)}, u32[]{:S(2)}) %collective-permute-start.38) | collective-permute-done | bytes 262176 | tf_op jit(solution)/shard_map/ppermute | solution.py:246
  106.6 1.6 collective-permute-start.44
  108.8 2.8 %collective-permute-done.44.refs_2_ = bf16[64,1024]{1,0:T(8,128)(2,1)S(1)} collective-permute-done((bf16[64,1024]{1,0:T(8,128)(2,1)S(1)}, bf16[64,1024]{1,0:T(8,128)(2,1)S(1)}, u32[]{:S(2)}, u32[]{:S(2)}) %collective-permute-start.44) | collective-permute-done | bytes 131104 | tf_op jit(solution)/shard_map/ppermute | solution.py:246
  114.7 6.1 %collective-permute-done.46.refs_2_ = bf16[64,2560]{1,0:T(8,128)(2,1)S(1)} collective-permute-done((bf16[64,2560]{1,0:T(8,128)(2,1)S(1)}, bf16[64,2560]{1,0:T(8,128)(2,1)S(1)}, u32[]{:S(2)}, u32[]{:S(2)}) %collective-permute-start.46) | collective-permute-done | bytes 327712 | tf_op jit(solution)/shard_map/ppermute | solution.py:246
  123.8 11.1 %collective-permute-done.48.refs_2_ = bf16[128,2560]{1,0:T(8,128)(2,1)S(1)} collective-permute-done((bf16[128,2560]{1,0:T(8,128)(2,1)S(1)}, bf16[128,2560]{1,0:T(8,128)(2,1)S(1)}, u32[]{:S(2)}, u32[]{:S(2)}) %collective-permute-start.48) | collective-permute-done | bytes 655392 | tf_op jit(solution)/shard_map/ppermute | solution.py:246
  140.2 4.3 %update.6 = (bf16[896,512]{1,0:T(8,128)(2,1)S(1)}, bf16[896,512]{1,0:T(8,128)(2,1)S(1)}) custom-call(bf16[896,512]{1,0:T(8,128)(2,1)S(1)} %copy-done, bf16[896,512]{1,0:T(8,128)(2,1)S(1)} %collective-permute-done.refs_2_.refs_1_, bf16[896,512]{1,0:T(8,128)(2,1)S(1)} %collective-permute-done.1.refs_2_, bf16[896,512]{1,0:T(8,128)(2,1)S(1)} %collective-permute-done.19.refs_3_, ...), custom_call_target="tpu_custom_call" | custom-call | bytes 1 | tf_op jit(solution)/shard_map/update/pallas_call | solution.py:65
  144.6 2.0 collective-permute-start.56
  146.6 4.3 %update.7 = (bf16[896,512]{1,0:T(8,128)(2,1)S(1)}, bf16[896,512]{1,0:T(8,128)(2,1)S(1)}) custom-call(bf16[896,512]{1,0:T(8,128)(2,1)S(1)} %copy-done, bf16[896,512]{1,0:T(8,128)(2,1)S(1)} %collective-permute-done.refs_2_.refs_1_, bf16[896,512]{1,0:T(8,128)(2,1)S(1)} %collective-permute-done.1.refs_2_, bf16[896,512]{1,0:T(8,128)(2,1)S(1)} %collective-permute-done.19.refs_3_, ...), custom_call_target="tpu_custom_call" | custom-call | bytes 1 | tf_op jit(solution)/shard_map/update/pallas_call | solution.py:65
  150.9 2.5 %collective-permute-start.55 = (bf16[896,512]{1,0:T(8,128)(2,1)S(1)}, bf16[896,512]{1,0:T(8,128)(2,1)S(1)}, u32[]{:S(2)}, u32[]{:S(2)}) collective-permute-start(bf16[896,512]{1,0:T(8,128)(2,1)S(1)} %get-tuple-element.183.refs_2_), channel_id=1, source_target_pairs={{0,4},{1,2},{2,1},{3,7},{4,0},{5,6},{6,5},{7,3},{8,12},{9,10},{10,... | collective-permute-start | bytes 2752520 | tf_op jit(solution)/shard_map/ppermute | solution.py:252
  153.4 15.1 %collective-permute-done.57.refs_1_.refs_4_ = bf16[896,512]{1,0:T(8,128)(2,1)S(1)} collective-permute-done((bf16[896,512]{1,0:T(8,128)(2,1)S(1)}, bf16[896,512]{1,0:T(8,128)(2,1)S(1)}, u32[]{:S(2)}, u32[]{:S(2)}) %collective-permute-start.57) | collective-permute-done | bytes 917536 | tf_op jit(solution)/shard_map/ppermute | solution.py:252
  168.5 20.2 %collective-permute-done.56.refs_0_.refs_3_ = bf16[896,512]{1,0:T(8,128)(2,1)S(1)} collective-permute-done((bf16[896,512]{1,0:T(8,128)(2,1)S(1)}, bf16[896,512]{1,0:T(8,128)(2,1)S(1)}, u32[]{:S(2)}, u32[]{:S(2)}) %collective-permute-start.56) | collective-permute-done | bytes 917536 | tf_op jit(solution)/shard_map/ppermute | solution.py:252
  190.2 17.0 %collective-permute-done.55.refs_0_ = bf16[896,512]{1,0:T(8,128)(2,1)S(1)} collective-permute-done((bf16[896,512]{1,0:T(8,128)(2,1)S(1)}, bf16[896,512]{1,0:T(8,128)(2,1)S(1)}, u32[]{:S(2)}, u32[]{:S(2)}) %collective-permute-start.55) | collective-permute-done | bytes 917536 | tf_op jit(solution)/shard_map/ppermute | solution.py:252
  (138 shorter events, 51.8 us)
Async XLA Ops:
  3.5 22.6 %collective-permute-start = (bf16[896,512]{1,0:T(8,128)(2,1)}, bf16[896,512]{1,0:T(8,128)(2,1)S(1)}, u32[]{:S(2)}, u32[]{:S(2)}) collective-permute-start(bf16[896,512]{1,0:T(8,128)(2,1)} %get-tuple-element.97.refs_2_), channel_id=1, source_target_pairs={{0,1},{1,3},{2,0},{3,2},{4,5},{5,7},{6,4},{7,6},{8,9},{9,11},{10,8... | collective-permute-start | bytes 2752520 | tf_op jit(solution)/shard_map/ppermute | solution.py:252
  26.1 22.8 %collective-permute-start.1 = (bf16[896,512]{1,0:T(8,128)(2,1)S(1)}, bf16[896,512]{1,0:T(8,128)(2,1)S(1)}, u32[]{:S(2)}, u32[]{:S(2)}) collective-permute-start(bf16[896,512]{1,0:T(8,128)(2,1)S(1)} %gate.3.refs_2_), channel_id=1, source_target_pairs={{0,2},{1,0},{2,3},{3,1},{4,6},{5,4},{6,7},{7,5},{8,10},{9,8},{10,1... | collective-permute-start | bytes 2752520 | tf_op jit(solution)/shard_map/ppermute | solution.py:252
  48.9 7.2 %collective-permute-start.8 = (bf16[896,512]{1,0:T(8,128)(2,1)S(1)}, bf16[896,512]{1,0:T(8,128)(2,1)S(1)}, u32[]{:S(2)}, u32[]{:S(2)}) collective-permute-start(bf16[896,512]{1,0:T(8,128)(2,1)S(1)} %gate.4.refs_3_), channel_id=1, source_target_pairs={{0,3},{1,5},{2,6},{3,0},{4,7},{5,1},{6,2},{7,4},{8,11},{9,13},{10,... | collective-permute-start | bytes 2752520 | tf_op jit(solution)/shard_map/ppermute | solution.py:252
  63.6 25.8 %collective-permute-start.19 = (bf16[896,512]{1,0:T(8,128)(2,1)S(1)}, bf16[896,512]{1,0:T(8,128)(2,1)S(1)}, u32[]{:S(2)}, u32[]{:S(2)}) collective-permute-start(bf16[896,512]{1,0:T(8,128)(2,1)S(1)} %gate.5.refs_3_), channel_id=1, source_target_pairs={{0,4},{1,2},{2,1},{3,7},{4,0},{5,6},{6,5},{7,3},{8,12},{9,10},{10,... | collective-permute-start | bytes 2752520 | tf_op jit(solution)/shard_map/ppermute | solution.py:252
  67.1 11.4 %collective-permute-start.26 = (bf16[128,1536]{1,0:T(8,128)(2,1)S(1)}, bf16[128,1536]{1,0:T(8,128)(2,1)S(1)}, u32[]{:S(2)}, u32[]{:S(2)}) collective-permute-start(bf16[128,1536]{1,0:T(8,128)(2,1)S(1)} %get-tuple-element.142), channel_id=1, source_target_pairs={{0,4},{1,9},{2,10},{3,7},{4,0},{5,13},{6,14},{7,3},{8,12},{9,1},{1... | collective-permute-start | bytes 1179656 | tf_op jit(solution)/shard_map/ppermute | solution.py:246
  68.7 11.0 %collective-permute-start.27 = (bf16[128,1536]{1,0:T(8,128)(2,1)S(1)}, bf16[128,1536]{1,0:T(8,128)(2,1)S(1)}, u32[]{:S(2)}, u32[]{:S(2)}) collective-permute-start(bf16[128,1536]{1,0:T(8,128)(2,1)S(1)} %get-tuple-element.143), channel_id=1, source_target_pairs={{0,4},{1,17},{2,18},{3,7},{4,0},{5,21},{6,22},{7,3},{8,12},{9,25},... | collective-permute-start | bytes 1179656 | tf_op jit(solution)/shard_map/ppermute | solution.py:246
  71.8 8.0 %collective-permute-start.33 = (bf16[64,1792]{1,0:T(8,128)(2,1)S(1)}, bf16[64,1792]{1,0:T(8,128)(2,1)S(1)}, u32[]{:S(2)}, u32[]{:S(2)}) collective-permute-start(bf16[64,1792]{1,0:T(8,128)(2,1)S(1)} %get-tuple-element.153.refs_1_), channel_id=1, source_target_pairs={{0,8},{1,5},{2,6},{3,11},{4,12},{5,1},{6,2},{7,15},{8,0},{9,13},{1... | collective-permute-start | bytes 688136 | tf_op jit(solution)/shard_map/ppermute | solution.py:246
  72.2 7.6 %collective-permute-start.32 = (bf16[64,1792]{1,0:T(8,128)(2,1)S(1)}, bf16[64,1792]{1,0:T(8,128)(2,1)S(1)}, u32[]{:S(2)}, u32[]{:S(2)}) collective-permute-start(bf16[64,1792]{1,0:T(8,128)(2,1)S(1)} %get-tuple-element.148.refs_4_.refs_0_), channel_id=1, source_target_pairs={{0,16},{1,5},{2,6},{3,19},{4,20},{5,1},{6,2},{7,23},{8,24},{9,13},... | collective-permute-start | bytes 688136 | tf_op jit(solution)/shard_map/ppermute | solution.py:246
  79.9 11.9 %collective-permute-start.37 = (bf16[128,1792]{1,0:T(8,128)(2,1)S(1)}, bf16[128,1792]{1,0:T(8,128)(2,1)S(1)}, u32[]{:S(2)}, u32[]{:S(2)}) collective-permute-start(bf16[128,1792]{1,0:T(8,128)(2,1)S(1)} %get-tuple-element.159.refs_1_), channel_id=1, source_target_pairs={{0,16},{1,5},{2,6},{3,19},{4,20},{5,1},{6,2},{7,23},{8,24},{9,13},... | collective-permute-start | bytes 1376264 | tf_op jit(solution)/shard_map/ppermute | solution.py:246
  80.0 11.9 %collective-permute-start.36 = (bf16[128,1792]{1,0:T(8,128)(2,1)S(1)}, bf16[128,1792]{1,0:T(8,128)(2,1)S(1)}, u32[]{:S(2)}, u32[]{:S(2)}) collective-permute-start(bf16[128,1792]{1,0:T(8,128)(2,1)S(1)} %get-tuple-element.154.refs_4_.refs_0_), channel_id=1, source_target_pairs={{0,8},{1,5},{2,6},{3,11},{4,12},{5,1},{6,2},{7,15},{8,0},{9,13},{1... | collective-permute-start | bytes 1376264 | tf_op jit(solution)/shard_map/ppermute | solution.py:246
  80.5 6.9 %collective-permute-start.30 = (bf16[64,1536]{1,0:T(8,128)(2,1)S(1)}, bf16[64,1536]{1,0:T(8,128)(2,1)S(1)}, u32[]{:S(2)}, u32[]{:S(2)}) collective-permute-start(bf16[64,1536]{1,0:T(8,128)(2,1)S(1)} %get-tuple-element.151), channel_id=1, source_target_pairs={{0,4},{1,17},{2,18},{3,7},{4,0},{5,21},{6,22},{7,3},{8,12},{9,25},... | collective-permute-start | bytes 589832 | tf_op jit(solution)/shard_map/ppermute | solution.py:246
  82.0 6.6 %collective-permute-start.31 = (bf16[64,1536]{1,0:T(8,128)(2,1)S(1)}, bf16[64,1536]{1,0:T(8,128)(2,1)S(1)}, u32[]{:S(2)}, u32[]{:S(2)}) collective-permute-start(bf16[64,1536]{1,0:T(8,128)(2,1)S(1)} %get-tuple-element.152), channel_id=1, source_target_pairs={{0,4},{1,9},{2,10},{3,7},{4,0},{5,13},{6,14},{7,3},{8,12},{9,1},{1... | collective-permute-start | bytes 589832 | tf_op jit(solution)/shard_map/ppermute | solution.py:246
  92.0 8.0 %collective-permute-start.43 = (bf16[256,1792]{1,0:T(8,128)(2,1)S(1)}, bf16[256,1792]{1,0:T(8,128)(2,1)S(1)}, u32[]{:S(2)}, u32[]{:S(2)}) collective-permute-start(bf16[256,1792]{1,0:T(8,128)(2,1)S(1)} %get-tuple-element.166.refs_7_), channel_id=1, source_target_pairs={{0,4},{1,5},{2,6},{3,7},{4,0},{5,1},{6,2},{7,3},{8,12},{9,13},{10,... | collective-permute-start | bytes 2752520 | tf_op jit(solution)/shard_map/ppermute | solution.py:246
  92.5 7.5 %collective-permute-start.42 = (bf16[256,1792]{1,0:T(8,128)(2,1)S(1)}, bf16[256,1792]{1,0:T(8,128)(2,1)S(1)}, u32[]{:S(2)}, u32[]{:S(2)}) collective-permute-start(bf16[256,1792]{1,0:T(8,128)(2,1)S(1)} %get-tuple-element.160.refs_3_.refs_6_), channel_id=1, source_target_pairs={{0,4},{1,5},{2,6},{3,7},{4,0},{5,1},{6,2},{7,3},{8,12},{9,13},{10,... | collective-permute-start | bytes 2752520 | tf_op jit(solution)/shard_map/ppermute | solution.py:246
  97.3 8.4 %collective-permute-start.38 = (bf16[128,1024]{1,0:T(8,128)(2,1)S(1)}, bf16[128,1024]{1,0:T(8,128)(2,1)S(1)}, u32[]{:S(2)}, u32[]{:S(2)}) collective-permute-start(bf16[128,1024]{1,0:T(8,128)(2,1)S(1)} %get-tuple-element.163), channel_id=1, source_target_pairs={{0,4},{1,9},{2,10},{3,7},{4,0},{5,13},{6,14},{7,3},{8,12},{9,1},{1... | collective-permute-start | bytes 786440 | tf_op jit(solution)/shard_map/ppermute | solution.py:246
  98.5 8.1 %collective-permute-start.39 = (bf16[128,1024]{1,0:T(8,128)(2,1)S(1)}, bf16[128,1024]{1,0:T(8,128)(2,1)S(1)}, u32[]{:S(2)}, u32[]{:S(2)}) collective-permute-start(bf16[128,1024]{1,0:T(8,128)(2,1)S(1)} %get-tuple-element.164), channel_id=1, source_target_pairs={{0,4},{1,17},{2,18},{3,7},{4,0},{5,21},{6,22},{7,3},{8,12},{9,25},... | collective-permute-start | bytes 786440 | tf_op jit(solution)/shard_map/ppermute | solution.py:246
  113.2 7.5 %collective-permute-start.46 = (bf16[64,2560]{1,0:T(8,128)(2,1)S(1)}, bf16[64,2560]{1,0:T(8,128)(2,1)S(1)}, u32[]{:S(2)}, u32[]{:S(2)}) collective-permute-start(bf16[64,2560]{1,0:T(8,128)(2,1)S(1)} %get-tuple-element.172.refs_0_.refs_4_), channel_id=1, source_target_pairs={{0,4},{1,17},{2,18},{3,7},{4,0},{5,21},{6,22},{7,3},{8,12},{9,25},... | collective-permute-start | bytes 983048 | tf_op jit(solution)/shard_map/ppermute | solution.py:246
  113.8 7.4 %collective-permute-start.47 = (bf16[64,2560]{1,0:T(8,128)(2,1)S(1)}, bf16[64,2560]{1,0:T(8,128)(2,1)S(1)}, u32[]{:S(2)}, u32[]{:S(2)}) collective-permute-start(bf16[64,2560]{1,0:T(8,128)(2,1)S(1)} %get-tuple-element.173.refs_1_), channel_id=1, source_target_pairs={{0,4},{1,9},{2,10},{3,7},{4,0},{5,13},{6,14},{7,3},{8,12},{9,1},{1... | collective-permute-start | bytes 983048 | tf_op jit(solution)/shard_map/ppermute | solution.py:246
  121.3 13.6 %collective-permute-start.48 = (bf16[128,2560]{1,0:T(8,128)(2,1)S(1)}, bf16[128,2560]{1,0:T(8,128)(2,1)S(1)}, u32[]{:S(2)}, u32[]{:S(2)}) collective-permute-start(bf16[128,2560]{1,0:T(8,128)(2,1)S(1)} %get-tuple-element.174.refs_0_.refs_4_), channel_id=1, source_target_pairs={{0,4},{1,9},{2,10},{3,7},{4,0},{5,13},{6,14},{7,3},{8,12},{9,1},{1... | collective-permute-start | bytes 1966088 | tf_op jit(solution)/shard_map/ppermute | solution.py:246
  122.4 12.6 %collective-permute-start.49 = (bf16[128,2560]{1,0:T(8,128)(2,1)S(1)}, bf16[128,2560]{1,0:T(8,128)(2,1)S(1)}, u32[]{:S(2)}, u32[]{:S(2)}) collective-permute-start(bf16[128,2560]{1,0:T(8,128)(2,1)S(1)} %get-tuple-element.175.refs_1_), channel_id=1, source_target_pairs={{0,4},{1,17},{2,18},{3,7},{4,0},{5,21},{6,22},{7,3},{8,12},{9,25},... | collective-permute-start | bytes 1966088 | tf_op jit(solution)/shard_map/ppermute | solution.py:246
  123.8 22.8 %collective-permute-start.54 = (bf16[896,512]{1,0:T(8,128)(2,1)S(1)}, bf16[896,512]{1,0:T(8,128)(2,1)S(1)}, u32[]{:S(2)}, u32[]{:S(2)}) collective-permute-start(bf16[896,512]{1,0:T(8,128)(2,1)S(1)} %update.4.refs_4_), channel_id=1, source_target_pairs={{0,3},{1,5},{2,6},{3,0},{4,7},{5,1},{6,2},{7,4},{8,11},{9,13},{10,... | collective-permute-start | bytes 2752520 | tf_op jit(solution)/shard_map/ppermute | solution.py:252
  144.5 24.0 %collective-permute-start.57 = (bf16[896,512]{1,0:T(8,128)(2,1)S(1)}, bf16[896,512]{1,0:T(8,128)(2,1)S(1)}, u32[]{:S(2)}, u32[]{:S(2)}) collective-permute-start(bf16[896,512]{1,0:T(8,128)(2,1)S(1)} %get-tuple-element.184), channel_id=1, source_target_pairs={{0,1},{1,3},{2,0},{3,2},{4,5},{5,7},{6,4},{7,6},{8,9},{9,11},{10,8... | collective-permute-start | bytes 2752520 | tf_op jit(solution)/shard_map/ppermute | solution.py:252
  144.6 44.1 %collective-permute-start.56 = (bf16[896,512]{1,0:T(8,128)(2,1)S(1)}, bf16[896,512]{1,0:T(8,128)(2,1)S(1)}, u32[]{:S(2)}, u32[]{:S(2)}) collective-permute-start(bf16[896,512]{1,0:T(8,128)(2,1)S(1)} %get-tuple-element.182.refs_12_), channel_id=1, source_target_pairs={{0,2},{1,0},{2,3},{3,1},{4,6},{5,4},{6,7},{7,5},{8,10},{9,8},{10,1... | collective-permute-start | bytes 2752520 | tf_op jit(solution)/shard_map/ppermute | solution.py:252
  150.9 56.4 %collective-permute-start.55 = (bf16[896,512]{1,0:T(8,128)(2,1)S(1)}, bf16[896,512]{1,0:T(8,128)(2,1)S(1)}, u32[]{:S(2)}, u32[]{:S(2)}) collective-permute-start(bf16[896,512]{1,0:T(8,128)(2,1)S(1)} %get-tuple-element.183.refs_2_), channel_id=1, source_target_pairs={{0,4},{1,2},{2,1},{3,7},{4,0},{5,6},{6,5},{7,3},{8,12},{9,10},{10,... | collective-permute-start | bytes 2752520 | tf_op jit(solution)/shard_map/ppermute | solution.py:252
  (38 other events, 128.5 us)

commit v7 on v6

--- a/solution.py
+++ b/solution.py
@@ -27,7 +27,7 @@
         order = [
             "0pick00", "0send0", "0pick13", "0send1", "0gram0", "0split0", "0add00", "0add01", "0send2", "0gram1",
             "0split1", "0join00", "0add10", "0join01", "0add11", "0gram2", "0send3", "0split2", "1gram0", "0add20",
-            "1split0", "0add21", "1add00", "0join10", "1add01", "1gram1", "0join11", "1split1", "0update3", "1add10",
+            "1split0", "0add21", "1add00", "0join10", "1add01", "1gram1", "0join11", "1split1", "1add10", "0update3",
             "1add11", "1join00", "1join01", "0update120", "1update12", "0need3", "1update30", "0place0003",
             "0place0102101112", "0place13",
         ]
@@ -344,8 +344,10 @@
         steps = [step for rounds in self.phases[first : last + 1] for step in rounds]
         tables = [{p: to for p, to in enumerate(step) if p != to} for step in steps]
         places = {p: p for p in range(len(steps[0]))}
-        picked = pick(self.iterate, self.expert_order, tables if first else tables + [places], self.last, not first)
-        if not first:
+        ends = last == len(self.phases) - 1
+        tables = tables + [places] if ends else tables
+        picked = pick(self.iterate, self.expert_order, tables, self.last, not first)
+        if ends:
             self.own = picked.pop()
         for phase in range(first, last + 1):
             count = len(self.phases[phase])

time: 209 us -> 207 us (level)
  transfers between devices with their start and end apart: 58 -> 58, of which waited for: 42 -> 42; matrix products, arithmetic and copies ran while one was open for 0% -> 0% of each run, Pallas kernels for 7% -> 8%
where the time goes in v7:
time: 207 us
  waiting for transfers between devices  147 us (71%)
  starting transfers between devices  32.4 us (16%)
  Pallas kernels  23.5 us (11%)
  local copies, waits for them, and re-layouts  3.22 us (2%)
    ppermute x8, waiting for transfers between devices, shift(): return lax.ppermute(value, ('fsdp', 'loop'), pairs)  85.3 us
    ppermute x50, waiting for transfers between devices, swap(): return lax.ppermute(value, ('fsdp', 'loop'), pairs)  62 us
    ppermute x50, starting transfers between devices, swap(): return lax.ppermute(value, ('fsdp', 'loop'), pairs)  23.6 us
    pallas_call x32, Pallas kernels, call(): pl.pallas_call(wrapped, out_shape=outs, in_specs=list(specs) + [ANY] * ex...  21 us
    ppermute x8, starting transfers between devices, shift(): return lax.ppermute(value, ('fsdp', 'loop'), pairs)  8.77 us
  transfers between devices with their start and end apart: 58, of which 42 were waited for; matrix products, arithmetic and copies ran while one was open for 0% of the time, Pallas kernels for 8%

profile of v7, /device:TPU:8, one launch (start us, length us, event | category | flops | bytes accessed | tf_op | source)
XLA Modules:
  0.0 206.9 jit_solution(18346861775630267253)
XLA Ops:
  0.0 2.9 %pick.2.refs_2_ = bf16[896,512]{1,0:T(8,128)(2,1)} custom-call(s32[4]{0:T(128)} %refs_0_.3, bf16[4,896,512]{2,1,0:T(8,128)(2,1)} %refs_1_.3), custom_call_target="tpu_custom_call" | custom-call | bytes 1 | tf_op jit(solution)/shard_map/pick/pallas_call | solution.py:65
  2.9 2.6 %collective-permute-start = (bf16[896,512]{1,0:T(8,128)(2,1)}, bf16[896,512]{1,0:T(8,128)(2,1)S(1)}, u32[]{:S(2)}, u32[]{:S(2)}) collective-permute-start(bf16[896,512]{1,0:T(8,128)(2,1)} %pick.2.refs_2_), channel_id=1, source_target_pairs={{0,1},{1,3},{2,0},{3,2},{4,5},{5,7},{6,4},{7,6},{8,9},{9,11},{10,8... | collective-permute-start | bytes 2752520 | tf_op jit(solution)/shard_map/ppermute | solution.py:252
  5.6 2.0 copy-done
  10.3 15.2 %collective-permute-done.refs_2_.refs_1_ = bf16[896,512]{1,0:T(8,128)(2,1)S(1)} collective-permute-done((bf16[896,512]{1,0:T(8,128)(2,1)}, bf16[896,512]{1,0:T(8,128)(2,1)S(1)}, u32[]{:S(2)}, u32[]{:S(2)}) %collective-permute-start) | collective-permute-done | bytes 917536 | tf_op jit(solution)/shard_map/ppermute | solution.py:252
  32.5 15.8 %collective-permute-done.1.refs_2_ = bf16[896,512]{1,0:T(8,128)(2,1)S(1)} collective-permute-done((bf16[896,512]{1,0:T(8,128)(2,1)S(1)}, bf16[896,512]{1,0:T(8,128)(2,1)S(1)}, u32[]{:S(2)}, u32[]{:S(2)}) %collective-permute-start.1) | collective-permute-done | bytes 917536 | tf_op jit(solution)/shard_map/ppermute | solution.py:252
  49.3 2.0 collective-permute-done.9.refs_1_
  58.4 3.5 %gram_part.8 = (f32[256,3072]{1,0:T(8,128)S(1)}, bf16[256,1536]{1,0:T(8,128)(2,1)S(1)}, bf16[256,1536]{1,0:T(8,128)(2,1)S(1)}) custom-call(bf16[896,512]{1,0:T(8,128)(2,1)S(1)} %get-tuple-element.95.refs_0_, bf16[896,512]{1,0:T(8,128)(2,1)S(1)} %collective-permute-done.refs_2_.refs_1_, bf16[896,512]{1,0:T(8,128)(2,1)S(1)} %collective-permute-done.1.refs_2_, ...), custom_call_target="tpu_custom_call" | custom-call | bytes 1 | tf_op jit(solution)/shard_map/gram_part/pallas_call | solution.py:65
  63.7 2.0 collective-permute-done.24.refs_2_
  71.7 6.1 %collective-permute-done.26.refs_2_ = bf16[128,1536]{1,0:T(8,128)(2,1)S(1)} collective-permute-done((bf16[128,1536]{1,0:T(8,128)(2,1)S(1)}, bf16[128,1536]{1,0:T(8,128)(2,1)S(1)}, u32[]{:S(2)}, u32[]{:S(2)}) %collective-permute-start.26) | collective-permute-done | bytes 393248 | tf_op jit(solution)/shard_map/ppermute | solution.py:246
  82.0 3.2 %collective-permute-done.30.refs_2_ = bf16[64,1536]{1,0:T(8,128)(2,1)S(1)} collective-permute-done((bf16[64,1536]{1,0:T(8,128)(2,1)S(1)}, bf16[64,1536]{1,0:T(8,128)(2,1)S(1)}, u32[]{:S(2)}, u32[]{:S(2)}) %collective-permute-start.30) | collective-permute-done | bytes 196640 | tf_op jit(solution)/shard_map/ppermute | solution.py:246
  86.5 2.2 %collective-permute-done.19.refs_3_ = bf16[896,512]{1,0:T(8,128)(2,1)S(1)} collective-permute-done((bf16[896,512]{1,0:T(8,128)(2,1)S(1)}, bf16[896,512]{1,0:T(8,128)(2,1)S(1)}, u32[]{:S(2)}, u32[]{:S(2)}) %collective-permute-start.19) | collective-permute-done | bytes 917536 | tf_op jit(solution)/shard_map/ppermute | solution.py:252
  88.7 2.4 %gram_part.9 = (f32[256,2048]{1,0:T(8,128)S(1)}, bf16[256,1024]{1,0:T(8,128)(2,1)S(1)}, bf16[256,1024]{1,0:T(8,128)(2,1)S(1)}) custom-call(bf16[896,512]{1,0:T(8,128)(2,1)S(1)} %get-tuple-element.95.refs_0_, bf16[896,512]{1,0:T(8,128)(2,1)S(1)} %collective-permute-done.refs_2_.refs_1_, bf16[896,512]{1,0:T(8,128)(2,1)S(1)} %collective-permute-done.1.refs_2_, ...), custom_call_target="tpu_custom_call" | custom-call | bytes 1 | tf_op jit(solution)/shard_map/gram_part/pallas_call | solution.py:65
  96.7 5.7 %collective-permute-done.38.refs_2_ = bf16[128,1024]{1,0:T(8,128)(2,1)S(1)} collective-permute-done((bf16[128,1024]{1,0:T(8,128)(2,1)S(1)}, bf16[128,1024]{1,0:T(8,128)(2,1)S(1)}, u32[]{:S(2)}, u32[]{:S(2)}) %collective-permute-start.38) | collective-permute-done | bytes 262176 | tf_op jit(solution)/shard_map/ppermute | solution.py:246
  104.0 1.6 collective-permute-start.40
  106.2 3.0 %collective-permute-done.40.refs_2_ = bf16[64,1024]{1,0:T(8,128)(2,1)S(1)} collective-permute-done((bf16[64,1024]{1,0:T(8,128)(2,1)S(1)}, bf16[64,1024]{1,0:T(8,128)(2,1)S(1)}, u32[]{:S(2)}, u32[]{:S(2)}) %collective-permute-start.40) | collective-permute-done | bytes 131104 | tf_op jit(solution)/shard_map/ppermute | solution.py:246
  112.1 6.8 %collective-permute-done.46.refs_2_ = bf16[64,2560]{1,0:T(8,128)(2,1)S(1)} collective-permute-done((bf16[64,2560]{1,0:T(8,128)(2,1)S(1)}, bf16[64,2560]{1,0:T(8,128)(2,1)S(1)}, u32[]{:S(2)}, u32[]{:S(2)}) %collective-permute-start.46) | collective-permute-done | bytes 327712 | tf_op jit(solution)/shard_map/ppermute | solution.py:246
  121.4 12.0 %collective-permute-done.48.refs_2_ = bf16[128,2560]{1,0:T(8,128)(2,1)S(1)} collective-permute-done((bf16[128,2560]{1,0:T(8,128)(2,1)S(1)}, bf16[128,2560]{1,0:T(8,128)(2,1)S(1)}, u32[]{:S(2)}, u32[]{:S(2)}) %collective-permute-start.48) | collective-permute-done | bytes 655392 | tf_op jit(solution)/shard_map/ppermute | solution.py:246
  139.1 4.3 %update.6 = (bf16[896,512]{1,0:T(8,128)(2,1)S(1)}, bf16[896,512]{1,0:T(8,128)(2,1)S(1)}) custom-call(bf16[896,512]{1,0:T(8,128)(2,1)S(1)} %get-tuple-element.95.refs_0_, bf16[896,512]{1,0:T(8,128)(2,1)S(1)} %collective-permute-done.refs_2_.refs_1_, bf16[896,512]{1,0:T(8,128)(2,1)S(1)} %collective-permute-done.1.refs_2_, ...), custom_call_target="tpu_custom_call" | custom-call | bytes 1 | tf_op jit(solution)/shard_map/update/pallas_call | solution.py:65
  143.5 2.0 collective-permute-start.56
  145.5 4.3 %update.7 = (bf16[896,512]{1,0:T(8,128)(2,1)S(1)}, bf16[896,512]{1,0:T(8,128)(2,1)S(1)}) custom-call(bf16[896,512]{1,0:T(8,128)(2,1)S(1)} %get-tuple-element.95.refs_0_, bf16[896,512]{1,0:T(8,128)(2,1)S(1)} %collective-permute-done.refs_2_.refs_1_, bf16[896,512]{1,0:T(8,128)(2,1)S(1)} %collective-permute-done.1.refs_2_, ...), custom_call_target="tpu_custom_call" | custom-call | bytes 1 | tf_op jit(solution)/shard_map/update/pallas_call | solution.py:65
  149.8 2.2 %collective-permute-start.55 = (bf16[896,512]{1,0:T(8,128)(2,1)S(1)}, bf16[896,512]{1,0:T(8,128)(2,1)S(1)}, u32[]{:S(2)}, u32[]{:S(2)}) collective-permute-start(bf16[896,512]{1,0:T(8,128)(2,1)S(1)} %get-tuple-element.181.refs_2_), channel_id=1, source_target_pairs={{0,4},{1,2},{2,1},{3,7},{4,0},{5,6},{6,5},{7,3},{8,12},{9,10},{10,... | collective-permute-start | bytes 2752520 | tf_op jit(solution)/shard_map/ppermute | solution.py:252
  152.1 14.6 %collective-permute-done.57.refs_1_.refs_4_ = bf16[896,512]{1,0:T(8,128)(2,1)S(1)} collective-permute-done((bf16[896,512]{1,0:T(8,128)(2,1)S(1)}, bf16[896,512]{1,0:T(8,128)(2,1)S(1)}, u32[]{:S(2)}, u32[]{:S(2)}) %collective-permute-start.57) | collective-permute-done | bytes 917536 | tf_op jit(solution)/shard_map/ppermute | solution.py:252
  166.7 20.6 %collective-permute-done.56.refs_0_.refs_3_ = bf16[896,512]{1,0:T(8,128)(2,1)S(1)} collective-permute-done((bf16[896,512]{1,0:T(8,128)(2,1)S(1)}, bf16[896,512]{1,0:T(8,128)(2,1)S(1)}, u32[]{:S(2)}, u32[]{:S(2)}) %collective-permute-start.56) | collective-permute-done | bytes 917536 | tf_op jit(solution)/shard_map/ppermute | solution.py:252
  188.9 16.8 %collective-permute-done.55.refs_0_ = bf16[896,512]{1,0:T(8,128)(2,1)S(1)} collective-permute-done((bf16[896,512]{1,0:T(8,128)(2,1)S(1)}, bf16[896,512]{1,0:T(8,128)(2,1)S(1)}, u32[]{:S(2)}, u32[]{:S(2)}) %collective-permute-start.55) | collective-permute-done | bytes 917536 | tf_op jit(solution)/shard_map/ppermute | solution.py:252
  (136 shorter events, 52.3 us)
Async XLA Ops:
  2.9 22.6 %collective-permute-start = (bf16[896,512]{1,0:T(8,128)(2,1)}, bf16[896,512]{1,0:T(8,128)(2,1)S(1)}, u32[]{:S(2)}, u32[]{:S(2)}) collective-permute-start(bf16[896,512]{1,0:T(8,128)(2,1)} %pick.2.refs_2_), channel_id=1, source_target_pairs={{0,1},{1,3},{2,0},{3,2},{4,5},{5,7},{6,4},{7,6},{8,9},{9,11},{10,8... | collective-permute-start | bytes 2752520 | tf_op jit(solution)/shard_map/ppermute | solution.py:252
  25.5 22.8 %collective-permute-start.1 = (bf16[896,512]{1,0:T(8,128)(2,1)S(1)}, bf16[896,512]{1,0:T(8,128)(2,1)S(1)}, u32[]{:S(2)}, u32[]{:S(2)}) collective-permute-start(bf16[896,512]{1,0:T(8,128)(2,1)S(1)} %gate.3.refs_2_), channel_id=1, source_target_pairs={{0,2},{1,0},{2,3},{3,1},{4,6},{5,4},{6,7},{7,5},{8,10},{9,8},{10,1... | collective-permute-start | bytes 2752520 | tf_op jit(solution)/shard_map/ppermute | solution.py:252
  48.2 7.2 %collective-permute-start.8 = (bf16[896,512]{1,0:T(8,128)(2,1)S(1)}, bf16[896,512]{1,0:T(8,128)(2,1)S(1)}, u32[]{:S(2)}, u32[]{:S(2)}) collective-permute-start(bf16[896,512]{1,0:T(8,128)(2,1)S(1)} %gate.4.refs_3_), channel_id=1, source_target_pairs={{0,3},{1,5},{2,6},{3,0},{4,7},{5,1},{6,2},{7,4},{8,11},{9,13},{10,... | collective-permute-start | bytes 2752520 | tf_op jit(solution)/shard_map/ppermute | solution.py:252
  62.5 26.3 %collective-permute-start.19 = (bf16[896,512]{1,0:T(8,128)(2,1)S(1)}, bf16[896,512]{1,0:T(8,128)(2,1)S(1)}, u32[]{:S(2)}, u32[]{:S(2)}) collective-permute-start(bf16[896,512]{1,0:T(8,128)(2,1)S(1)} %gate.5.refs_3_), channel_id=1, source_target_pairs={{0,4},{1,2},{2,1},{3,7},{4,0},{5,6},{6,5},{7,3},{8,12},{9,10},{10,... | collective-permute-start | bytes 2752520 | tf_op jit(solution)/shard_map/ppermute | solution.py:252
  66.5 11.4 %collective-permute-start.26 = (bf16[128,1536]{1,0:T(8,128)(2,1)S(1)}, bf16[128,1536]{1,0:T(8,128)(2,1)S(1)}, u32[]{:S(2)}, u32[]{:S(2)}) collective-permute-start(bf16[128,1536]{1,0:T(8,128)(2,1)S(1)} %get-tuple-element.140), channel_id=1, source_target_pairs={{0,4},{1,9},{2,10},{3,7},{4,0},{5,13},{6,14},{7,3},{8,12},{9,1},{1... | collective-permute-start | bytes 1179656 | tf_op jit(solution)/shard_map/ppermute | solution.py:246
  68.0 11.0 %collective-permute-start.27 = (bf16[128,1536]{1,0:T(8,128)(2,1)S(1)}, bf16[128,1536]{1,0:T(8,128)(2,1)S(1)}, u32[]{:S(2)}, u32[]{:S(2)}) collective-permute-start(bf16[128,1536]{1,0:T(8,128)(2,1)S(1)} %get-tuple-element.141), channel_id=1, source_target_pairs={{0,4},{1,17},{2,18},{3,7},{4,0},{5,21},{6,22},{7,3},{8,12},{9,25},... | collective-permute-start | bytes 1179656 | tf_op jit(solution)/shard_map/ppermute | solution.py:246
  71.2 10.2 %collective-permute-start.33 = (bf16[64,1792]{1,0:T(8,128)(2,1)S(1)}, bf16[64,1792]{1,0:T(8,128)(2,1)S(1)}, u32[]{:S(2)}, u32[]{:S(2)}) collective-permute-start(bf16[64,1792]{1,0:T(8,128)(2,1)S(1)} %get-tuple-element.151.refs_1_), channel_id=1, source_target_pairs={{0,8},{1,5},{2,6},{3,11},{4,12},{5,1},{6,2},{7,15},{8,0},{9,13},{1... | collective-permute-start | bytes 688136 | tf_op jit(solution)/shard_map/ppermute | solution.py:246
  71.6 9.8 %collective-permute-start.32 = (bf16[64,1792]{1,0:T(8,128)(2,1)S(1)}, bf16[64,1792]{1,0:T(8,128)(2,1)S(1)}, u32[]{:S(2)}, u32[]{:S(2)}) collective-permute-start(bf16[64,1792]{1,0:T(8,128)(2,1)S(1)} %get-tuple-element.146.refs_4_.refs_0_), channel_id=1, source_target_pairs={{0,16},{1,5},{2,6},{3,19},{4,20},{5,1},{6,2},{7,23},{8,24},{9,13},... | collective-permute-start | bytes 688136 | tf_op jit(solution)/shard_map/ppermute | solution.py:246
  79.2 6.0 %collective-permute-start.30 = (bf16[64,1536]{1,0:T(8,128)(2,1)S(1)}, bf16[64,1536]{1,0:T(8,128)(2,1)S(1)}, u32[]{:S(2)}, u32[]{:S(2)}) collective-permute-start(bf16[64,1536]{1,0:T(8,128)(2,1)S(1)} %get-tuple-element.149), channel_id=1, source_target_pairs={{0,4},{1,17},{2,18},{3,7},{4,0},{5,21},{6,22},{7,3},{8,12},{9,25},... | collective-permute-start | bytes 589832 | tf_op jit(solution)/shard_map/ppermute | solution.py:246
  81.4 10.3 %collective-permute-start.37 = (bf16[128,1792]{1,0:T(8,128)(2,1)S(1)}, bf16[128,1792]{1,0:T(8,128)(2,1)S(1)}, u32[]{:S(2)}, u32[]{:S(2)}) collective-permute-start(bf16[128,1792]{1,0:T(8,128)(2,1)S(1)} %get-tuple-element.157.refs_1_), channel_id=1, source_target_pairs={{0,16},{1,5},{2,6},{3,19},{4,20},{5,1},{6,2},{7,23},{8,24},{9,13},... | collective-permute-start | bytes 1376264 | tf_op jit(solution)/shard_map/ppermute | solution.py:246
  81.5 10.2 %collective-permute-start.36 = (bf16[128,1792]{1,0:T(8,128)(2,1)S(1)}, bf16[128,1792]{1,0:T(8,128)(2,1)S(1)}, u32[]{:S(2)}, u32[]{:S(2)}) collective-permute-start(bf16[128,1792]{1,0:T(8,128)(2,1)S(1)} %get-tuple-element.152.refs_4_.refs_0_), channel_id=1, source_target_pairs={{0,8},{1,5},{2,6},{3,11},{4,12},{5,1},{6,2},{7,15},{8,0},{9,13},{1... | collective-permute-start | bytes 1376264 | tf_op jit(solution)/shard_map/ppermute | solution.py:246
  91.8 14.3 %collective-permute-start.45 = (bf16[256,1792]{1,0:T(8,128)(2,1)S(1)}, bf16[256,1792]{1,0:T(8,128)(2,1)S(1)}, u32[]{:S(2)}, u32[]{:S(2)}) collective-permute-start(bf16[256,1792]{1,0:T(8,128)(2,1)S(1)} %get-tuple-element.169.refs_7_), channel_id=1, source_target_pairs={{0,4},{1,5},{2,6},{3,7},{4,0},{5,1},{6,2},{7,3},{8,12},{9,13},{10,... | collective-permute-start | bytes 2752520 | tf_op jit(solution)/shard_map/ppermute | solution.py:246
  92.0 14.2 %collective-permute-start.44 = (bf16[256,1792]{1,0:T(8,128)(2,1)S(1)}, bf16[256,1792]{1,0:T(8,128)(2,1)S(1)}, u32[]{:S(2)}, u32[]{:S(2)}) collective-permute-start(bf16[256,1792]{1,0:T(8,128)(2,1)S(1)} %get-tuple-element.158.refs_3_.refs_6_), channel_id=1, source_target_pairs={{0,4},{1,5},{2,6},{3,7},{4,0},{5,1},{6,2},{7,3},{8,12},{9,13},{10,... | collective-permute-start | bytes 2752520 | tf_op jit(solution)/shard_map/ppermute | solution.py:246
  94.0 8.4 %collective-permute-start.38 = (bf16[128,1024]{1,0:T(8,128)(2,1)S(1)}, bf16[128,1024]{1,0:T(8,128)(2,1)S(1)}, u32[]{:S(2)}, u32[]{:S(2)}) collective-permute-start(bf16[128,1024]{1,0:T(8,128)(2,1)S(1)} %get-tuple-element.161), channel_id=1, source_target_pairs={{0,4},{1,9},{2,10},{3,7},{4,0},{5,13},{6,14},{7,3},{8,12},{9,1},{1... | collective-permute-start | bytes 786440 | tf_op jit(solution)/shard_map/ppermute | solution.py:246
  95.2 10.4 %collective-permute-start.43 = (bf16[256,768]{1,0:T(8,128)(2,1)S(1)}, bf16[256,768]{1,0:T(8,128)(2,1)S(1)}, u32[]{:S(2)}, u32[]{:S(2)}) collective-permute-start(bf16[256,768]{1,0:T(8,128)(2,1)S(1)} %get-tuple-element.168.refs_5_), channel_id=1, source_target_pairs={{0,4},{1,5},{2,6},{3,7},{4,0},{5,1},{6,2},{7,3},{8,12},{9,13},{10,... | collective-permute-start | bytes 1179656 | tf_op jit(solution)/shard_map/ppermute | solution.py:246
  95.2 8.7 %collective-permute-start.39 = (bf16[128,1024]{1,0:T(8,128)(2,1)S(1)}, bf16[128,1024]{1,0:T(8,128)(2,1)S(1)}, u32[]{:S(2)}, u32[]{:S(2)}) collective-permute-start(bf16[128,1024]{1,0:T(8,128)(2,1)S(1)} %get-tuple-element.162), channel_id=1, source_target_pairs={{0,4},{1,17},{2,18},{3,7},{4,0},{5,21},{6,22},{7,3},{8,12},{9,25},... | collective-permute-start | bytes 786440 | tf_op jit(solution)/shard_map/ppermute | solution.py:246
  110.6 8.3 %collective-permute-start.46 = (bf16[64,2560]{1,0:T(8,128)(2,1)S(1)}, bf16[64,2560]{1,0:T(8,128)(2,1)S(1)}, u32[]{:S(2)}, u32[]{:S(2)}) collective-permute-start(bf16[64,2560]{1,0:T(8,128)(2,1)S(1)} %get-tuple-element.170.refs_0_.refs_4_), channel_id=1, source_target_pairs={{0,4},{1,17},{2,18},{3,7},{4,0},{5,21},{6,22},{7,3},{8,12},{9,25},... | collective-permute-start | bytes 983048 | tf_op jit(solution)/shard_map/ppermute | solution.py:246
  111.2 7.9 %collective-permute-start.47 = (bf16[64,2560]{1,0:T(8,128)(2,1)S(1)}, bf16[64,2560]{1,0:T(8,128)(2,1)S(1)}, u32[]{:S(2)}, u32[]{:S(2)}) collective-permute-start(bf16[64,2560]{1,0:T(8,128)(2,1)S(1)} %get-tuple-element.171.refs_1_), channel_id=1, source_target_pairs={{0,4},{1,9},{2,10},{3,7},{4,0},{5,13},{6,14},{7,3},{8,12},{9,1},{1... | collective-permute-start | bytes 983048 | tf_op jit(solution)/shard_map/ppermute | solution.py:246
  119.3 14.1 %collective-permute-start.48 = (bf16[128,2560]{1,0:T(8,128)(2,1)S(1)}, bf16[128,2560]{1,0:T(8,128)(2,1)S(1)}, u32[]{:S(2)}, u32[]{:S(2)}) collective-permute-start(bf16[128,2560]{1,0:T(8,128)(2,1)S(1)} %get-tuple-element.172.refs_0_.refs_4_), channel_id=1, source_target_pairs={{0,4},{1,9},{2,10},{3,7},{4,0},{5,13},{6,14},{7,3},{8,12},{9,1},{1... | collective-permute-start | bytes 1966088 | tf_op jit(solution)/shard_map/ppermute | solution.py:246
  120.2 13.7 %collective-permute-start.49 = (bf16[128,2560]{1,0:T(8,128)(2,1)S(1)}, bf16[128,2560]{1,0:T(8,128)(2,1)S(1)}, u32[]{:S(2)}, u32[]{:S(2)}) collective-permute-start(bf16[128,2560]{1,0:T(8,128)(2,1)S(1)} %get-tuple-element.173.refs_1_), channel_id=1, source_target_pairs={{0,4},{1,17},{2,18},{3,7},{4,0},{5,21},{6,22},{7,3},{8,12},{9,25},... | collective-permute-start | bytes 1966088 | tf_op jit(solution)/shard_map/ppermute | solution.py:246
  121.4 24.2 %collective-permute-start.54 = (bf16[896,512]{1,0:T(8,128)(2,1)S(1)}, bf16[896,512]{1,0:T(8,128)(2,1)S(1)}, u32[]{:S(2)}, u32[]{:S(2)}) collective-permute-start(bf16[896,512]{1,0:T(8,128)(2,1)S(1)} %update.4.refs_6_), channel_id=1, source_target_pairs={{0,3},{1,5},{2,6},{3,0},{4,7},{5,1},{6,2},{7,4},{8,11},{9,13},{10,... | collective-permute-start | bytes 2752520 | tf_op jit(solution)/shard_map/ppermute | solution.py:252
  143.5 23.2 %collective-permute-start.57 = (bf16[896,512]{1,0:T(8,128)(2,1)S(1)}, bf16[896,512]{1,0:T(8,128)(2,1)S(1)}, u32[]{:S(2)}, u32[]{:S(2)}) collective-permute-start(bf16[896,512]{1,0:T(8,128)(2,1)S(1)} %get-tuple-element.182), channel_id=1, source_target_pairs={{0,1},{1,3},{2,0},{3,2},{4,5},{5,7},{6,4},{7,6},{8,9},{9,11},{10,8... | collective-permute-start | bytes 2752520 | tf_op jit(solution)/shard_map/ppermute | solution.py:252
  143.5 43.8 %collective-permute-start.56 = (bf16[896,512]{1,0:T(8,128)(2,1)S(1)}, bf16[896,512]{1,0:T(8,128)(2,1)S(1)}, u32[]{:S(2)}, u32[]{:S(2)}) collective-permute-start(bf16[896,512]{1,0:T(8,128)(2,1)S(1)} %get-tuple-element.180.refs_12_), channel_id=1, source_target_pairs={{0,2},{1,0},{2,3},{3,1},{4,6},{5,4},{6,7},{7,5},{8,10},{9,8},{10,1... | collective-permute-start | bytes 2752520 | tf_op jit(solution)/shard_map/ppermute | solution.py:252
  149.8 55.9 %collective-permute-start.55 = (bf16[896,512]{1,0:T(8,128)(2,1)S(1)}, bf16[896,512]{1,0:T(8,128)(2,1)S(1)}, u32[]{:S(2)}, u32[]{:S(2)}) collective-permute-start(bf16[896,512]{1,0:T(8,128)(2,1)S(1)} %get-tuple-element.181.refs_2_), channel_id=1, source_target_pairs={{0,4},{1,2},{2,1},{3,7},{4,0},{5,6},{6,5},{7,3},{8,12},{9,10},{10,... | collective-permute-start | bytes 2752520 | tf_op jit(solution)/shard_map/ppermute | solution.py:252
  (37 other events, 99.0 us)
